TPU v7x, 32 devices: a whole 2x2x4 slice. The times are simulated.
32 devices in a mesh: dp: 4 (over z), expert: 8 (over y, x, core).
Axes of the slice: x: 2, y: 2, z: 4, core: 2. Of those that a mesh axis runs over, the one named last changes fastest.
Arguments:
- out_grad: bfloat16 [4096, 1440], P(('dp', 'expert')), may hold values from -0.119628906 to 0.119628906
- expert_ids: int32 [4096, 4], P(('dp', 'expert')), may hold values from 0 to 7, all different within a row; in each aligned block of 128 rows (0 to 127, 128 to 255, ...) at most 64 rows name the same one
- gate_weight: float32 [4096, 4], P(('dp', 'expert')), may hold values from 0.1 to 1
- saved_hidden: bfloat16 [4, 8, 8, 64, 1440], P('dp', 'expert'), may hold values from -6 to 6
- saved_output: bfloat16 [4, 8, 8, 64, 1440], P('dp', 'expert'), may hold values from -6 to 6
Outputs:
- down_grad: bfloat16 [8, 1440, 1440], P('expert', 'dp')
- route_grad: float32 [4096, 4], P(('dp', 'expert'))
Inputs may be any that keep to these rules, and one draw needn't show every extreme that they name: `expert_ids`: among the 128 tokens of one device each expert is named by at most 64 of the top-4 choices, a bound that some block reaches; a token names 4 different experts.
All inputs are finite; a program needn't handle non-finite values.
Results may differ from a plain program's by a relative error of at most 0.015.
Values may be sent and summed in bfloat16 or wider, within the bound.
No kernel may reach another device: no remote copies, remote signals or barrier semaphores. Data moves between devices by JAX's collectives and lax.ppermute only.
A program may use at most 64 MiB of HBM per device.

v0:
```python
import jax
import jax.numpy as jnp
from jax import lax
from jax.sharding import PartitionSpec as P


def slot_numbers(ids, experts, capacity):
    rows = ids.shape[0] * ids.shape[1]
    flat = (ids.reshape(rows, 1) == jnp.arange(experts, dtype=jnp.int32)[None, :]).astype(jnp.int32)
    earlier = jnp.cumsum(flat, axis=0) - flat
    position = jnp.sum(earlier * flat, axis=1).reshape(ids.shape)
    return ids * capacity + position


def per_device(out_grad, expert_ids, gate_weight, saved_hidden, saved_output):
    tokens_here, width = out_grad.shape
    experts = lax.axis_size("expert")
    capacity = saved_hidden.shape[3]
    hidden_width = saved_hidden.shape[4]
    sources = saved_hidden.shape[2]
    slot = slot_numbers(expert_ids, experts, capacity)
    table = slot[:, :, None] == jnp.arange(experts * capacity, dtype=jnp.int32)[None, None, :]
    occupancy = jnp.sum(table, axis=1).astype(jnp.bfloat16)
    sent = lax.dot_general(
        occupancy, out_grad, (((0,), (0,)), ((), ())), preferred_element_type=jnp.float32
    )
    sent = sent.astype(jnp.bfloat16).reshape(experts, capacity, width)
    gate_slots = jnp.sum(jnp.where(table, gate_weight[:, :, None], jnp.float32(0.0)), axis=(0, 1))
    gate_slots = gate_slots.reshape(experts, capacity)
    arrived, arrived_gate = (
        lax.all_to_all(sent, "expert", split_axis=0, concat_axis=0, tiled=True),
        lax.all_to_all(
            gate_slots.astype(jnp.bfloat16), "expert", split_axis=0, concat_axis=0, tiled=True
        ).astype(gate_slots.dtype),
    )
    scaled = (
        (arrived_gate[:, :, None] * arrived).astype(jnp.bfloat16).reshape(sources * capacity, width)
    )
    hidden = saved_hidden.reshape(sources * capacity, hidden_width)
    own_rows = hidden_width // lax.axis_size("dp")
    down_grad = lax.psum_scatter(
        lax.dot_general(
            hidden, scaled, (((0,), (0,)), ((), ())), preferred_element_type=jnp.float32
        ).astype(jnp.bfloat16),
        "dp",
        scatter_dimension=0,
        tiled=True,
    ).astype(jnp.float32)
    down_grad = down_grad.astype(jnp.bfloat16).reshape(1, own_rows, width)
    outputs = saved_output.reshape(sources, capacity, width)
    returned = lax.all_to_all(outputs, "expert", split_axis=0, concat_axis=0, tiled=True)
    picked = returned.reshape(experts * capacity, width)[slot.reshape(-1)]
    picked = picked.reshape(tokens_here, expert_ids.shape[1], width)
    route_grad = jnp.einsum("tkd,td->tk", picked, out_grad, preferred_element_type=jnp.float32)
    return (down_grad, route_grad)


def solution(mesh):
    placed = (
        P(("dp", "expert"), None),
        P(("dp", "expert"), None),
        P(("dp", "expert"), None),
        P("dp", "expert", None, None, None),
        P("dp", "expert", None, None, None),
    )
    return jax.shard_map(
        per_device,
        mesh=mesh,
        in_specs=placed,
        out_specs=(P("expert", "dp", None), P(("dp", "expert"), None)),
        check_vma=False,
    )
```

profile of v0, /device:TPU:0, one launch (start us, length us, event | category | flops | bytes accessed | tf_op | source)
XLA Modules:
  0.0 149.1 jit_solution(1786062738714405850)
XLA Ops:
  7.2 0.0 copy-start
  7.2 0.9 copy.40
  8.1 0.1 eq.42
  8.2 0.1 eq.38
  8.3 1.1 reduce-window.6
  9.5 0.2 slice_reduce_fusion
  9.7 0.1 fusion.3
  9.8 0.1 reshape.101
  9.9 0.1 copy.42
  10.0 0.7 multiply_add_fusion
  10.7 0.9 select_reduce_fusion
  11.6 0.7 convert_element_type.67
  12.3 5.2 %all-to-all-start = ((bf16[8,1,64]{2,1,0:T(2,128)(2,1)}), bf16[8,1,64]{2,1,0:T(2,128)(2,1)S(1)}, u32[]{:S(2)}, u32[]{:S(2)}) async-start(bf16[8,1,64]{2,1,0:T(2,128)(2,1)} %convert_element_type.67), calls=%async_computation | async-start | bytes 8192 | tf_op jit(solution)/shard_map/all_to_all | solution.py:32
  17.4 0.2 convert_reduce_fusion
  17.6 1.5 %convolution_convert_fusion.1 = bf16[512,1440]{0,1:T(8,128)(2,1)S(1)} fusion(bf16[128,1440]{0,1:T(8,128)(2,1)} %param.5, s32[128,512]{1,0:T(8,128)S(1)} %convert_reduce_fusion), kind=kOutput, calls=%fused_computation.5 | convolution fusion | flops 189546496 | bytes 2105344 | tf_op jit(solution)/shard_map/dot_general | solution.py:24
  19.1 1.6 %copy.44 = bf16[512,1440]{1,0:T(8,128)(2,1)} copy(bf16[512,1440]{0,1:T(8,128)(2,1)S(1)} %convolution_convert_fusion.1) | data formatting | bytes 2949120 | tf_op jit(solution)/shard_map/convert_element_type | solution.py:27
  20.7 1.3 all-to-all-done
  22.0 3.6 %all-to-all-start.1 = ((bf16[8,64,1440]{2,1,0:T(8,128)(2,1)}), bf16[8,64,1440]{2,1,0:T(8,128)(2,1)S(1)}, u32[]{:S(2)}, u32[]{:S(2)}) async-start(bf16[8,64,1440]{2,1,0:T(8,128)(2,1)} %bitcast.4), calls=%async_computation.1 | async-start | bytes 3145728 | tf_op jit(solution)/shard_map/all_to_all | solution.py:31
  25.6 0.0 reduce-scatter.4.cloned.1.call-start
  25.7 20.9 %all-to-all-done.1 = bf16[8,64,1440]{2,1,0:T(8,128)(2,1)S(1)} async-done(((bf16[8,64,1440]{2,1,0:T(8,128)(2,1)}), bf16[8,64,1440]{2,1,0:T(8,128)(2,1)S(1)}, u32[]{:S(2)}, u32[]{:S(2)}) %all-to-all-start.1) | async-done | bytes 1474592 | tf_op jit(solution)/shard_map/all_to_all | solution.py:31
  46.6 0.3 multiply_convert_fusion
  46.9 0.0 copy-done
  46.9 4.6 %fusion = bf16[1440,1440]{0,1:T(8,128)(2,1)} fusion(bf16[512,1440]{1,0:T(8,128)(2,1)S(1)} %bitcast.28, bf16[512,1440]{1,0:T(8,128)(2,1)S(1)} %bitcast.24), kind=kOutput, calls=%fused_computation.2 | convolution fusion | flops 2125440000 | bytes 7096320 | tf_op jit(solution)/shard_map/dot_general | solution.py:42
  51.5 6.5 %copy.52 = bf16[1440,1440]{1,0:T(8,128)(2,1)} copy(bf16[1440,1440]{0,1:T(8,128)(2,1)} %fusion) | data formatting | bytes 8294400
  58.0 0.0 reduce-scatter.4.cloned.1.call-update
  58.0 0.0 copy-start.1
  58.0 3.7 %all-to-all-start.2 = ((bf16[8,64,1440]{2,1,0:T(8,128)(2,1)}), bf16[8,64,1440]{2,1,0:T(8,128)(2,1)S(1)}, u32[]{:S(2)}, u32[]{:S(2)}) async-start(bf16[8,64,1440]{2,1,0:T(8,128)(2,1)} %bitcast.27), calls=%async_computation.2 | async-start | bytes 3145728 | tf_op jit(solution)/shard_map/all_to_all | solution.py:51
  61.7 0.7 copy.45
  62.5 0.0 copy-done.1
  62.5 1.1 copy.54
  63.5 1.0 reshape.108
  64.5 18.2 %all-to-all-done.2 = bf16[8,64,1440]{2,1,0:T(8,128)(2,1)S(1)} async-done(((bf16[8,64,1440]{2,1,0:T(8,128)(2,1)}), bf16[8,64,1440]{2,1,0:T(8,128)(2,1)S(1)}, u32[]{:S(2)}, u32[]{:S(2)}) %all-to-all-start.2) | async-done | bytes 1474592 | tf_op jit(solution)/shard_map/all_to_all | solution.py:51
  82.7 3.0 %gather_fusion = bf16[512,1440]{1,0:T(8,128)(2,1)} fusion(bf16[512,1440]{1,0:T(8,128)(2,1)S(1)} %bitcast.25, s32[1024]{0:T(1024)S(1)} %pad_clamp_fusion), kind=kCustom, calls=%fused_computation | custom fusion | bytes 2951168 | tf_op jit(solution)/shard_map/gather | solution.py:52
  85.7 2.9 %reshape.109 = bf16[128,4,1440]{2,1,0:T(4,128)(2,1)S(1)} reshape(bf16[512,1440]{1,0:T(8,128)(2,1)} %gather_fusion) | data formatting | bytes 2949120 | tf_op jit(solution)/shard_map/reshape | solution.py:53
  88.6 2.0 %multiply_reduce_fusion = f32[128,4]{1,0:T(8,128)S(1)} fusion(f32[128,1440]{1,0:T(8,128)} %copy.54, bf16[128,4,1440]{2,1,0:T(4,128)(2,1)S(1)} %reshape.109), kind=kLoop, calls=%fused_computation.3 | loop fusion | flops 2211328 | bytes 2213888
  90.6 0.7 copy.51
  91.3 46.7 %reduce-scatter.4.cloned.1.call-done = bf16[360,1440]{1,0:T(8,128)(2,1)} async-done(((bf16[1440,1440]{1,0:T(8,128)(2,1)}), bf16[360,1440]{1,0:T(8,128)(2,1)}) %reduce-scatter.4.cloned.1.call-update) | async-done | bytes 1036816
  138.0 2.2 %copy.53 = bf16[360,1440]{0,1:T(8,128)(2,1)S(1)} copy(bf16[360,1440]{1,0:T(8,128)(2,1)} %reduce-scatter.4.cloned.1.call-done) | data formatting | bytes 2073600
  140.2 2.0 %copy.46 = bf16[1,360,1440]{2,1,0:T(8,128)(2,1)} copy(bf16[1,360,1440]{1,2,0:T(8,128)(2,1)S(1)} %bitcast.26) | data formatting | bytes 2073600
  (6 shorter events, 0.1 us)
Async XLA Ops:
  7.2 39.7 %copy-start = (bf16[1,1,8,64,1440]{4,3,2,1,0:T(8,128)(2,1)S(1)}, bf16[1,1,8,64,1440]{4,3,2,1,0:T(8,128)(2,1)}, u32[]{:S(2)}) copy-start(bf16[1,1,8,64,1440]{4,3,2,1,0:T(8,128)(2,1)} %param.8) | copy-start | bytes 4423684
  12.3 9.8 %all-to-all-start = ((bf16[8,1,64]{2,1,0:T(2,128)(2,1)}), bf16[8,1,64]{2,1,0:T(2,128)(2,1)S(1)}, u32[]{:S(2)}, u32[]{:S(2)}) async-start(bf16[8,1,64]{2,1,0:T(2,128)(2,1)} %convert_element_type.67), calls=%async_computation | async-start | bytes 8192 | tf_op jit(solution)/shard_map/all_to_all | solution.py:32
  22.0 24.5 %all-to-all-start.1 = ((bf16[8,64,1440]{2,1,0:T(8,128)(2,1)}), bf16[8,64,1440]{2,1,0:T(8,128)(2,1)S(1)}, u32[]{:S(2)}, u32[]{:S(2)}) async-start(bf16[8,64,1440]{2,1,0:T(8,128)(2,1)} %bitcast.4), calls=%async_computation.1 | async-start | bytes 3145728 | tf_op jit(solution)/shard_map/all_to_all | solution.py:31
  25.6 112.4 %reduce-scatter.4.cloned.1.call-start = ((), (), s32[]{:S(2)}) async-start(), calls=%async_computation.4 | async-start | bytes 5529600
  58.0 4.5 %copy-start.1 = (bf16[128,1440]{0,1:T(8,128)(2,1)S(1)}, bf16[128,1440]{0,1:T(8,128)(2,1)}, u32[]{:S(2)}) copy-start(bf16[128,1440]{0,1:T(8,128)(2,1)} %param.5) | copy-start | bytes 1105924
  58.0 24.7 %all-to-all-start.2 = ((bf16[8,64,1440]{2,1,0:T(8,128)(2,1)}), bf16[8,64,1440]{2,1,0:T(8,128)(2,1)S(1)}, u32[]{:S(2)}, u32[]{:S(2)}) async-start(bf16[8,64,1440]{2,1,0:T(8,128)(2,1)} %bitcast.27), calls=%async_computation.2 | async-start | bytes 3145728 | tf_op jit(solution)/shard_map/all_to_all | solution.py:51
Sparse Core Ops, SparseCore 0:
  58.1 79.8 reduce-scatter.3
where the time goes:
time: 150 us; the launch traced here: 149 us
  waiting for transfers between devices  87.1 us (58%)
  local copies, waits for them, and re-layouts  23.7 us (16%)
  between operations  14.2 us (9%)
  starting transfers between devices  12.5 us (8%)
  matrix products  6.1 us (4%)
  other arithmetic  5.43 us (4%)
    unnamed x2, waiting for transfers between devices  46.8 us
    all_to_all x1, waiting for transfers between devices, per_device(): lax.all_to_all(sent, 'expert', split_axis=0, concat_axis=0, tiled=True)  20.9 us
    all_to_all x1, waiting for transfers between devices, per_device(): lax.all_to_all(outputs, 'expert', split_axis=0, concat_axis=0, tiled=True)  18.2 us
    unnamed x9, local copies, waits for them, and re-layouts  12.6 us
    all_to_all x1, starting transfers between devices, per_device(): lax.all_to_all(gate_slots.astype(jnp.bfloat16), 'expert', split_axis=0, c...  5.17 us
    dot_general x1, matrix products, per_device(): lax.dot_general(hidden, scaled, (((0,), (0,)), ((), ())), preferred_eleme...  4.59 us
    all_to_all x1, starting transfers between devices, per_device(): lax.all_to_all(outputs, 'expert', split_axis=0, concat_axis=0, tiled=True)  3.73 us
    all_to_all x1, starting transfers between devices, per_device(): lax.all_to_all(sent, 'expert', split_axis=0, concat_axis=0, tiled=True)  3.58 us
  transfers between devices with their start and end apart: 4, of which 4 were waited for; matrix products, arithmetic and copies ran while one was open for 10% of the time, Pallas kernels for 0%

commit v1 on v0

--- a/solution.py
+++ b/solution.py
@@ -1,7 +1,14 @@
+import functools
+
 import jax
 import jax.numpy as jnp
 from jax import lax
+from jax.experimental import pallas as pl
+from jax.experimental.pallas import tpu as pltpu
 from jax.sharding import PartitionSpec as P
+
+LANES = 128
+META = 16
 
 
 def slot_numbers(ids, experts, capacity):
@@ -12,7 +19,7 @@
     return ids * capacity + position
 
 
-def per_device(out_grad, expert_ids, gate_weight, saved_hidden, saved_output):
+def general(out_grad, expert_ids, gate_weight, saved_hidden, saved_output):
     tokens_here, width = out_grad.shape
     experts = lax.axis_size("expert")
     capacity = saved_hidden.shape[3]
@@ -55,6 +62,261 @@
     return (down_grad, route_grad)
 
 
+def pack_kernel(grad_ref, ids_ref, gate_ref, out_ref):
+    tokens, width = grad_ref.shape
+    full, rest = width // LANES, width % LANES
+    for j in range(full):
+        out_ref[j * tokens:(j + 1) * tokens, :] = grad_ref[:, j * LANES:(j + 1) * LANES]
+    tail = grad_ref[:, full * LANES:].astype(jnp.float32)
+    out_ref[full * tokens:full * tokens + rest, :] = jnp.concatenate(
+        [tail[a * rest:(a + 1) * rest] for a in range(tokens // rest)], axis=1
+    ).astype(jnp.bfloat16)
+    lane = lax.broadcasted_iota(jnp.int32, (tokens, LANES), 1)
+    ids, gate = ids_ref[...], gate_ref[...]
+    dense = jnp.zeros((tokens, LANES), jnp.float32)
+    for k in range(ids.shape[1]):
+        dense = dense + jnp.where(lane == ids[:, k:k + 1], gate[:, k:k + 1], 0.0)
+    dense = dense.T[:META // 2]
+    high = dense.astype(jnp.bfloat16).astype(jnp.float32)
+    out_ref[width:, :] = jnp.concatenate([high, dense - high], axis=0).astype(jnp.bfloat16)
+
+
+def hidden_kernel(info_ref, hidden_ref, *rest):
+    outs, scratch = rest[:-1], rest[-1]
+    planes = len(outs)
+    rows = outs[0].shape[0]
+    for q in range(planes):
+        scratch[q] = hidden_ref[:, q * rows:(q + 1) * rows].T
+    for o in range(planes):
+        outs[o][...] = scratch[info_ref[1] ^ o]
+
+
+def block_tables(info_ref, mine, other):
+    me = info_ref[0]
+    width = mine[0].shape[0] - META
+    rows = lax.broadcasted_iota(jnp.int32, (META, LANES), 0)
+    picked = jnp.logical_or(rows == me, rows == me + META // 2)
+    gates = jnp.concatenate(
+        [
+            jnp.sum(jnp.where(picked, ref[width:, :].astype(jnp.float32), 0.0), axis=0, keepdims=True)
+            for ref in mine + other
+        ],
+        axis=0,
+    )
+    routed = gates > 0.0
+    before = lax.broadcasted_iota(jnp.int32, (LANES, LANES), 0) < lax.broadcasted_iota(jnp.int32, (LANES, LANES), 1)
+    earlier = jnp.dot(
+        routed.astype(jnp.bfloat16), before.astype(jnp.bfloat16), preferred_element_type=jnp.float32
+    ).astype(jnp.int32)
+    core = me & 1
+    half = LANES // 2
+    number = len(mine)
+    first = lax.broadcasted_iota(jnp.int32, gates.shape, 0) < number
+    side = jnp.where(first, core, 1 - core)
+    return gates, jnp.where(routed, earlier + side * half, -1)
+
+
+def columns(refs, start, stop):
+    tokens = LANES
+    parts = []
+    for ref in refs:
+        width = ref.shape[0] - META
+        full, rest = width // LANES, width % LANES
+        pieces = []
+        for j in range(start // LANES, -(-stop // LANES)):
+            if j < full:
+                pieces.append(ref[j * tokens:(j + 1) * tokens, :])
+            else:
+                packed = ref[full * tokens:width, :]
+                pieces.append(
+                    jnp.concatenate([packed[:, a * rest:(a + 1) * rest] for a in range(tokens // rest)], axis=0)
+                )
+        parts.append(pieces[0] if len(pieces) == 1 else jnp.concatenate(pieces, axis=1))
+    return jnp.concatenate(parts, axis=0)
+
+
+def pair_onehot(position, n, number):
+    pair = jnp.concatenate([position[n:n + 1], position[number + n:number + n + 1]], axis=1)
+    return lax.broadcasted_iota(jnp.int32, (LANES, 2 * LANES), 0) == pair
+
+
+def gather_hidden(info_ref, hidden_of, gates, position, number):
+    out = []
+    for n in range(number):
+        start = pl.multiple_of(((info_ref[0] >> 1) ^ n) * LANES, LANES)
+        gate = jnp.concatenate([gates[n:n + 1], gates[number + n:number + n + 1]], axis=1)
+        placed = jnp.dot(
+            hidden_of(start),
+            pair_onehot(position, n, number).astype(jnp.bfloat16),
+            preferred_element_type=jnp.float32,
+        )
+        out.append((placed * gate).astype(jnp.bfloat16))
+    return jnp.concatenate(out, axis=1)
+
+
+def interleave(mine, other):
+    return [ref for pair in zip(mine, other) for ref in pair]
+
+
+def column_chunks(width):
+    step = 2 * LANES
+    return [(a, min(a + step, width)) for a in range(0, width, step)]
+
+
+def accumulate(hidden, mine, other, acc_ref, out_ref):
+    refs = interleave(mine, other)
+    width = mine[0].shape[0] - META
+    for start, stop in column_chunks(width):
+        total = jnp.dot(hidden, columns(refs, start, stop), preferred_element_type=jnp.float32)
+        if acc_ref is not None:
+            total = total + acc_ref[:, start:stop]
+        out_ref[:, start:stop] = total.astype(out_ref.dtype)
+
+
+def own_kernel(info_ref, hidden_ref, saved_ref, *refs):
+    blocks, (acc_ref, score_ref) = refs[:-2], refs[-2:]
+    number = len(blocks) // 2
+    mine, other = list(blocks[:number]), list(blocks[number:])
+    gates, position = block_tables(info_ref, mine, other)
+    hidden = gather_hidden(info_ref, lambda s: hidden_ref[:, pl.ds(s, LANES)], gates, position, number)
+    accumulate(hidden, mine, other, None, acc_ref)
+    width = mine[0].shape[0] - META
+    first, second = [], []
+    for n in range(number):
+        start = pl.multiple_of(((info_ref[0] >> 1) ^ n) * LANES, LANES)
+        total = jnp.zeros((LANES, 2 * LANES), jnp.float32)
+        for a, b in column_chunks(width):
+            total = total + lax.dot_general(
+                saved_ref[pl.ds(start, LANES), a:b],
+                columns([mine[n], other[n]], a, b),
+                (((1,), (1,)), ((), ())),
+                preferred_element_type=jnp.float32,
+            )
+        row = jnp.sum(jnp.where(pair_onehot(position, n, number), total, 0.0), axis=0, keepdims=True)
+        first.append(row[:, :LANES])
+        second.append(row[:, LANES:])
+    score_ref[...] = jnp.concatenate(first + second, axis=0)
+
+
+def next_kernel(info_ref, near_ref, far_ref, acc_ref, *refs):
+    blocks, out_ref = refs[:-1], refs[-1]
+    number = len(blocks) // 2
+    mine, other = list(blocks[:number]), list(blocks[number:])
+    gates, position = block_tables(info_ref, mine, other)
+
+    def hidden_of(start):
+        if far_ref is near_ref:
+            return near_ref[:, pl.ds(start, LANES)]
+        return jnp.where(info_ref[2] != 0, far_ref[:, pl.ds(start, LANES)], near_ref[:, pl.ds(start, LANES)])
+
+    hidden = gather_hidden(info_ref, hidden_of, gates, position, number)
+    accumulate(hidden, mine, other, acc_ref, out_ref)
+
+
+def one_hidden_kernel(info_ref, near_ref, acc_ref, *refs):
+    next_kernel(info_ref, near_ref, near_ref, acc_ref, *refs)
+
+
+def call(kernel, outs, args, scratch=(), flops=0):
+    smem, vmem = pl.BlockSpec(memory_space=pltpu.SMEM), pl.BlockSpec(memory_space=pltpu.VMEM)
+    moved = sum(a.size * a.dtype.itemsize for a in (*args, *outs))
+    return pl.pallas_call(
+        kernel,
+        out_shape=outs,
+        in_specs=[smem if a.ndim == 1 else vmem for a in args],
+        out_specs=[vmem] * len(outs),
+        scratch_shapes=list(scratch),
+        compiler_params=pltpu.CompilerParams(vmem_limit_bytes=48 * 1024 * 1024),
+        cost_estimate=pl.CostEstimate(flops=flops, bytes_accessed=moved, transcendentals=0),
+    )(*args)
+
+
+def planes4(out_grad, expert_ids, gate_weight, saved_hidden, saved_output):
+    tokens, width = out_grad.shape
+    hidden_width = saved_hidden.shape[4]
+    slots = saved_hidden.shape[2] * saved_hidden.shape[3]
+    planes = lax.axis_size("dp")
+    rows = hidden_width // planes
+    me, plane = lax.axis_index("expert"), lax.axis_index("dp")
+    middle = jnp.logical_or(plane == 1, plane == 2)
+    bf16 = jnp.bfloat16
+
+    def along(name, bit):
+        return lambda x: lax.ppermute(x, name, [(i, i ^ bit) for i in range(lax.axis_size(name))])
+
+    core, px, py = along("expert", 1), along("expert", 2), along("expert", 4)
+    inner = lambda x: lax.ppermute(x, "dp", [(1, 2), (2, 1)])
+    outward = lambda x: lax.ppermute(x, "dp", [(1, 0), (2, 3)])
+    info = jnp.stack([me, plane, middle.astype(jnp.int32)]).astype(jnp.int32)
+    info_flip = jnp.stack([me, plane, 1 - middle.astype(jnp.int32)]).astype(jnp.int32)
+
+    packed = jax.ShapeDtypeStruct((width + META, LANES), bf16)
+    (own,) = call(pack_kernel, [packed], (out_grad, expert_ids, gate_weight))
+    near = along("dp", 1)(own)
+    across = inner(own)
+    hidden = call(
+        hidden_kernel,
+        [jax.ShapeDtypeStruct((rows, slots), bf16)] * planes,
+        (info, saved_hidden.reshape(slots, hidden_width)),
+        scratch=[pltpu.VMEM((planes, rows, slots), bf16)],
+    )
+    second_in = inner(near)
+    second_out = outward(across)
+    third_out = outward(second_in)
+    sets = [own, near, jnp.where(middle, across, second_out), jnp.where(middle, second_in, third_out)]
+    arrived = [hidden[0]] + [along("dp", o)(hidden[o]) for o in range(1, planes)]
+
+    blocks = []
+    for number, block in enumerate(sets):
+        bx, by = px(block), py(block)
+        diagonal = px(by) if number % 2 == 0 else py(bx)
+        mine = [block, bx, by, diagonal]
+        blocks.append(mine + [core(b) for b in mine])
+
+    flops = 2 * rows * width * 8 * tokens
+    acc = jax.ShapeDtypeStruct((rows, width), jnp.float32)
+    total, score = call(
+        own_kernel,
+        [acc, jax.ShapeDtypeStruct((8, LANES), jnp.float32)],
+        (info, arrived[0], saved_output.reshape(slots, width), *blocks[0]),
+        flops=flops,
+    )
+    (total,) = call(one_hidden_kernel, [acc], (info, arrived[1], total, *blocks[1]), flops=flops)
+    (total,) = call(next_kernel, [acc], (info, arrived[2], arrived[3], total, *blocks[2]), flops=flops)
+    (down_grad,) = call(
+        next_kernel,
+        [jax.ShapeDtypeStruct((rows, width), bf16)],
+        (info_flip, arrived[2], arrived[3], total, *blocks[3]),
+        flops=flops,
+    )
+
+    scores = score[None]
+    scores = jnp.concatenate([scores, px(scores)], axis=0)
+    scores = jnp.concatenate([scores, py(scores)], axis=0)
+    scores = jnp.concatenate([scores, core(scores)], axis=0)
+    offsets = [0, 2, 4, 6, 1, 3, 5, 7]
+    back = jnp.stack([scores[n, n] for n in range(8)])
+    wanted = (expert_ids ^ me)[:, :, None] == jnp.array(offsets, jnp.int32)[None, None, :]
+    route_grad = jnp.sum(jnp.where(wanted, back.T[:, None, :], 0.0), axis=-1)
+    return (down_grad.reshape(1, rows, width), route_grad)
+
+
+def fits(mesh, out_grad, expert_ids, gate_weight, saved_hidden, saved_output):
+    planes, experts = mesh.shape["dp"], mesh.shape["expert"]
+    tokens, width = out_grad.shape[0] // (planes * experts), out_grad.shape[1]
+    rest = width % LANES
+    return (
+        planes == 4
+        and experts == 8
+        and tokens == LANES
+        and 2 * saved_hidden.shape[3] == LANES
+        and saved_hidden.shape[4] % (8 * planes) == 0
+        and rest > 0
+        and rest % 8 == 0
+        and LANES % rest == 0
+    )
+
+
 def solution(mesh):
     placed = (
         P(("dp", "expert"), None),
@@ -63,10 +325,14 @@
         P("dp", "expert", None, None, None),
         P("dp", "expert", None, None, None),
     )
-    return jax.shard_map(
-        per_device,
-        mesh=mesh,
-        in_specs=placed,
-        out_specs=(P("expert", "dp", None), P(("dp", "expert"), None)),
-        check_vma=False,
-    )
+
+    def run(*arrays):
+        return jax.shard_map(
+            planes4 if fits(mesh, *arrays) else general,
+            mesh=mesh,
+            in_specs=placed,
+            out_specs=(P("expert", "dp", None), P(("dp", "expert"), None)),
+            check_vma=False,
+        )(*arrays)
+
+    return run

time: 150 us -> 144 us (0.960)
  starting transfers between devices: 12.5 us -> 36.1 us
  waiting for transfers between devices: 87.1 us -> 64.2 us
  Pallas kernels: 0 us -> 20 us
  between operations: 14.2 us -> 0.9 us
  matrix products: 6.1 us -> 0 us
  other arithmetic: 5.43 us -> 1.92 us
  local copies, waits for them, and re-layouts: 23.7 us -> 20.4 us
    ppermute x0 -> x39, waiting for transfers between devices: none -> 64.2 us  [the longest x35 60.4 us: along(): lax.ppermute(x, name, [(i, i ^ bit) for i in range(lax.axis_size(name))])]
    unnamed x2 -> x0, waiting for transfers between devices: 46.8 us -> none
    all_to_all x3 -> x0, waiting for transfers between devices: 40.4 us -> none  [the longest x1 20.9 us: per_device(): lax.all_to_all(sent, 'expert', split_axis=0, concat_axis=0, tiled=True)]
    ppermute x0 -> x39, starting transfers between devices: none -> 36.1 us  [the longest x35 30.8 us: along(): lax.ppermute(x, name, [(i, i ^ bit) for i in range(lax.axis_size(name))])]
    pallas_call x0 -> x6, Pallas kernels: none -> 20 us  [call(): pl.pallas_call(kernel, out_shape=outs, in_specs=[smem if a.ndim == 1 else...]
    all_to_all x3 -> x0, starting transfers between devices: 12.5 us -> none  [the longest x1 5.17 us: per_device(): lax.all_to_all(gate_slots.astype(jnp.bfloat16), 'expert', split_axis=0, c...]
    unnamed x9 -> x61, local copies, waits for them, and re-layouts: 12.6 us -> 20.4 us
    dot_general x2 -> x0, matrix products: 6.1 us -> none  [the longest x1 4.59 us: per_device(): lax.dot_general(hidden, scaled, (((0,), (0,)), ((), ())), preferred_eleme...]
  transfers between devices with their start and end apart: 4 -> 39, of which waited for: 4 -> 13; matrix products, arithmetic and copies ran while one was open for 10% -> 1% of each run, Pallas kernels for 0% -> 10%
where the time goes in v1:
time: 144 us; the launch traced here: 143 us
  waiting for transfers between devices  64.2 us (45%)
  starting transfers between devices  36.1 us (25%)
  local copies, waits for them, and re-layouts  20.4 us (14%)
  Pallas kernels  20 us (14%)
  other arithmetic  1.92 us (1%)
    ppermute x35, waiting for transfers between devices, along(): lax.ppermute(x, name, [(i, i ^ bit) for i in range(lax.axis_size(name))])  60.4 us
    ppermute x35, starting transfers between devices, along(): lax.ppermute(x, name, [(i, i ^ bit) for i in range(lax.axis_size(name))])  30.8 us
    unnamed x61, local copies, waits for them, and re-layouts  20.4 us
    pallas_call x6, Pallas kernels, call(): pl.pallas_call(kernel, out_shape=outs, in_specs=[smem if a.ndim == 1 else...  20 us
    ppermute x2, waiting for transfers between devices, planes4(): outward = lambda x: lax.ppermute(x, 'dp', [(1, 0), (2, 3)])  3.72 us
  transfers between devices with their start and end apart: 39, of which 13 were waited for; matrix products, arithmetic and copies ran while one was open for 1% of the time, Pallas kernels for 10%

profile of v1, /device:TPU:0, one launch (start us, length us, event | category | flops | bytes accessed | tf_op | source)
XLA Modules:
  0.0 143.5 jit_solution(14455996404980703248)
XLA Ops:
  0.6 1.3 copy.13.grad_ref
  2.0 1.4 copy.14.ids_ref
  3.4 1.4 copy.15.gate_ref
  4.8 0.8 copy-done.23
  5.6 0.8 copy-done.24
  6.5 1.0 shard_map.78.refs_0_
  7.5 3.0 %collective-permute-start.4 = (bf16[1456,128]{1,0:T(8,128)(2,1)}, bf16[1456,128]{1,0:T(8,128)(2,1)}, u32[]{:S(2)}, u32[]{:S(2)}) collective-permute-start(bf16[1456,128]{1,0:T(8,128)(2,1)} %shard_map.78.refs_0_), channel_id=1, source_target_pairs={{0,4},{1,5},{2,6},{3,7},{4,0},{5,1},{6,2},{7,3},{8,12},{9,13},{10,... | collective-permute-start | bytes 1118216 | tf_op jit(solution)/shard_map/ppermute | solution.py:245
  10.4 1.5 %collective-permute-start.3 = (bf16[1456,128]{1,0:T(8,128)(2,1)}, bf16[1456,128]{1,0:T(8,128)(2,1)}, u32[]{:S(2)}, u32[]{:S(2)}) collective-permute-start(bf16[1456,128]{1,0:T(8,128)(2,1)} %shard_map.78.refs_0_), channel_id=1, source_target_pairs={{0,2},{1,3},{2,0},{3,1},{4,6},{5,7},{6,4},{7,5},{8,10},{9,11},{10,... | collective-permute-start | bytes 1118216 | tf_op jit(solution)/shard_map/ppermute | solution.py:245
  11.9 7.5 %collective-permute-done.4.refs_2_ = bf16[1456,128]{1,0:T(8,128)(2,1)} collective-permute-done((bf16[1456,128]{1,0:T(8,128)(2,1)}, bf16[1456,128]{1,0:T(8,128)(2,1)}, u32[]{:S(2)}, u32[]{:S(2)}) %collective-permute-start.4) | collective-permute-done | bytes 372768 | tf_op jit(solution)/shard_map/ppermute | solution.py:245
  19.4 1.7 %collective-permute-start.5 = (bf16[1456,128]{1,0:T(8,128)(2,1)}, bf16[1456,128]{1,0:T(8,128)(2,1)}, u32[]{:S(2)}, u32[]{:S(2)}) collective-permute-start(bf16[1456,128]{1,0:T(8,128)(2,1)} %collective-permute-done.4.refs_2_), channel_id=1, source_target_pairs={{0,2},{1,3},{2,0},{3,1},{4,6},{5,7},{6,4},{7,5},{8,10},{9,11},{10,... | collective-permute-start | bytes 1118216 | tf_op jit(solution)/shard_map/ppermute | solution.py:245
  21.1 1.4 collective-permute-start.18
  22.5 3.7 %collective-permute-start.10 = (bf16[1456,128]{1,0:T(8,128)(2,1)}, bf16[1456,128]{1,0:T(8,128)(2,1)S(1)}, u32[]{:S(2)}, u32[]{:S(2)}) collective-permute-start(bf16[1456,128]{1,0:T(8,128)(2,1)} %shard_map.78.refs_0_), channel_id=1, source_target_pairs={{0,8},{8,0},{16,24},{24,16},{1,9},{9,1},{17,25},{25,17},{2,10},{10... | collective-permute-start | bytes 1118216 | tf_op jit(solution)/shard_map/ppermute | solution.py:245
  27.6 2.1 %collective-permute-done.5.refs_3_ = bf16[1456,128]{1,0:T(8,128)(2,1)} collective-permute-done((bf16[1456,128]{1,0:T(8,128)(2,1)}, bf16[1456,128]{1,0:T(8,128)(2,1)}, u32[]{:S(2)}, u32[]{:S(2)}) %collective-permute-start.5) | collective-permute-done | bytes 372768 | tf_op jit(solution)/shard_map/ppermute | solution.py:245
  29.6 1.3 collective-permute-start.19
  30.9 2.8 %collective-permute-done.10.refs_0_ = bf16[1456,128]{1,0:T(8,128)(2,1)S(1)} collective-permute-done((bf16[1456,128]{1,0:T(8,128)(2,1)}, bf16[1456,128]{1,0:T(8,128)(2,1)S(1)}, u32[]{:S(2)}, u32[]{:S(2)}) %collective-permute-start.10) | collective-permute-done | bytes 372768 | tf_op jit(solution)/shard_map/ppermute | solution.py:245
  33.7 1.4 collective-permute-start.27
  35.2 2.4 %shard_map.77 = (bf16[360,512]{1,0:T(8,128)(2,1)S(1)}, bf16[360,512]{1,0:T(8,128)(2,1)}, bf16[360,512]{1,0:T(8,128)(2,1)}, bf16[360,512]{1,0:T(8,128)(2,1)S(1)}) custom-call(s32[3]{0:T(128)S(1)} %pad_add_fusion.2.info_ref, bf16[512,1440]{1,0:T(8,128)(2,1)S(1)} %bitcast.26), custom_call_target="tpu_custom_call" | custom-call | bytes 2949132 | tf_op jit(solution)/shard_map/pallas_call | solution.py:223
  38.3 4.6 %collective-permute-start.2 = (bf16[360,512]{1,0:T(8,128)(2,1)}, bf16[360,512]{1,0:T(8,128)(2,1)S(1)}, u32[]{:S(2)}, u32[]{:S(2)}) collective-permute-start(bf16[360,512]{1,0:T(8,128)(2,1)} %get-tuple-element.10), channel_id=1, source_target_pairs={{0,8},{8,0},{16,24},{24,16},{1,9},{9,1},{17,25},{25,17},{2,10},{10... | collective-permute-start | bytes 1105928 | tf_op jit(solution)/shard_map/ppermute | solution.py:245
  42.9 1.0 copy-done.10
  43.9 5.3 %shard_map.79 = (f32[360,1440]{1,0:T(8,128)}, f32[8,128]{1,0:T(8,128)S(1)}) custom-call(s32[3]{0:T(128)S(1)} %pad_add_fusion.2.info_ref, bf16[360,512]{1,0:T(8,128)(2,1)S(1)} %get-tuple-element.11.hidden_ref, bf16[512,1440]{1,0:T(8,128)(2,1)S(1)} %bitcast.25, bf16[1456,128]{1,0:T(8,128)(2,1)} %shard_map.78.refs_0_, ...), custom_call_target="tpu_custom_call" | custom-call | flops 1061683200 | bytes 6902796 | tf_op jit(solution)/shard_map/pallas_call | solution.py:223
  49.9 5.7 %collective-permute-done.2.near_ref = bf16[360,512]{1,0:T(8,128)(2,1)S(1)} collective-permute-done((bf16[360,512]{1,0:T(8,128)(2,1)}, bf16[360,512]{1,0:T(8,128)(2,1)S(1)}, u32[]{:S(2)}, u32[]{:S(2)}) %collective-permute-start.2) | collective-permute-done | bytes 368672 | tf_op jit(solution)/shard_map/ppermute | solution.py:245
  56.3 3.3 %collective-permute-start.1 = (bf16[360,512]{1,0:T(8,128)(2,1)S(1)}, bf16[360,512]{1,0:T(8,128)(2,1)S(1)}, u32[]{:S(2)}, u32[]{:S(2)}) collective-permute-start(bf16[360,512]{1,0:T(8,128)(2,1)S(1)} %copy-done.26), channel_id=1, source_target_pairs={{0,24},{8,16},{16,8},{24,0},{1,25},{9,17},{17,9},{25,1},{2,26},{10... | collective-permute-start | bytes 1105928 | tf_op jit(solution)/shard_map/ppermute | solution.py:245
  59.6 13.3 %collective-permute-done.near_ref = bf16[360,512]{1,0:T(8,128)(2,1)S(1)} collective-permute-done((bf16[360,512]{1,0:T(8,128)(2,1)}, bf16[360,512]{1,0:T(8,128)(2,1)S(1)}, u32[]{:S(2)}, u32[]{:S(2)}) %collective-permute-start) | collective-permute-done | bytes 368672 | tf_op jit(solution)/shard_map/ppermute | solution.py:245
  73.4 1.5 %collective-permute-start.12 = (bf16[1456,128]{1,0:T(8,128)(2,1)S(1)}, bf16[1456,128]{1,0:T(8,128)(2,1)S(1)}, u32[]{:S(2)}, u32[]{:S(2)}) collective-permute-start(bf16[1456,128]{1,0:T(8,128)(2,1)S(1)} %collective-permute-done.10.refs_0_), channel_id=1, source_target_pairs={{0,4},{1,5},{2,6},{3,7},{4,0},{5,1},{6,2},{7,3},{8,12},{9,13},{10,... | collective-permute-start | bytes 1118216 | tf_op jit(solution)/shard_map/ppermute | solution.py:245
  74.9 1.3 collective-permute-start.28
  76.2 1.0 broadcast_select_fusion.1.refs_0_
  77.8 2.8 %collective-permute-done.11.refs_1_ = bf16[1456,128]{1,0:T(8,128)(2,1)S(1)} collective-permute-done((bf16[1456,128]{1,0:T(8,128)(2,1)S(1)}, bf16[1456,128]{1,0:T(8,128)(2,1)S(1)}, u32[]{:S(2)}, u32[]{:S(2)}) %collective-permute-start.11) | collective-permute-done | bytes 372768 | tf_op jit(solution)/shard_map/ppermute | solution.py:245
  80.7 1.5 %collective-permute-start.13 = (bf16[1456,128]{1,0:T(8,128)(2,1)S(1)}, bf16[1456,128]{1,0:T(8,128)(2,1)S(1)}, u32[]{:S(2)}, u32[]{:S(2)}) collective-permute-start(bf16[1456,128]{1,0:T(8,128)(2,1)S(1)} %collective-permute-done.11.refs_1_), channel_id=1, source_target_pairs={{0,4},{1,5},{2,6},{3,7},{4,0},{5,1},{6,2},{7,3},{8,12},{9,13},{10,... | collective-permute-start | bytes 1118216 | tf_op jit(solution)/shard_map/ppermute | solution.py:245
  82.2 1.7 %collective-permute-done.12.refs_2_ = bf16[1456,128]{1,0:T(8,128)(2,1)S(1)} collective-permute-done((bf16[1456,128]{1,0:T(8,128)(2,1)S(1)}, bf16[1456,128]{1,0:T(8,128)(2,1)S(1)}, u32[]{:S(2)}, u32[]{:S(2)}) %collective-permute-start.12) | collective-permute-done | bytes 372768 | tf_op jit(solution)/shard_map/ppermute | solution.py:245
  84.4 3.7 %collective-permute-done.28 = bf16[1456,128]{1,0:T(8,128)(2,1)S(1)} collective-permute-done((bf16[1456,128]{1,0:T(8,128)(2,1)}, bf16[1456,128]{1,0:T(8,128)(2,1)S(1)}, u32[]{:S(2)}, u32[]{:S(2)}) %collective-permute-start.28) | collective-permute-done | bytes 372768 | tf_op jit(solution)/shard_map/ppermute | solution.py:249
  88.6 9.6 %collective-permute-done.13.refs_3_ = bf16[1456,128]{1,0:T(8,128)(2,1)S(1)} collective-permute-done((bf16[1456,128]{1,0:T(8,128)(2,1)S(1)}, bf16[1456,128]{1,0:T(8,128)(2,1)S(1)}, u32[]{:S(2)}, u32[]{:S(2)}) %collective-permute-start.13) | collective-permute-done | bytes 372768 | tf_op jit(solution)/shard_map/ppermute | solution.py:245
  100.0 1.7 %collective-permute-start.29 = (bf16[1456,128]{1,0:T(8,128)(2,1)S(1)}, bf16[1456,128]{1,0:T(8,128)(2,1)}, u32[]{:S(2)}, u32[]{:S(2)}) collective-permute-start(bf16[1456,128]{1,0:T(8,128)(2,1)S(1)} %broadcast_select_fusion.refs_0_), channel_id=1, source_target_pairs={{0,2},{1,3},{2,0},{3,1},{4,6},{5,7},{6,4},{7,5},{8,10},{9,11},{10,... | collective-permute-start | bytes 1118216 | tf_op jit(solution)/shard_map/ppermute | solution.py:245
  102.4 7.4 %collective-permute-done.20.refs_1_ = bf16[1456,128]{1,0:T(8,128)(2,1)S(1)} collective-permute-done((bf16[1456,128]{1,0:T(8,128)(2,1)S(1)}, bf16[1456,128]{1,0:T(8,128)(2,1)S(1)}, u32[]{:S(2)}, u32[]{:S(2)}) %collective-permute-start.20) | collective-permute-done | bytes 372768 | tf_op jit(solution)/shard_map/ppermute | solution.py:245
  109.8 0.8 collective-permute-start.30
  110.6 0.8 copy-done.15
  111.4 1.0 collective-permute-start.22
  113.2 0.8 copy-done.7
  115.2 2.7 %collective-permute-done.29.refs_1_ = bf16[1456,128]{1,0:T(8,128)(2,1)} collective-permute-done((bf16[1456,128]{1,0:T(8,128)(2,1)S(1)}, bf16[1456,128]{1,0:T(8,128)(2,1)}, u32[]{:S(2)}, u32[]{:S(2)}) %collective-permute-start.29) | collective-permute-done | bytes 372768 | tf_op jit(solution)/shard_map/ppermute | solution.py:245
  117.9 0.8 collective-permute-start.31
  118.7 4.5 %collective-permute-done.22.refs_3_ = bf16[1456,128]{1,0:T(8,128)(2,1)} collective-permute-done((bf16[1456,128]{1,0:T(8,128)(2,1)S(1)}, bf16[1456,128]{1,0:T(8,128)(2,1)}, u32[]{:S(2)}, u32[]{:S(2)}) %collective-permute-start.22) | collective-permute-done | bytes 372768 | tf_op jit(solution)/shard_map/ppermute | solution.py:245
  126.8 1.0 copy-done.4
  127.8 1.0 copy-done.6
  128.8 1.0 copy-done.8
  129.8 1.0 copy-done.22
  130.8 3.4 %shard_map.80.acc_ref = f32[360,1440]{1,0:T(8,128)S(1)} custom-call(s32[3]{0:T(128)S(1)} %pad_add_fusion.2.info_ref, bf16[360,512]{1,0:T(8,128)(2,1)S(1)} %copy-done.22, f32[360,1440]{1,0:T(8,128)} %get-tuple-element.12.acc_ref, bf16[1456,128]{1,0:T(8,128)(2,1)S(1)} %collective-permute-done.10.refs_0_, ...), custom_call_target="tpu_custom_call" | custom-call | flops 1061683200 | bytes 7497740 | tf_op jit(solution)/shard_map/pallas_call | solution.py:223
  134.3 1.3 copy-done
  135.6 3.5 %shard_map.81.acc_ref = f32[360,1440]{1,0:T(8,128)S(1)} custom-call(s32[3]{0:T(128)S(1)} %pad_add_fusion.2.info_ref, bf16[360,512]{1,0:T(8,128)(2,1)S(1)} %collective-permute-done.near_ref, bf16[360,512]{1,0:T(8,128)(2,1)S(1)} %collective-permute-done.1.far_ref, f32[360,1440]{1,0:T(8,128)} %copy-done, bf16[1456,128]{1,0:T(8,128)(2,1)S(1)} %broadcast_select_fusion.1.refs_0_, ...), custom_call_target="tpu_custom_call" | custom-call | flops 1061683200 | bytes 7866380 | tf_op jit(solution)/shard_map/pallas_call | solution.py:223
  139.1 4.4 %shard_map.82 = bf16[360,1440]{1,0:T(8,128)(2,1)} custom-call(s32[3]{0:T(128)S(1)} %pad_add_fusion.info_ref, bf16[360,512]{1,0:T(8,128)(2,1)S(1)} %collective-permute-done.near_ref, bf16[360,512]{1,0:T(8,128)(2,1)S(1)} %collective-permute-done.1.far_ref, f32[360,1440]{1,0:T(8,128)S(1)} %shard_map.81.acc_ref, ...), custom_call_target="tpu_custom_call" | custom-call | flops 1061683200 | bytes 6829580 | tf_op jit(solution)/shard_map/pallas_call | solution.py:223
  (110 shorter events, 13.7 us)
Async XLA Ops:
  0.6 34.6 %copy-start.2 = (bf16[1,1,8,64,1440]{4,3,2,1,0:T(8,128)(2,1)S(1)}, bf16[1,1,8,64,1440]{4,3,2,1,0:T(8,128)(2,1)}, u32[]{:S(2)}) copy-start(bf16[1,1,8,64,1440]{4,3,2,1,0:T(8,128)(2,1)} %param.9) | copy-start | bytes 4423684
  0.6 42.3 %copy-start.1 = (bf16[1,1,8,64,1440]{4,3,2,1,0:T(8,128)(2,1)S(1)}, bf16[1,1,8,64,1440]{4,3,2,1,0:T(8,128)(2,1)}, u32[]{:S(2)}) copy-start(bf16[1,1,8,64,1440]{4,3,2,1,0:T(8,128)(2,1)} %param.10) | copy-start | bytes 4423684
  7.5 12.0 %collective-permute-start.4 = (bf16[1456,128]{1,0:T(8,128)(2,1)}, bf16[1456,128]{1,0:T(8,128)(2,1)}, u32[]{:S(2)}, u32[]{:S(2)}) collective-permute-start(bf16[1456,128]{1,0:T(8,128)(2,1)} %shard_map.78.refs_0_), channel_id=1, source_target_pairs={{0,4},{1,5},{2,6},{3,7},{4,0},{5,1},{6,2},{7,3},{8,12},{9,13},{10,... | collective-permute-start | bytes 1118216 | tf_op jit(solution)/shard_map/ppermute | solution.py:245
  10.4 15.8 %collective-permute-start.3 = (bf16[1456,128]{1,0:T(8,128)(2,1)}, bf16[1456,128]{1,0:T(8,128)(2,1)}, u32[]{:S(2)}, u32[]{:S(2)}) collective-permute-start(bf16[1456,128]{1,0:T(8,128)(2,1)} %shard_map.78.refs_0_), channel_id=1, source_target_pairs={{0,2},{1,3},{2,0},{3,1},{4,6},{5,7},{6,4},{7,5},{8,10},{9,11},{10,... | collective-permute-start | bytes 1118216 | tf_op jit(solution)/shard_map/ppermute | solution.py:245
  11.9 14.3 %collective-permute-start.6 = (bf16[1456,128]{1,0:T(8,128)(2,1)}, bf16[1456,128]{1,0:T(8,128)(2,1)S(1)}, u32[]{:S(2)}, u32[]{:S(2)}) collective-permute-start(bf16[1456,128]{1,0:T(8,128)(2,1)} %shard_map.78.refs_0_), channel_id=1, source_target_pairs={{0,1},{1,0},{2,3},{3,2},{4,5},{5,4},{6,7},{7,6},{8,9},{9,8},{10,11... | collective-permute-start | bytes 1118216 | tf_op jit(solution)/shard_map/ppermute | solution.py:245
  19.4 10.2 %collective-permute-start.5 = (bf16[1456,128]{1,0:T(8,128)(2,1)}, bf16[1456,128]{1,0:T(8,128)(2,1)}, u32[]{:S(2)}, u32[]{:S(2)}) collective-permute-start(bf16[1456,128]{1,0:T(8,128)(2,1)} %collective-permute-done.4.refs_2_), channel_id=1, source_target_pairs={{0,2},{1,3},{2,0},{3,1},{4,6},{5,7},{6,4},{7,5},{8,10},{9,11},{10,... | collective-permute-start | bytes 1118216 | tf_op jit(solution)/shard_map/ppermute | solution.py:245
  21.1 8.5 %collective-permute-start.18 = (bf16[1456,128]{1,0:T(8,128)(2,1)}, bf16[1456,128]{1,0:T(8,128)(2,1)}, u32[]{:S(2)}, u32[]{:S(2)}) collective-permute-start(bf16[1456,128]{1,0:T(8,128)(2,1)} %shard_map.78.refs_0_), channel_id=1, source_target_pairs={{8,16},{16,8},{9,17},{17,9},{10,18},{18,10},{11,19},{19,11},{12,20... | collective-permute-start | bytes 1118216 | tf_op jit(solution)/shard_map/ppermute | solution.py:248
  22.5 11.2 %collective-permute-start.10 = (bf16[1456,128]{1,0:T(8,128)(2,1)}, bf16[1456,128]{1,0:T(8,128)(2,1)S(1)}, u32[]{:S(2)}, u32[]{:S(2)}) collective-permute-start(bf16[1456,128]{1,0:T(8,128)(2,1)} %shard_map.78.refs_0_), channel_id=1, source_target_pairs={{0,8},{8,0},{16,24},{24,16},{1,9},{9,1},{17,25},{25,17},{2,10},{10... | collective-permute-start | bytes 1118216 | tf_op jit(solution)/shard_map/ppermute | solution.py:245
  26.3 12.0 %collective-permute-start.8 = (bf16[1456,128]{1,0:T(8,128)(2,1)}, bf16[1456,128]{1,0:T(8,128)(2,1)}, u32[]{:S(2)}, u32[]{:S(2)}) collective-permute-start(bf16[1456,128]{1,0:T(8,128)(2,1)} %collective-permute-done.4.refs_2_), channel_id=1, source_target_pairs={{0,1},{1,0},{2,3},{3,2},{4,5},{5,4},{6,7},{7,6},{8,9},{9,8},{10,11... | collective-permute-start | bytes 1118216 | tf_op jit(solution)/shard_map/ppermute | solution.py:245
  27.0 15.9 %collective-permute-start.7 = (bf16[1456,128]{1,0:T(8,128)(2,1)}, bf16[1456,128]{1,0:T(8,128)(2,1)}, u32[]{:S(2)}, u32[]{:S(2)}) collective-permute-start(bf16[1456,128]{1,0:T(8,128)(2,1)} %collective-permute-done.3.refs_1_), channel_id=1, source_target_pairs={{0,1},{1,0},{2,3},{3,2},{4,5},{5,4},{6,7},{7,6},{8,9},{9,8},{10,11... | collective-permute-start | bytes 1118216 | tf_op jit(solution)/shard_map/ppermute | solution.py:245
  29.6 13.3 %collective-permute-start.9 = (bf16[1456,128]{1,0:T(8,128)(2,1)}, bf16[1456,128]{1,0:T(8,128)(2,1)}, u32[]{:S(2)}, u32[]{:S(2)}) collective-permute-start(bf16[1456,128]{1,0:T(8,128)(2,1)} %collective-permute-done.5.refs_3_), channel_id=1, source_target_pairs={{0,1},{1,0},{2,3},{3,2},{4,5},{5,4},{6,7},{7,6},{8,9},{9,8},{10,11... | collective-permute-start | bytes 1118216 | tf_op jit(solution)/shard_map/ppermute | solution.py:245
  29.6 43.7 %collective-permute-start.19 = (bf16[1456,128]{1,0:T(8,128)(2,1)}, bf16[1456,128]{1,0:T(8,128)(2,1)}, u32[]{:S(2)}, u32[]{:S(2)}) collective-permute-start(bf16[1456,128]{1,0:T(8,128)(2,1)} %collective-permute-done.18), channel_id=1, source_target_pairs={{8,0},{16,24},{9,1},{17,25},{10,2},{18,26},{11,3},{19,27},{12,4},{... | collective-permute-start | bytes 1118216 | tf_op jit(solution)/shard_map/ppermute | solution.py:249
  33.7 41.2 %collective-permute-start.27 = (bf16[1456,128]{1,0:T(8,128)(2,1)S(1)}, bf16[1456,128]{1,0:T(8,128)(2,1)}, u32[]{:S(2)}, u32[]{:S(2)}) collective-permute-start(bf16[1456,128]{1,0:T(8,128)(2,1)S(1)} %collective-permute-done.10.refs_0_), channel_id=1, source_target_pairs={{8,16},{16,8},{9,17},{17,9},{10,18},{18,10},{11,19},{19,11},{12,20... | collective-permute-start | bytes 1118216 | tf_op jit(solution)/shard_map/ppermute | solution.py:248
  38.3 17.2 %collective-permute-start.2 = (bf16[360,512]{1,0:T(8,128)(2,1)}, bf16[360,512]{1,0:T(8,128)(2,1)S(1)}, u32[]{:S(2)}, u32[]{:S(2)}) collective-permute-start(bf16[360,512]{1,0:T(8,128)(2,1)} %get-tuple-element.10), channel_id=1, source_target_pairs={{0,8},{8,0},{16,24},{24,16},{1,9},{9,1},{17,25},{25,17},{2,10},{10... | collective-permute-start | bytes 1105928 | tf_op jit(solution)/shard_map/ppermute | solution.py:245
  42.9 29.9 %collective-permute-start = (bf16[360,512]{1,0:T(8,128)(2,1)}, bf16[360,512]{1,0:T(8,128)(2,1)S(1)}, u32[]{:S(2)}, u32[]{:S(2)}) collective-permute-start(bf16[360,512]{1,0:T(8,128)(2,1)} %get-tuple-element.8), channel_id=1, source_target_pairs={{0,16},{8,24},{16,0},{24,8},{1,17},{9,25},{17,1},{25,9},{2,18},{10... | collective-permute-start | bytes 1105928 | tf_op jit(solution)/shard_map/ppermute | solution.py:245
  43.9 5.9 %copy-start.27 = (s32[128,4]{0,1:T(4,128)S(1)}, s32[128,4]{0,1:T(4,128)}, u32[]{:S(2)}) copy-start(s32[128,4]{0,1:T(4,128)} %param.7) | copy-start | bytes 6148
  43.9 12.4 %copy-start.26 = (bf16[360,512]{1,0:T(8,128)(2,1)S(1)}, bf16[360,512]{1,0:T(8,128)(2,1)}, u32[]{:S(2)}) copy-start(bf16[360,512]{1,0:T(8,128)(2,1)} %copy-done.25) | copy-start | bytes 1105924
  49.3 76.9 %copy-start.28 = (s32[8]{0:T(128)S(1)}, s32[8]{0:T(128)}, u32[]{:S(2)}) copy-start(s32[8]{0:T(128)} %constant.16.clone) | copy-start | bytes 100
  49.3 25.6 %collective-permute-start.36 = (f32[1,8,128]{2,1,0:T(8,128)S(1)}, f32[1,8,128]{2,1,0:T(8,128)S(1)}, u32[]{:S(2)}, u32[]{:S(2)}) collective-permute-start(f32[1,8,128]{2,1,0:T(8,128)S(1)} %bitcast.27), channel_id=1, source_target_pairs={{0,2},{1,3},{2,0},{3,1},{4,6},{5,7},{6,4},{7,5},{8,10},{9,11},{10,... | collective-permute-start | bytes 12296 | tf_op jit(solution)/shard_map/ppermute | solution.py:245
  56.3 20.9 %collective-permute-start.1 = (bf16[360,512]{1,0:T(8,128)(2,1)S(1)}, bf16[360,512]{1,0:T(8,128)(2,1)S(1)}, u32[]{:S(2)}, u32[]{:S(2)}) collective-permute-start(bf16[360,512]{1,0:T(8,128)(2,1)S(1)} %copy-done.26), channel_id=1, source_target_pairs={{0,24},{8,16},{16,8},{24,0},{1,25},{9,17},{17,9},{25,1},{2,26},{10... | collective-permute-start | bytes 1105928 | tf_op jit(solution)/shard_map/ppermute | solution.py:245
  72.9 7.8 %collective-permute-start.11 = (bf16[1456,128]{1,0:T(8,128)(2,1)S(1)}, bf16[1456,128]{1,0:T(8,128)(2,1)S(1)}, u32[]{:S(2)}, u32[]{:S(2)}) collective-permute-start(bf16[1456,128]{1,0:T(8,128)(2,1)S(1)} %collective-permute-done.10.refs_0_), channel_id=1, source_target_pairs={{0,2},{1,3},{2,0},{3,1},{4,6},{5,7},{6,4},{7,5},{8,10},{9,11},{10,... | collective-permute-start | bytes 1118216 | tf_op jit(solution)/shard_map/ppermute | solution.py:245
  73.4 10.5 %collective-permute-start.12 = (bf16[1456,128]{1,0:T(8,128)(2,1)S(1)}, bf16[1456,128]{1,0:T(8,128)(2,1)S(1)}, u32[]{:S(2)}, u32[]{:S(2)}) collective-permute-start(bf16[1456,128]{1,0:T(8,128)(2,1)S(1)} %collective-permute-done.10.refs_0_), channel_id=1, source_target_pairs={{0,4},{1,5},{2,6},{3,7},{4,0},{5,1},{6,2},{7,3},{8,12},{9,13},{10,... | collective-permute-start | bytes 1118216 | tf_op jit(solution)/shard_map/ppermute | solution.py:245
  74.9 9.0 %collective-permute-start.14 = (bf16[1456,128]{1,0:T(8,128)(2,1)S(1)}, bf16[1456,128]{1,0:T(8,128)(2,1)S(1)}, u32[]{:S(2)}, u32[]{:S(2)}) collective-permute-start(bf16[1456,128]{1,0:T(8,128)(2,1)S(1)} %collective-permute-done.10.refs_0_), channel_id=1, source_target_pairs={{0,1},{1,0},{2,3},{3,2},{4,5},{5,4},{6,7},{7,6},{8,9},{9,8},{10,11... | collective-permute-start | bytes 1118216 | tf_op jit(solution)/shard_map/ppermute | solution.py:245
  74.9 13.2 %collective-permute-start.28 = (bf16[1456,128]{1,0:T(8,128)(2,1)}, bf16[1456,128]{1,0:T(8,128)(2,1)S(1)}, u32[]{:S(2)}, u32[]{:S(2)}) collective-permute-start(bf16[1456,128]{1,0:T(8,128)(2,1)} %collective-permute-done.27), channel_id=1, source_target_pairs={{8,0},{16,24},{9,1},{17,25},{10,2},{18,26},{11,3},{19,27},{12,4},{... | collective-permute-start | bytes 1118216 | tf_op jit(solution)/shard_map/ppermute | solution.py:249
  77.3 24.8 %collective-permute-start.21 = (bf16[1456,128]{1,0:T(8,128)(2,1)S(1)}, bf16[1456,128]{1,0:T(8,128)(2,1)S(1)}, u32[]{:S(2)}, u32[]{:S(2)}) collective-permute-start(bf16[1456,128]{1,0:T(8,128)(2,1)S(1)} %broadcast_select_fusion.1.refs_0_), channel_id=1, source_target_pairs={{0,4},{1,5},{2,6},{3,7},{4,0},{5,1},{6,2},{7,3},{8,12},{9,13},{10,... | collective-permute-start | bytes 1118216 | tf_op jit(solution)/shard_map/ppermute | solution.py:245
  80.7 17.5 %collective-permute-start.13 = (bf16[1456,128]{1,0:T(8,128)(2,1)S(1)}, bf16[1456,128]{1,0:T(8,128)(2,1)S(1)}, u32[]{:S(2)}, u32[]{:S(2)}) collective-permute-start(bf16[1456,128]{1,0:T(8,128)(2,1)S(1)} %collective-permute-done.11.refs_1_), channel_id=1, source_target_pairs={{0,4},{1,5},{2,6},{3,7},{4,0},{5,1},{6,2},{7,3},{8,12},{9,13},{10,... | collective-permute-start | bytes 1118216 | tf_op jit(solution)/shard_map/ppermute | solution.py:245
  83.8 14.7 %collective-permute-start.15 = (bf16[1456,128]{1,0:T(8,128)(2,1)S(1)}, bf16[1456,128]{1,0:T(8,128)(2,1)S(1)}, u32[]{:S(2)}, u32[]{:S(2)}) collective-permute-start(bf16[1456,128]{1,0:T(8,128)(2,1)S(1)} %collective-permute-done.11.refs_1_), channel_id=1, source_target_pairs={{0,1},{1,0},{2,3},{3,2},{4,5},{5,4},{6,7},{7,6},{8,9},{9,8},{10,11... | collective-permute-start | bytes 1118216 | tf_op jit(solution)/shard_map/ppermute | solution.py:245
  83.8 15.4 %collective-permute-start.16 = (bf16[1456,128]{1,0:T(8,128)(2,1)S(1)}, bf16[1456,128]{1,0:T(8,128)(2,1)S(1)}, u32[]{:S(2)}, u32[]{:S(2)}) collective-permute-start(bf16[1456,128]{1,0:T(8,128)(2,1)S(1)} %collective-permute-done.12.refs_2_), channel_id=1, source_target_pairs={{0,1},{1,0},{2,3},{3,2},{4,5},{5,4},{6,7},{7,6},{8,9},{9,8},{10,11... | collective-permute-start | bytes 1118216 | tf_op jit(solution)/shard_map/ppermute | solution.py:245
  88.1 13.7 %collective-permute-start.37 = (f32[2,8,128]{2,1,0:T(8,128)S(1)}, f32[2,8,128]{2,1,0:T(8,128)S(1)}, u32[]{:S(2)}, u32[]{:S(2)}) collective-permute-start(f32[2,8,128]{2,1,0:T(8,128)S(1)} %pad_maximum_fusion.1), channel_id=1, source_target_pairs={{0,4},{1,5},{2,6},{3,7},{4,0},{5,1},{6,2},{7,3},{8,12},{9,13},{10,... | collective-permute-start | bytes 24584 | tf_op jit(solution)/shard_map/ppermute | solution.py:245
  98.2 11.6 %collective-permute-start.20 = (bf16[1456,128]{1,0:T(8,128)(2,1)S(1)}, bf16[1456,128]{1,0:T(8,128)(2,1)S(1)}, u32[]{:S(2)}, u32[]{:S(2)}) collective-permute-start(bf16[1456,128]{1,0:T(8,128)(2,1)S(1)} %broadcast_select_fusion.1.refs_0_), channel_id=1, source_target_pairs={{0,2},{1,3},{2,0},{3,1},{4,6},{5,7},{6,4},{7,5},{8,10},{9,11},{10,... | collective-permute-start | bytes 1118216 | tf_op jit(solution)/shard_map/ppermute | solution.py:245
  99.3 11.4 %collective-permute-start.23 = (bf16[1456,128]{1,0:T(8,128)(2,1)S(1)}, bf16[1456,128]{1,0:T(8,128)(2,1)S(1)}, u32[]{:S(2)}, u32[]{:S(2)}) collective-permute-start(bf16[1456,128]{1,0:T(8,128)(2,1)S(1)} %broadcast_select_fusion.1.refs_0_), channel_id=1, source_target_pairs={{0,1},{1,0},{2,3},{3,2},{4,5},{5,4},{6,7},{7,6},{8,9},{9,8},{10,11... | collective-permute-start | bytes 1118216 | tf_op jit(solution)/shard_map/ppermute | solution.py:245
  100.0 17.9 %collective-permute-start.29 = (bf16[1456,128]{1,0:T(8,128)(2,1)S(1)}, bf16[1456,128]{1,0:T(8,128)(2,1)}, u32[]{:S(2)}, u32[]{:S(2)}) collective-permute-start(bf16[1456,128]{1,0:T(8,128)(2,1)S(1)} %broadcast_select_fusion.refs_0_), channel_id=1, source_target_pairs={{0,2},{1,3},{2,0},{3,1},{4,6},{5,7},{6,4},{7,5},{8,10},{9,11},{10,... | collective-permute-start | bytes 1118216 | tf_op jit(solution)/shard_map/ppermute | solution.py:245
  101.7 11.4 %collective-permute-start.17 = (bf16[1456,128]{1,0:T(8,128)(2,1)S(1)}, bf16[1456,128]{1,0:T(8,128)(2,1)S(1)}, u32[]{:S(2)}, u32[]{:S(2)}) collective-permute-start(bf16[1456,128]{1,0:T(8,128)(2,1)S(1)} %collective-permute-done.13.refs_3_), channel_id=1, source_target_pairs={{0,1},{1,0},{2,3},{3,2},{4,5},{5,4},{6,7},{7,6},{8,9},{9,8},{10,11... | collective-permute-start | bytes 1118216 | tf_op jit(solution)/shard_map/ppermute | solution.py:245
  102.0 10.4 %collective-permute-start.38 = (f32[4,8,128]{2,1,0:T(8,128)S(1)}, f32[4,8,128]{2,1,0:T(8,128)S(1)}, u32[]{:S(2)}, u32[]{:S(2)}) collective-permute-start(f32[4,8,128]{2,1,0:T(8,128)S(1)} %pad_maximum_fusion), channel_id=1, source_target_pairs={{0,1},{1,0},{2,3},{3,2},{4,5},{5,4},{6,7},{7,6},{8,9},{9,8},{10,11... | collective-permute-start | bytes 49160 | tf_op jit(solution)/shard_map/ppermute | solution.py:245
  109.8 15.4 %collective-permute-start.30 = (bf16[1456,128]{1,0:T(8,128)(2,1)S(1)}, bf16[1456,128]{1,0:T(8,128)(2,1)}, u32[]{:S(2)}, u32[]{:S(2)}) collective-permute-start(bf16[1456,128]{1,0:T(8,128)(2,1)S(1)} %broadcast_select_fusion.refs_0_), channel_id=1, source_target_pairs={{0,4},{1,5},{2,6},{3,7},{4,0},{5,1},{6,2},{7,3},{8,12},{9,13},{10,... | collective-permute-start | bytes 1118216 | tf_op jit(solution)/shard_map/ppermute | solution.py:245
  111.4 11.8 %collective-permute-start.22 = (bf16[1456,128]{1,0:T(8,128)(2,1)S(1)}, bf16[1456,128]{1,0:T(8,128)(2,1)}, u32[]{:S(2)}, u32[]{:S(2)}) collective-permute-start(bf16[1456,128]{1,0:T(8,128)(2,1)S(1)} %collective-permute-done.21.refs_2_), channel_id=1, source_target_pairs={{0,2},{1,3},{2,0},{3,1},{4,6},{5,7},{6,4},{7,5},{8,10},{9,11},{10,... | collective-permute-start | bytes 1118216 | tf_op jit(solution)/shard_map/ppermute | solution.py:245
  112.4 10.8 %collective-permute-start.25 = (bf16[1456,128]{1,0:T(8,128)(2,1)S(1)}, bf16[1456,128]{1,0:T(8,128)(2,1)S(1)}, u32[]{:S(2)}, u32[]{:S(2)}) collective-permute-start(bf16[1456,128]{1,0:T(8,128)(2,1)S(1)} %collective-permute-done.21.refs_2_), channel_id=1, source_target_pairs={{0,1},{1,0},{2,3},{3,2},{4,5},{5,4},{6,7},{7,6},{8,9},{9,8},{10,11... | collective-permute-start | bytes 1118216 | tf_op jit(solution)/shard_map/ppermute | solution.py:245
  114.0 10.5 %collective-permute-start.24 = (bf16[1456,128]{1,0:T(8,128)(2,1)S(1)}, bf16[1456,128]{1,0:T(8,128)(2,1)S(1)}, u32[]{:S(2)}, u32[]{:S(2)}) collective-permute-start(bf16[1456,128]{1,0:T(8,128)(2,1)S(1)} %collective-permute-done.20.refs_1_), channel_id=1, source_target_pairs={{0,1},{1,0},{2,3},{3,2},{4,5},{5,4},{6,7},{7,6},{8,9},{9,8},{10,11... | collective-permute-start | bytes 1118216 | tf_op jit(solution)/shard_map/ppermute | solution.py:245
  117.9 8.2 %collective-permute-start.31 = (bf16[1456,128]{1,0:T(8,128)(2,1)}, bf16[1456,128]{1,0:T(8,128)(2,1)}, u32[]{:S(2)}, u32[]{:S(2)}) collective-permute-start(bf16[1456,128]{1,0:T(8,128)(2,1)} %collective-permute-done.29.refs_1_), channel_id=1, source_target_pairs={{0,4},{1,5},{2,6},{3,7},{4,0},{5,1},{6,2},{7,3},{8,12},{9,13},{10,... | collective-permute-start | bytes 1118216 | tf_op jit(solution)/shard_map/ppermute | solution.py:245
  123.2 15.9 %collective-permute-start.32 = (bf16[1456,128]{1,0:T(8,128)(2,1)S(1)}, bf16[1456,128]{1,0:T(8,128)(2,1)}, u32[]{:S(2)}, u32[]{:S(2)}) collective-permute-start(bf16[1456,128]{1,0:T(8,128)(2,1)S(1)} %broadcast_select_fusion.refs_0_), channel_id=1, source_target_pairs={{0,1},{1,0},{2,3},{3,2},{4,5},{5,4},{6,7},{7,6},{8,9},{9,8},{10,11... | collective-permute-start | bytes 1118216 | tf_op jit(solution)/shard_map/ppermute | solution.py:245
  124.0 15.1 %collective-permute-start.33 = (bf16[1456,128]{1,0:T(8,128)(2,1)}, bf16[1456,128]{1,0:T(8,128)(2,1)}, u32[]{:S(2)}, u32[]{:S(2)}) collective-permute-start(bf16[1456,128]{1,0:T(8,128)(2,1)} %collective-permute-done.29.refs_1_), channel_id=1, source_target_pairs={{0,1},{1,0},{2,3},{3,2},{4,5},{5,4},{6,7},{7,6},{8,9},{9,8},{10,11... | collective-permute-start | bytes 1118216 | tf_op jit(solution)/shard_map/ppermute | solution.py:245
  125.2 10.3 %collective-permute-start.26 = (bf16[1456,128]{1,0:T(8,128)(2,1)}, bf16[1456,128]{1,0:T(8,128)(2,1)}, u32[]{:S(2)}, u32[]{:S(2)}) collective-permute-start(bf16[1456,128]{1,0:T(8,128)(2,1)} %collective-permute-done.22.refs_3_), channel_id=1, source_target_pairs={{0,1},{1,0},{2,3},{3,2},{4,5},{5,4},{6,7},{7,6},{8,9},{9,8},{10,11... | collective-permute-start | bytes 1118216 | tf_op jit(solution)/shard_map/ppermute | solution.py:245
  125.3 13.9 %collective-permute-start.34 = (bf16[1456,128]{1,0:T(8,128)(2,1)}, bf16[1456,128]{1,0:T(8,128)(2,1)}, u32[]{:S(2)}, u32[]{:S(2)}) collective-permute-start(bf16[1456,128]{1,0:T(8,128)(2,1)} %collective-permute-done.30.refs_2_), channel_id=1, source_target_pairs={{0,1},{1,0},{2,3},{3,2},{4,5},{5,4},{6,7},{7,6},{8,9},{9,8},{10,11... | collective-permute-start | bytes 1118216 | tf_op jit(solution)/shard_map/ppermute | solution.py:245
  126.1 13.0 %collective-permute-start.35 = (bf16[1456,128]{1,0:T(8,128)(2,1)}, bf16[1456,128]{1,0:T(8,128)(2,1)}, u32[]{:S(2)}, u32[]{:S(2)}) collective-permute-start(bf16[1456,128]{1,0:T(8,128)(2,1)} %collective-permute-done.31.refs_3_), channel_id=1, source_target_pairs={{0,1},{1,0},{2,3},{3,2},{4,5},{5,4},{6,7},{7,6},{8,9},{9,8},{10,11... | collective-permute-start | bytes 1118216 | tf_op jit(solution)/shard_map/ppermute | solution.py:245
  130.8 4.8 %copy-start.14 = (bf16[1456,128]{1,0:T(8,128)(2,1)S(1)}, bf16[1456,128]{1,0:T(8,128)(2,1)}, u32[]{:S(2)}) copy-start(bf16[1456,128]{1,0:T(8,128)(2,1)} %copy-done.13) | copy-start | bytes 1118212
  130.8 4.8 %copy-start.16 = (bf16[1456,128]{1,0:T(8,128)(2,1)S(1)}, bf16[1456,128]{1,0:T(8,128)(2,1)}, u32[]{:S(2)}) copy-start(bf16[1456,128]{1,0:T(8,128)(2,1)} %copy-done.15) | copy-start | bytes 1118212
  130.8 4.8 %copy-start.18 = (bf16[1456,128]{1,0:T(8,128)(2,1)S(1)}, bf16[1456,128]{1,0:T(8,128)(2,1)}, u32[]{:S(2)}) copy-start(bf16[1456,128]{1,0:T(8,128)(2,1)} %copy-done.17) | copy-start | bytes 1118212
  130.8 4.8 %copy-start.20 = (bf16[1456,128]{1,0:T(8,128)(2,1)S(1)}, bf16[1456,128]{1,0:T(8,128)(2,1)}, u32[]{:S(2)}) copy-start(bf16[1456,128]{1,0:T(8,128)(2,1)} %copy-done.19) | copy-start | bytes 1118212
  (20 other events, 21.1 us)

commit v2 on v0

--- a/solution.py
+++ b/solution.py
@@ -1,7 +1,14 @@
+import functools
+
 import jax
 import jax.numpy as jnp
 from jax import lax
+from jax.experimental import pallas as pl
+from jax.experimental.pallas import tpu as pltpu
 from jax.sharding import PartitionSpec as P
+
+LANES = 128
+META = 16
 
 
 def slot_numbers(ids, experts, capacity):
@@ -12,7 +19,7 @@
     return ids * capacity + position
 
 
-def per_device(out_grad, expert_ids, gate_weight, saved_hidden, saved_output):
+def general(out_grad, expert_ids, gate_weight, saved_hidden, saved_output):
     tokens_here, width = out_grad.shape
     experts = lax.axis_size("expert")
     capacity = saved_hidden.shape[3]
@@ -55,6 +62,297 @@
     return (down_grad, route_grad)
 
 
+def pack_kernel(grad_ref, ids_ref, gate_ref, out_ref):
+    width, tokens = grad_ref.shape
+    out_ref[:width, :] = grad_ref[...]
+    expert = lax.broadcasted_iota(jnp.int32, (META // 2, tokens), 0)
+    dense = jnp.zeros((META // 2, tokens), jnp.float32)
+    for k in range(ids_ref.shape[0]):
+        dense = dense + jnp.where(expert == ids_ref[k:k + 1, :], gate_ref[k:k + 1, :], 0.0)
+    high = dense.astype(jnp.bfloat16).astype(jnp.float32)
+    out_ref[width:, :] = jnp.concatenate([high, dense - high], axis=0).astype(jnp.bfloat16)
+
+
+def rows_of_core(ref, core, cols):
+    return jnp.concatenate([ref[c, core, :, cols] for c in range(ref.shape[0])], axis=0)
+
+
+def turn_kernel(info_ref, hidden_ref, keep_ref, leave_ref):
+    core = info_ref[0] & 1
+    width = hidden_ref.shape[3]
+    for a in range(0, width, LANES):
+        cols = slice(a, min(a + LANES, width))
+        keep_ref[cols, :] = rows_of_core(hidden_ref, core, cols).T
+        leave_ref[cols, :] = rows_of_core(hidden_ref, 1 - core, cols).T
+
+
+def quarter_kernel(info_ref, keep_ref, got_ref, *rest):
+    outs, scratch = rest[:-1], rest[-1]
+    planes, rows, half = len(outs), outs[0].shape[0], keep_ref.shape[1]
+    for q in range(planes):
+        scratch[q, :, :half] = keep_ref[q * rows:(q + 1) * rows, :]
+        scratch[q, :, half:] = got_ref[q * rows:(q + 1) * rows, :]
+    for o in range(planes):
+        outs[o][...] = scratch[info_ref[1] ^ o]
+
+
+def saved_kernel(info_ref, saved_ref, out_ref):
+    theirs = 1 - (info_ref[0] & 1)
+    rows, width = saved_ref.shape[0] * saved_ref.shape[2], saved_ref.shape[3]
+    full, rest = width // LANES, width % LANES
+    for j in range(full):
+        out_ref[j * rows:(j + 1) * rows, :] = rows_of_core(saved_ref, theirs, slice(j * LANES, (j + 1) * LANES))
+    tail = rows_of_core(saved_ref, theirs, slice(full * LANES, width)).astype(jnp.float32)
+    step = rows * rest // LANES
+    out_ref[full * rows:, :] = jnp.concatenate(
+        [tail[a * step:(a + 1) * step] for a in range(LANES // rest)], axis=1
+    ).astype(jnp.bfloat16)
+
+
+def block_tables(info_ref, blocks):
+    me = info_ref[0]
+    core, chip = me & 1, me >> 1
+    offsets = [0, 1 + core, 2 - core, 3]
+    width = blocks[0].shape[0] - META
+    rows = lax.broadcasted_iota(jnp.int32, (META, LANES), 0)
+    metas = [ref[width:, :].astype(jnp.float32) for ref in blocks]
+    gates = []
+    for expert in (me, me ^ 1):
+        picked = jnp.logical_or(rows == expert, rows == expert + META // 2)
+        gates += [jnp.sum(jnp.where(picked, meta, 0.0), axis=0, keepdims=True) for meta in metas]
+    gates = jnp.concatenate(gates, axis=0)
+    routed = gates > 0.0
+    before = lax.broadcasted_iota(jnp.int32, (LANES, LANES), 0) < lax.broadcasted_iota(jnp.int32, (LANES, LANES), 1)
+    earlier = jnp.dot(
+        routed.astype(jnp.bfloat16), before.astype(jnp.bfloat16), preferred_element_type=jnp.float32
+    ).astype(jnp.int32)
+    position = jnp.where(routed, earlier, -LANES * LANES)
+    number = len(blocks)
+    out = []
+    for w in range(2):
+        gate = jnp.concatenate([gates[w * number + n:w * number + n + 1] for n in range(number)], axis=1)
+        place = jnp.concatenate(
+            [position[w * number + n:w * number + n + 1] + (chip ^ offsets[n]) * (LANES // 2) for n in range(number)],
+            axis=1,
+        )
+        out.append((gate, place))
+    return out
+
+
+def chosen(place, slots):
+    return lax.broadcasted_iota(jnp.int32, (slots, place.shape[1]), 0) == place
+
+
+def gather_hidden(hidden, table):
+    gate, place = table
+    placed = jnp.dot(
+        hidden, chosen(place, hidden.shape[1]).astype(jnp.bfloat16), preferred_element_type=jnp.float32
+    )
+    return (placed * gate).astype(jnp.bfloat16)
+
+
+def chunks(width, step=2 * LANES):
+    return [(a, min(a + step, width)) for a in range(0, width, step)]
+
+
+def tokens_of(blocks, a, b):
+    return jnp.concatenate([ref[a:b, :] for ref in blocks], axis=1)
+
+
+def accumulate(hidden, blocks, acc_refs, out_refs):
+    width = blocks[0].shape[0] - META
+    rows = out_refs[0].shape[0]
+    for a, b in chunks(width):
+        total = lax.dot_general(
+            hidden, tokens_of(blocks, a, b), (((1,), (1,)), ((), ())), preferred_element_type=jnp.float32
+        )
+        for w, out_ref in enumerate(out_refs):
+            value = total[w * rows:(w + 1) * rows]
+            if acc_refs:
+                value = value + acc_refs[w][:, a:b]
+            out_ref[:, a:b] = value.astype(out_ref.dtype)
+
+
+def hidden_part(info_ref, hidden_refs, w):
+    half = hidden_refs[0].shape[1] // 2
+    picked = [ref[:, w * half:(w + 1) * half] for ref in hidden_refs]
+    if len(picked) == 1:
+        return picked[0]
+    return jnp.where(info_ref[2] != 0, picked[1], picked[0])
+
+
+def sum_kernel(hiddens, experts, started, info_ref, *refs):
+    hidden_refs, refs = refs[:hiddens], refs[hiddens:]
+    number = len(experts)
+    outs, refs = refs[-number:], refs[:-number]
+    accs, blocks = (refs[:number], list(refs[number:])) if started else ((), list(refs))
+    tables = block_tables(info_ref, blocks)
+    hidden = [gather_hidden(hidden_part(info_ref, hidden_refs, w), tables[w]) for w in experts]
+    accumulate(hidden[0] if number == 1 else jnp.concatenate(hidden, axis=0), blocks, accs, outs)
+
+
+def score_kernel(info_ref, saved_ref, got_ref, *refs):
+    blocks, score_ref = list(refs[:-1]), refs[-1]
+    tables = block_tables(info_ref, blocks)
+    core = info_ref[0] & 1
+    rows, width = saved_ref.shape[0] * saved_ref.shape[2], saved_ref.shape[3]
+    full, rest = width // LANES, width % LANES
+    total = jnp.zeros((2 * rows, len(blocks) * LANES), jnp.float32)
+    for a, b in chunks(width):
+        pieces = []
+        for j in range(a // LANES, -(-b // LANES)):
+            if j < full:
+                pieces.append(got_ref[j * rows:(j + 1) * rows, :])
+            else:
+                tail = got_ref[full * rows:, :]
+                pieces.append(
+                    jnp.concatenate([tail[:, n * rest:(n + 1) * rest] for n in range(LANES // rest)], axis=0)
+                )
+        theirs = pieces[0] if len(pieces) == 1 else jnp.concatenate(pieces, axis=1)
+        saved = jnp.concatenate([rows_of_core(saved_ref, core, slice(a, b)), theirs], axis=0)
+        total = total + jnp.dot(saved, tokens_of(blocks, a, b), preferred_element_type=jnp.float32)
+    scores = []
+    for w in range(2):
+        row = jnp.sum(
+            jnp.where(chosen(tables[w][1], rows), total[w * rows:(w + 1) * rows], 0.0), axis=0, keepdims=True
+        )
+        scores += [row[:, n * LANES:(n + 1) * LANES] for n in range(len(blocks))]
+    score_ref[...] = jnp.concatenate(scores, axis=0)
+
+
+def add_kernel(a_ref, b_ref, out_ref):
+    out_ref[...] = (a_ref[...] + b_ref[...].astype(jnp.float32)).astype(out_ref.dtype)
+
+
+def call(kernel, outs, args, scratch=(), flops=0, limit=16):
+    smem, vmem = pl.BlockSpec(memory_space=pltpu.SMEM), pl.BlockSpec(memory_space=pltpu.VMEM)
+    moved = sum(a.size * a.dtype.itemsize for a in (*args, *outs))
+    return pl.pallas_call(
+        kernel,
+        out_shape=outs,
+        in_specs=[smem if a.ndim == 1 else vmem for a in args],
+        out_specs=[vmem] * len(outs),
+        scratch_shapes=list(scratch),
+        compiler_params=pltpu.CompilerParams(vmem_limit_bytes=limit * 1024 * 1024),
+        cost_estimate=pl.CostEstimate(flops=flops, bytes_accessed=moved, transcendentals=0),
+    )(*args)
+
+
+def after(value, *earlier):
+    return lax.optimization_barrier((value, *earlier))[0]
+
+
+def planes4(out_grad, expert_ids, gate_weight, saved_hidden, saved_output):
+    tokens, width = out_grad.shape
+    hidden_width = saved_hidden.shape[4]
+    sources, capacity = saved_hidden.shape[2:4]
+    slots = sources * capacity
+    planes = lax.axis_size("dp")
+    rows = hidden_width // planes
+    me, plane = lax.axis_index("expert"), lax.axis_index("dp")
+    middle = jnp.logical_or(plane == 1, plane == 2)
+    bf16 = jnp.bfloat16
+
+    def permute(name, target):
+        return lambda x: lax.ppermute(x, name, [(i, target(i)) for i in range(lax.axis_size(name))])
+
+    core = permute("expert", lambda i: i ^ 1)
+    first = permute("expert", lambda i: i ^ (4 if i & 1 else 2))
+    second = permute("expert", lambda i: i ^ (2 if i & 1 else 4))
+    diagonal = permute("expert", lambda i: i ^ 6)
+    near_plane, far2, far3 = (permute("dp", lambda i, o=o: i ^ o) for o in (1, 2, 3))
+    inner = lambda x: lax.ppermute(x, "dp", [(1, 2), (2, 1)])
+    outward = lambda x: lax.ppermute(x, "dp", [(1, 0), (2, 3)])
+    info = jnp.stack([me, plane, middle.astype(jnp.int32)]).astype(jnp.int32)
+    info_flip = jnp.stack([me, plane, 1 - middle.astype(jnp.int32)]).astype(jnp.int32)
+    hidden4 = saved_hidden.reshape(sources // 2, 2, capacity, hidden_width)
+    saved4 = saved_output.reshape(sources // 2, 2, capacity, width)
+
+    def shaped(*shape, dtype=bf16):
+        return jax.ShapeDtypeStruct(shape, dtype)
+
+    acc = shaped(rows, width, dtype=jnp.float32)
+    flops = 4 * rows * width * 4 * tokens
+
+    (own,) = call(pack_kernel, [shaped(width + META, tokens)], (out_grad.T, expert_ids.T, gate_weight.T))
+    near, across = near_plane(own), inner(own)
+    a0, b0 = first(own), second(own)
+    kept, leaving = call(turn_kernel, [shaped(hidden_width, slots // 2)] * 2, (info, hidden4))
+    hidden = call(
+        quarter_kernel,
+        [shaped(rows, slots)] * planes,
+        (info, kept, core(leaving)),
+        scratch=[pltpu.VMEM((planes, rows, slots), bf16)],
+    )
+    (saved_leaving,) = call(saved_kernel, [shaped(width * slots // 2 // LANES, LANES)], (info, saved4))
+    saved_got = core(saved_leaving)
+    second_in, second_out = inner(near), outward(across)
+    d0 = second(a0)
+    a1, b1 = first(near), second(near)
+    totals = call(
+        functools.partial(sum_kernel, 1, (0, 1), False), [acc, acc], (info, hidden[0], own, a0, b0, d0), flops=flops
+    )
+    (score,) = call(
+        score_kernel, [shaped(8, LANES, dtype=jnp.float32)], (info, saved4, saved_got, own, a0, b0, d0),
+        flops=4 * slots * width * tokens,
+    )
+    third_out = outward(second_in)
+    h3 = far3(after(hidden[3], second_in, second_out))
+    block2 = jnp.where(middle, across, second_out)
+    d1 = second(a1)
+    a2, b2 = first(after(block2, a1)), second(after(block2, b1))
+    block3 = jnp.where(middle, second_in, third_out)
+    h2 = far2(after(hidden[2], h3, third_out))
+    h1 = near_plane(after(hidden[1], h3, third_out))
+    d2 = second(a2)
+    a3, b3 = first(after(block3, a2)), second(after(block3, b2))
+    d3 = second(a3)
+
+    ra, rb, rd = first(score), second(score), diagonal(score)
+
+    totals = call(
+        functools.partial(sum_kernel, 1, (0, 1), True), [acc, acc], (info, h1, *totals, near, a1, b1, d1), flops=flops
+    )
+    own_total, other_total = call(
+        functools.partial(sum_kernel, 2, (0, 1), True), [acc, acc],
+        (info, h2, h3, *totals, block2, a2, b2, d2), flops=flops,
+    )
+    (leaving_part,) = call(
+        functools.partial(sum_kernel, 2, (1,), True), [shaped(rows, width)],
+        (info_flip, h2, h3, other_total, block3, a3, b3, d3), flops=flops // 2,
+    )
+    got_part = core(leaving_part)
+    (own_total,) = call(
+        functools.partial(sum_kernel, 2, (0,), True), [acc],
+        (info_flip, h2, h3, own_total, block3, a3, b3, d3), flops=flops // 2,
+    )
+    (down_grad,) = call(add_kernel, [shaped(rows, width)], (own_total, got_part))
+
+    odd = me & 1
+    offsets = jnp.stack([0 * odd, 2 + 2 * odd, 4 - 2 * odd, 6 + 0 * odd])
+    offsets = jnp.concatenate([offsets, offsets ^ 1])
+    back = jnp.stack([r[4 * w + n] for w in range(2) for n, r in enumerate((score, ra, rb, rd))])
+    wanted = (expert_ids.T ^ me)[:, None, :] == offsets[None, :, None]
+    route_grad = jnp.sum(jnp.where(wanted, back[None], 0.0), axis=1).T
+    return (down_grad.reshape(1, rows, width), route_grad)
+
+
+def fits(mesh, out_grad, expert_ids, gate_weight, saved_hidden, saved_output):
+    planes, experts = mesh.shape["dp"], mesh.shape["expert"]
+    tokens, width = out_grad.shape[0] // (planes * experts), out_grad.shape[1]
+    rest = width % LANES
+    return (
+        planes == 4
+        and experts == 8
+        and tokens == LANES
+        and 2 * saved_hidden.shape[3] == LANES
+        and saved_hidden.shape[4] % (8 * planes) == 0
+        and rest > 0
+        and rest % 8 == 0
+        and LANES % rest == 0
+    )
+
+
 def solution(mesh):
     placed = (
         P(("dp", "expert"), None),
@@ -63,10 +361,14 @@
         P("dp", "expert", None, None, None),
         P("dp", "expert", None, None, None),
     )
-    return jax.shard_map(
-        per_device,
-        mesh=mesh,
-        in_specs=placed,
-        out_specs=(P("expert", "dp", None), P(("dp", "expert"), None)),
-        check_vma=False,
-    )
+
+    def run(*arrays):
+        return jax.shard_map(
+            planes4 if fits(mesh, *arrays) else general,
+            mesh=mesh,
+            in_specs=placed,
+            out_specs=(P("expert", "dp", None), P(("dp", "expert"), None)),
+            check_vma=False,
+        )(*arrays)
+
+    return run

time: 150 us -> 103 us (0.69)
  waiting for transfers between devices: 87.1 us -> 24.9 us
  starting transfers between devices: 12.5 us -> 40.3 us
  Pallas kernels: 0 us -> 21.3 us
  between operations: 14.2 us -> 0.97 us
  local copies, waits for them, and re-layouts: 23.7 us -> 11.9 us
  matrix products: 6.1 us -> 0 us
  other arithmetic: 5.43 us -> 2.74 us
    unnamed x2 -> x0, waiting for transfers between devices: 46.8 us -> none
    all_to_all x3 -> x0, waiting for transfers between devices: 40.4 us -> none  [the longest x1 20.9 us: per_device(): lax.all_to_all(sent, 'expert', split_axis=0, concat_axis=0, tiled=True)]
    ppermute x0 -> x26, starting transfers between devices: none -> 40.3 us  [the longest x22 35.6 us: permute(): lax.ppermute(x, name, [(i, target(i)) for i in range(lax.axis_size(name))])]
    ppermute x0 -> x26, waiting for transfers between devices: none -> 24.9 us  [the longest x22 18.8 us: permute(): lax.ppermute(x, name, [(i, target(i)) for i in range(lax.axis_size(name))])]
    pallas_call x0 -> x11, Pallas kernels: none -> 21.3 us  [call(): pl.pallas_call(kernel, out_shape=outs, in_specs=[smem if a.ndim == 1 else...]
    all_to_all x3 -> x0, starting transfers between devices: 12.5 us -> none  [the longest x1 5.17 us: per_device(): lax.all_to_all(gate_slots.astype(jnp.bfloat16), 'expert', split_axis=0, c...]
    dot_general x2 -> x0, matrix products: 6.1 us -> none  [the longest x1 4.59 us: per_device(): lax.dot_general(hidden, scaled, (((0,), (0,)), ((), ())), preferred_eleme...]
    reshape x4 -> x0, local copies, waits for them, and re-layouts: 4.04 us -> none  [the longest x1 2.9 us: per_device(): picked = picked.reshape(tokens_here, expert_ids.shape[1], width)]
  transfers between devices with their start and end apart: 4 -> 26, of which waited for: 4 -> 6; matrix products, arithmetic and copies ran while one was open for 10% -> 3% of each run, Pallas kernels for 0% -> 18%
where the time goes in v2:
time: 103 us; the launch traced here: 102 us
  starting transfers between devices  40.3 us (39%)
  waiting for transfers between devices  24.9 us (24%)
  Pallas kernels  21.3 us (21%)
  local copies, waits for them, and re-layouts  11.9 us (12%)
  other arithmetic  2.74 us (3%)
    ppermute x22, starting transfers between devices, permute(): lax.ppermute(x, name, [(i, target(i)) for i in range(lax.axis_size(name))])  35.6 us
    pallas_call x11, Pallas kernels, call(): pl.pallas_call(kernel, out_shape=outs, in_specs=[smem if a.ndim == 1 else...  21.3 us
    ppermute x22, waiting for transfers between devices, permute(): lax.ppermute(x, name, [(i, target(i)) for i in range(lax.axis_size(name))])  18.8 us
    unnamed x48, local copies, waits for them, and re-layouts  11.8 us
    ppermute x2, waiting for transfers between devices, planes4(): outward = lambda x: lax.ppermute(x, 'dp', [(1, 0), (2, 3)])  6.13 us
    ppermute x2, starting transfers between devices, planes4(): outward = lambda x: lax.ppermute(x, 'dp', [(1, 0), (2, 3)])  2.57 us
    ppermute x2, starting transfers between devices, planes4(): inner = lambda x: lax.ppermute(x, 'dp', [(1, 2), (2, 1)])  2.11 us
  transfers between devices with their start and end apart: 26, of which 6 were waited for; matrix products, arithmetic and copies ran while one was open for 3% of the time, Pallas kernels for 18%

profile of v2, /device:TPU:0, one launch (start us, length us, event | category | flops | bytes accessed | tf_op | source)
XLA Modules:
  0.0 102.0 jit_solution(14219549194100033168)
XLA Ops:
  0.6 1.1 %copy-done.17 = bf16[128,1440]{0,1:T(8,128)(2,1)S(1)} copy-done((bf16[128,1440]{0,1:T(8,128)(2,1)S(1)}, bf16[128,1440]{0,1:T(8,128)(2,1)}, u32[]{:S(2)}) %copy-start.17) | copy-done | bytes 368664
  1.7 0.7 copy-done.18
  2.4 0.7 copy-done.20
  3.1 3.1 %collective-permute-start.1 = (bf16[1456,128]{1,0:T(8,128)(2,1)S(1)}, bf16[1456,128]{1,0:T(8,128)(2,1)S(1)}, u32[]{:S(2)}, u32[]{:S(2)}) collective-permute-start(bf16[1456,128]{1,0:T(8,128)(2,1)S(1)} %shard_map.70.refs_1_.refs_0_), channel_id=1, source_target_pairs={{0,8},{8,0},{16,24},{24,16},{1,9},{9,1},{17,25},{25,17},{2,10},{10... | collective-permute-start | bytes 1118216 | tf_op jit(solution)/shard_map/ppermute | solution.py:257
  6.2 1.4 %collective-permute-start.3 = (bf16[1456,128]{1,0:T(8,128)(2,1)S(1)}, bf16[1456,128]{1,0:T(8,128)(2,1)}, u32[]{:S(2)}, u32[]{:S(2)}) collective-permute-start(bf16[1456,128]{1,0:T(8,128)(2,1)S(1)} %shard_map.70.refs_1_.refs_0_), channel_id=1, source_target_pairs={{8,16},{16,8},{9,17},{17,9},{10,18},{18,10},{11,19},{19,11},{12,20... | collective-permute-start | bytes 1118216 | tf_op jit(solution)/shard_map/ppermute | solution.py:264
  7.7 7.2 %collective-permute-done.1.refs_3_ = bf16[1456,128]{1,0:T(8,128)(2,1)S(1)} collective-permute-done((bf16[1456,128]{1,0:T(8,128)(2,1)S(1)}, bf16[1456,128]{1,0:T(8,128)(2,1)S(1)}, u32[]{:S(2)}, u32[]{:S(2)}) %collective-permute-start.1) | collective-permute-done | bytes 372768 | tf_op jit(solution)/shard_map/ppermute | solution.py:257
  14.9 0.7 collective-permute-start.2
  15.6 1.3 %collective-permute-start.4 = (bf16[1456,128]{1,0:T(8,128)(2,1)}, bf16[1456,128]{1,0:T(8,128)(2,1)}, u32[]{:S(2)}, u32[]{:S(2)}) collective-permute-start(bf16[1456,128]{1,0:T(8,128)(2,1)} %collective-permute-done.3), channel_id=1, source_target_pairs={{8,0},{16,24},{9,1},{17,25},{10,2},{18,26},{11,3},{19,27},{12,4},{... | collective-permute-start | bytes 1118216 | tf_op jit(solution)/shard_map/ppermute | solution.py:265
  17.0 1.4 %copy-done.3 = bf16[1,1,8,64,1440]{4,3,2,1,0:T(8,128)(2,1)S(1)} copy-done((bf16[1,1,8,64,1440]{4,3,2,1,0:T(8,128)(2,1)S(1)}, bf16[1,1,8,64,1440]{4,3,2,1,0:T(8,128)(2,1)}, u32[]{:S(2)}) %copy-start.3) | copy-done | bytes 1474584
  18.4 1.0 shard_map.68
  19.5 1.7 %collective-permute-start.9 = (bf16[1456,128]{1,0:T(8,128)(2,1)S(1)}, bf16[1456,128]{1,0:T(8,128)(2,1)S(1)}, u32[]{:S(2)}, u32[]{:S(2)}) collective-permute-start(bf16[1456,128]{1,0:T(8,128)(2,1)S(1)} %shard_map.70.refs_1_.refs_0_), channel_id=1, source_target_pairs={{0,2},{1,5},{2,0},{3,7},{4,6},{5,1},{6,4},{7,3},{8,10},{9,13},{10,... | collective-permute-start | bytes 1118216 | tf_op jit(solution)/shard_map/ppermute | solution.py:257
  21.6 1.7 %collective-permute-start.13 = (bf16[1456,128]{1,0:T(8,128)(2,1)S(1)}, bf16[1456,128]{1,0:T(8,128)(2,1)S(1)}, u32[]{:S(2)}, u32[]{:S(2)}) collective-permute-start(bf16[1456,128]{1,0:T(8,128)(2,1)S(1)} %collective-permute-done.1.refs_3_), channel_id=1, source_target_pairs={{0,4},{1,3},{2,6},{3,1},{4,0},{5,7},{6,2},{7,5},{8,12},{9,11},{10,... | collective-permute-start | bytes 1118216 | tf_op jit(solution)/shard_map/ppermute | solution.py:257
  23.2 6.1 %collective-permute-done.4 = bf16[1456,128]{1,0:T(8,128)(2,1)} collective-permute-done((bf16[1456,128]{1,0:T(8,128)(2,1)}, bf16[1456,128]{1,0:T(8,128)(2,1)}, u32[]{:S(2)}, u32[]{:S(2)}) %collective-permute-start.4) | collective-permute-done | bytes 372768 | tf_op jit(solution)/shard_map/ppermute | solution.py:265
  29.4 1.3 %collective-permute-start.6 = (bf16[1456,128]{1,0:T(8,128)(2,1)S(1)}, bf16[1456,128]{1,0:T(8,128)(2,1)S(1)}, u32[]{:S(2)}, u32[]{:S(2)}) collective-permute-start(bf16[1456,128]{1,0:T(8,128)(2,1)S(1)} %collective-permute-done.2), channel_id=1, source_target_pairs={{8,0},{16,24},{9,1},{17,25},{10,2},{18,26},{11,3},{19,27},{12,4},{... | collective-permute-start | bytes 1118216 | tf_op jit(solution)/shard_map/ppermute | solution.py:265
  30.7 1.8 %broadcast_select_fusion.1.refs_4_ = bf16[1456,128]{1,0:T(8,128)(2,1)} fusion(bf16[1456,128]{1,0:T(8,128)(2,1)} %collective-permute-done.3, bf16[1456,128]{1,0:T(8,128)(2,1)} %collective-permute-done.4, pred[]{:T(512)S(6)} %or.3), kind=kLoop, calls=%fused_computation.1 | loop fusion | flops 186368 | bytes 1118209 | tf_op jit(solution)/shard_map/jit(_where)/select_n | solution.py:301
  32.5 2.7 %collective-permute-done.12.refs_4_ = bf16[1456,128]{1,0:T(8,128)(2,1)} collective-permute-done((bf16[1456,128]{1,0:T(8,128)(2,1)S(1)}, bf16[1456,128]{1,0:T(8,128)(2,1)}, u32[]{:S(2)}, u32[]{:S(2)}) %collective-permute-start.12) | collective-permute-done | bytes 372768 | tf_op jit(solution)/shard_map/ppermute | solution.py:257
  35.2 1.7 %collective-permute-start.15 = (bf16[1456,128]{1,0:T(8,128)(2,1)}, bf16[1456,128]{1,0:T(8,128)(2,1)S(1)}, u32[]{:S(2)}, u32[]{:S(2)}) collective-permute-start(bf16[1456,128]{1,0:T(8,128)(2,1)} %broadcast_select_fusion.1.refs_4_), channel_id=1, source_target_pairs={{0,2},{1,5},{2,0},{3,7},{4,6},{5,1},{6,4},{7,3},{8,10},{9,13},{10,... | collective-permute-start | bytes 1118216 | tf_op jit(solution)/shard_map/ppermute | solution.py:257
  36.8 0.7 shard_map.77
  37.6 1.5 %shard_map.69 = (bf16[360,512]{1,0:T(8,128)(2,1)S(1)}, bf16[360,512]{1,0:T(8,128)(2,1)}, bf16[360,512]{1,0:T(8,128)(2,1)S(1)}, bf16[360,512]{1,0:T(8,128)(2,1)S(1)}) custom-call(s32[3]{0:T(128)S(1)} %pad_add_fusion.2.info_ref, bf16[1440,256]{1,0:T(8,128)(2,1)S(1)} %get-tuple-element.21.keep_ref, bf16[1440,256]{1,0:T(8,128)(2,1)S(1)} %collective-permute-done.got_ref), custom_call_target="tpu_custom_call" | custom-call | bytes 2949132 | tf_op jit(solution)/shard_map/pallas_call | solution.py:230
  39.1 0.8 copy-done.21
  39.9 0.7 copy-done.22
  40.6 1.5 %collective-permute-start.10 = (bf16[1456,128]{1,0:T(8,128)(2,1)S(1)}, bf16[1456,128]{1,0:T(8,128)(2,1)S(1)}, u32[]{:S(2)}, u32[]{:S(2)}) collective-permute-start(bf16[1456,128]{1,0:T(8,128)(2,1)S(1)} %shard_map.70.refs_1_.refs_0_), channel_id=1, source_target_pairs={{0,4},{1,3},{2,6},{3,1},{4,0},{5,7},{6,2},{7,5},{8,12},{9,11},{10,... | collective-permute-start | bytes 1118216 | tf_op jit(solution)/shard_map/ppermute | solution.py:257
  42.6 3.6 %collective-permute-start.5 = (bf16[360,512]{1,0:T(8,128)(2,1)S(1)}, bf16[360,512]{1,0:T(8,128)(2,1)S(1)}, u32[]{:S(2)}, u32[]{:S(2)}) collective-permute-start(bf16[360,512]{1,0:T(8,128)(2,1)S(1)} %get-tuple-element.25), channel_id=1, source_target_pairs={{0,24},{8,16},{16,8},{24,0},{1,25},{9,17},{17,9},{25,1},{2,26},{10... | collective-permute-start | bytes 1105928 | tf_op jit(solution)/shard_map/ppermute | solution.py:257
  46.3 1.5 %collective-permute-start.16 = (bf16[1456,128]{1,0:T(8,128)(2,1)}, bf16[1456,128]{1,0:T(8,128)(2,1)}, u32[]{:S(2)}, u32[]{:S(2)}) collective-permute-start(bf16[1456,128]{1,0:T(8,128)(2,1)} %broadcast_select_fusion.1.refs_4_), channel_id=1, source_target_pairs={{0,4},{1,3},{2,6},{3,1},{4,0},{5,7},{6,2},{7,5},{8,12},{9,11},{10,... | collective-permute-start | bytes 1118216 | tf_op jit(solution)/shard_map/ppermute | solution.py:257
  48.2 0.7 copy-done.15
  48.9 1.5 %collective-permute-start.14 = (bf16[1456,128]{1,0:T(8,128)(2,1)}, bf16[1456,128]{1,0:T(8,128)(2,1)}, u32[]{:S(2)}, u32[]{:S(2)}) collective-permute-start(bf16[1456,128]{1,0:T(8,128)(2,1)} %collective-permute-done.12.refs_4_), channel_id=1, source_target_pairs={{0,4},{1,3},{2,6},{3,1},{4,0},{5,7},{6,2},{7,5},{8,12},{9,11},{10,... | collective-permute-start | bytes 1118216 | tf_op jit(solution)/shard_map/ppermute | solution.py:257
  50.4 4.6 %collective-permute-done.5.refs_1_ = bf16[360,512]{1,0:T(8,128)(2,1)S(1)} collective-permute-done((bf16[360,512]{1,0:T(8,128)(2,1)S(1)}, bf16[360,512]{1,0:T(8,128)(2,1)S(1)}, u32[]{:S(2)}, u32[]{:S(2)}) %collective-permute-start.5) | collective-permute-done | bytes 368672 | tf_op jit(solution)/shard_map/ppermute | solution.py:257
  55.6 0.9 copy-done.4
  56.4 8.5 %collective-permute-start.8 = (bf16[360,512]{1,0:T(8,128)(2,1)}, bf16[360,512]{1,0:T(8,128)(2,1)}, u32[]{:S(2)}, u32[]{:S(2)}) collective-permute-start(bf16[360,512]{1,0:T(8,128)(2,1)} %get-tuple-element.28), channel_id=1, source_target_pairs={{0,8},{8,0},{16,24},{24,16},{1,9},{9,1},{17,25},{25,17},{2,10},{10... | collective-permute-start | bytes 1105928 | tf_op jit(solution)/shard_map/ppermute | solution.py:257
  65.0 2.0 %collective-permute-start.7 = (bf16[360,512]{1,0:T(8,128)(2,1)}, bf16[360,512]{1,0:T(8,128)(2,1)S(1)}, u32[]{:S(2)}, u32[]{:S(2)}) collective-permute-start(bf16[360,512]{1,0:T(8,128)(2,1)} %copy-done.21), channel_id=1, source_target_pairs={{0,16},{8,24},{16,0},{24,8},{1,17},{9,25},{17,1},{25,9},{2,18},{10... | collective-permute-start | bytes 1105928 | tf_op jit(solution)/shard_map/ppermute | solution.py:257
  67.0 1.5 %collective-permute-start.17 = (bf16[1456,128]{1,0:T(8,128)(2,1)}, bf16[1456,128]{1,0:T(8,128)(2,1)}, u32[]{:S(2)}, u32[]{:S(2)}) collective-permute-start(bf16[1456,128]{1,0:T(8,128)(2,1)} %copy-done.10), channel_id=1, source_target_pairs={{0,4},{1,3},{2,6},{3,1},{4,0},{5,7},{6,2},{7,5},{8,12},{9,11},{10,... | collective-permute-start | bytes 1118216 | tf_op jit(solution)/shard_map/ppermute | solution.py:257
  69.1 1.5 %collective-permute-start.20 = (bf16[1456,128]{1,0:T(8,128)(2,1)S(1)}, bf16[1456,128]{1,0:T(8,128)(2,1)}, u32[]{:S(2)}, u32[]{:S(2)}) collective-permute-start(bf16[1456,128]{1,0:T(8,128)(2,1)S(1)} %collective-permute-done.18.refs_4_), channel_id=1, source_target_pairs={{0,4},{1,3},{2,6},{3,1},{4,0},{5,7},{6,2},{7,5},{8,12},{9,11},{10,... | collective-permute-start | bytes 1118216 | tf_op jit(solution)/shard_map/ppermute | solution.py:257
  70.8 1.1 %copy-done.5 = bf16[2880,128]{1,0:T(8,128)(2,1)S(1)} copy-done((bf16[2880,128]{1,0:T(8,128)(2,1)S(1)}, bf16[2880,128]{1,0:T(8,128)(2,1)}, u32[]{:S(2)}) %copy-start.5) | copy-done | bytes 737304
  71.9 1.0 copy-done.13
  72.9 1.0 copy-done.16
  73.9 2.1 %shard_map.78 = f32[8,128]{1,0:T(8,128)S(1)} custom-call(s32[3]{0:T(128)S(1)} %pad_add_fusion.2.info_ref, bf16[4,2,64,1440]{3,2,1,0:T(8,128)(2,1)S(1)} %bitcast.15, bf16[2880,128]{1,0:T(8,128)(2,1)S(1)} %copy-done.5, bf16[1456,128]{1,0:T(8,128)(2,1)S(1)} %shard_map.70.refs_1_.refs_0_, bf16[1456,128]{1,0:T(8,128)(2,1)S(1)} %copy-done.13, ...), custom_call_target="tpu_custom_call" | custom-call | flops 377487360 | bytes 3706892 | tf_op jit(solution)/shard_map/pallas_call | solution.py:230
  76.0 2.8 %shard_map.71 = (f32[360,1440]{1,0:T(8,128)S(1)}, f32[360,1440]{1,0:T(8,128)S(1)}) custom-call(s32[3]{0:T(128)S(1)} %pad_add_fusion.2.info_ref, bf16[360,512]{1,0:T(8,128)(2,1)S(1)} %copy-done.23, bf16[1456,128]{1,0:T(8,128)(2,1)S(1)} %shard_map.70.refs_1_.refs_0_, bf16[1456,128]{1,0:T(8,128)(2,1)S(1)} %copy-done.14, bf16[1456,128]{1,0:T(8,128)(2,1)S(1)} %copy-done.16, ...), custom_call_target="tpu_custom_call" | custom-call | flops 1061683200 | bytes 6006796 | tf_op jit(solution)/shard_map/pallas_call | solution.py:230
  78.8 3.8 %collective-permute-done.8.refs_0_ = bf16[360,512]{1,0:T(8,128)(2,1)} collective-permute-done((bf16[360,512]{1,0:T(8,128)(2,1)}, bf16[360,512]{1,0:T(8,128)(2,1)}, u32[]{:S(2)}, u32[]{:S(2)}) %collective-permute-start.8) | collective-permute-done | bytes 368672 | tf_op jit(solution)/shard_map/ppermute | solution.py:257
  82.6 0.5 collective-permute-start.25
  83.1 3.0 %shard_map.72 = (f32[360,1440]{1,0:T(8,128)S(1)}, f32[360,1440]{1,0:T(8,128)S(1)}) custom-call(s32[3]{0:T(128)S(1)} %pad_add_fusion.2.info_ref, bf16[360,512]{1,0:T(8,128)(2,1)} %collective-permute-done.8.refs_0_, f32[360,1440]{1,0:T(8,128)S(1)} %get-tuple-element.30.refs_1_, f32[360,1440]{1,0:T(8,128)S(1)} %get-tuple-element.31.refs_2_, ...), custom_call_target="tpu_custom_call" | custom-call | flops 1061683200 | bytes 10153996 | tf_op jit(solution)/shard_map/pallas_call | solution.py:230
  86.1 1.6 %collective-permute-start.24 = (f32[8,128]{1,0:T(8,128)S(1)}, f32[8,128]{1,0:T(8,128)S(1)}, u32[]{:S(2)}, u32[]{:S(2)}) collective-permute-start(f32[8,128]{1,0:T(8,128)S(1)} %shard_map.78), channel_id=1, source_target_pairs={{0,4},{1,3},{2,6},{3,1},{4,0},{5,7},{6,2},{7,5},{8,12},{9,11},{10,... | collective-permute-start | bytes 12296 | tf_op jit(solution)/shard_map/ppermute | solution.py:257
  87.7 1.4 %collective-permute-start.23 = (f32[8,128]{1,0:T(8,128)S(1)}, f32[8,128]{1,0:T(8,128)S(1)}, u32[]{:S(2)}, u32[]{:S(2)}) collective-permute-start(f32[8,128]{1,0:T(8,128)S(1)} %shard_map.78), channel_id=1, source_target_pairs={{0,2},{1,5},{2,0},{3,7},{4,6},{5,1},{6,4},{7,3},{8,10},{9,13},{10,... | collective-permute-start | bytes 12296 | tf_op jit(solution)/shard_map/ppermute | solution.py:257
  89.2 2.9 %shard_map.73 = (f32[360,1440]{1,0:T(8,128)S(1)}, f32[360,1440]{1,0:T(8,128)S(1)}) custom-call(s32[3]{0:T(128)S(1)} %pad_add_fusion.2.info_ref, bf16[360,512]{1,0:T(8,128)(2,1)S(1)} %collective-permute-done.7.refs_0_, bf16[360,512]{1,0:T(8,128)(2,1)S(1)} %collective-permute-done.5.refs_1_, f32[360,1440]{1,0:T(8,128)S(1)} %get-tuple-element.32.refs_2_, ...), custom_call_target="tpu_custom_call" | custom-call | flops 1061683200 | bytes 10522636 | tf_op jit(solution)/shard_map/pallas_call | solution.py:230
  92.1 2.7 %shard_map.75 = bf16[360,1440]{1,0:T(8,128)(2,1)S(1)} custom-call(s32[3]{0:T(128)S(1)} %pad_add_fusion.info_ref, bf16[360,512]{1,0:T(8,128)(2,1)S(1)} %collective-permute-done.7.refs_0_, bf16[360,512]{1,0:T(8,128)(2,1)S(1)} %collective-permute-done.5.refs_1_, f32[360,1440]{1,0:T(8,128)S(1)} %get-tuple-element.39.refs_2_, ...), custom_call_target="tpu_custom_call" | custom-call | flops 530841600 | bytes 5338636 | tf_op jit(solution)/shard_map/pallas_call | solution.py:230
  95.0 0.7 select_reduce_fusion
  95.7 1.6 %copy-done.2 = f32[360,1440]{1,0:T(8,128)S(1)} copy-done((f32[360,1440]{1,0:T(8,128)S(1)}, f32[360,1440]{1,0:T(8,128)}, u32[]{:S(2)}) %copy-start.2) | copy-done | bytes 2073624
  97.3 2.2 %shard_map.74.a_ref = f32[360,1440]{1,0:T(8,128)S(1)} custom-call(s32[3]{0:T(128)S(1)} %pad_add_fusion.info_ref, bf16[360,512]{1,0:T(8,128)(2,1)S(1)} %collective-permute-done.7.refs_0_, bf16[360,512]{1,0:T(8,128)(2,1)S(1)} %collective-permute-done.5.refs_1_, f32[360,1440]{1,0:T(8,128)S(1)} %copy-done.2, bf16[1456,128]{1,0:T(8,128)(2,1)S(1)} %broadcast_select_fusion.refs_3_, ...), custom_call_target="tpu_custom_call" | custom-call | flops 530841600 | bytes 6375436 | tf_op jit(solution)/shard_map/pallas_call | solution.py:230
  99.5 2.5 %shard_map.76 = bf16[360,1440]{1,0:T(8,128)(2,1)} custom-call(f32[360,1440]{1,0:T(8,128)S(1)} %shard_map.74.a_ref, bf16[360,1440]{1,0:T(8,128)(2,1)} %collective-permute-done.21.b_ref), custom_call_target="tpu_custom_call" | custom-call | bytes 4147200 | tf_op jit(solution)/shard_map/pallas_call | solution.py:230
  (76 shorter events, 3.0 us)
Async XLA Ops:
  0.6 36.2 %copy-start = (bf16[1,1,8,64,1440]{4,3,2,1,0:T(8,128)(2,1)S(1)}, bf16[1,1,8,64,1440]{4,3,2,1,0:T(8,128)(2,1)}, u32[]{:S(2)}) copy-start(bf16[1,1,8,64,1440]{4,3,2,1,0:T(8,128)(2,1)} %param.9) | copy-start | bytes 4423684
  0.6 1.1 %copy-start.17 = (bf16[128,1440]{0,1:T(8,128)(2,1)S(1)}, bf16[128,1440]{0,1:T(8,128)(2,1)}, u32[]{:S(2)}) copy-start(bf16[128,1440]{0,1:T(8,128)(2,1)} %param.5) | copy-start | bytes 1105924
  3.1 11.8 %collective-permute-start.1 = (bf16[1456,128]{1,0:T(8,128)(2,1)S(1)}, bf16[1456,128]{1,0:T(8,128)(2,1)S(1)}, u32[]{:S(2)}, u32[]{:S(2)}) collective-permute-start(bf16[1456,128]{1,0:T(8,128)(2,1)S(1)} %shard_map.70.refs_1_.refs_0_), channel_id=1, source_target_pairs={{0,8},{8,0},{16,24},{24,16},{1,9},{9,1},{17,25},{25,17},{2,10},{10... | collective-permute-start | bytes 1118216 | tf_op jit(solution)/shard_map/ppermute | solution.py:257
  6.2 9.4 %collective-permute-start.3 = (bf16[1456,128]{1,0:T(8,128)(2,1)S(1)}, bf16[1456,128]{1,0:T(8,128)(2,1)}, u32[]{:S(2)}, u32[]{:S(2)}) collective-permute-start(bf16[1456,128]{1,0:T(8,128)(2,1)S(1)} %shard_map.70.refs_1_.refs_0_), channel_id=1, source_target_pairs={{8,16},{16,8},{9,17},{17,9},{10,18},{18,10},{11,19},{19,11},{12,20... | collective-permute-start | bytes 1118216 | tf_op jit(solution)/shard_map/ppermute | solution.py:264
  14.9 22.6 %copy-start.6 = (bf16[1456,128]{1,0:T(8,128)(2,1)}, bf16[1456,128]{1,0:T(8,128)(2,1)S(1)}, u32[]{:S(2)}) copy-start(bf16[1456,128]{1,0:T(8,128)(2,1)S(1)} %collective-permute-done.1.refs_3_) | copy-start | bytes 1118212
  14.9 6.6 %collective-permute-start.2 = (bf16[1456,128]{1,0:T(8,128)(2,1)S(1)}, bf16[1456,128]{1,0:T(8,128)(2,1)S(1)}, u32[]{:S(2)}, u32[]{:S(2)}) collective-permute-start(bf16[1456,128]{1,0:T(8,128)(2,1)S(1)} %collective-permute-done.1.refs_3_), channel_id=1, source_target_pairs={{8,16},{16,8},{9,17},{17,9},{10,18},{18,10},{11,19},{19,11},{12,20... | collective-permute-start | bytes 1118216 | tf_op jit(solution)/shard_map/ppermute | solution.py:264
  15.6 13.8 %collective-permute-start.4 = (bf16[1456,128]{1,0:T(8,128)(2,1)}, bf16[1456,128]{1,0:T(8,128)(2,1)}, u32[]{:S(2)}, u32[]{:S(2)}) collective-permute-start(bf16[1456,128]{1,0:T(8,128)(2,1)} %collective-permute-done.3), channel_id=1, source_target_pairs={{8,0},{16,24},{9,1},{17,25},{10,2},{18,26},{11,3},{19,27},{12,4},{... | collective-permute-start | bytes 1118216 | tf_op jit(solution)/shard_map/ppermute | solution.py:265
  17.0 1.4 %copy-start.3 = (bf16[1,1,8,64,1440]{4,3,2,1,0:T(8,128)(2,1)S(1)}, bf16[1,1,8,64,1440]{4,3,2,1,0:T(8,128)(2,1)}, u32[]{:S(2)}) copy-start(bf16[1,1,8,64,1440]{4,3,2,1,0:T(8,128)(2,1)} %param.8) | copy-start | bytes 4423684
  19.4 18.1 %collective-permute-start = (bf16[1440,256]{1,0:T(8,128)(2,1)S(1)}, bf16[1440,256]{1,0:T(8,128)(2,1)S(1)}, u32[]{:S(2)}, u32[]{:S(2)}) collective-permute-start(bf16[1440,256]{1,0:T(8,128)(2,1)S(1)} %get-tuple-element.22), channel_id=1, source_target_pairs={{0,1},{1,0},{2,3},{3,2},{4,5},{5,4},{6,7},{7,6},{8,9},{9,8},{10,11... | collective-permute-start | bytes 2211848 | tf_op jit(solution)/shard_map/ppermute | solution.py:257
  19.5 21.1 %collective-permute-start.9 = (bf16[1456,128]{1,0:T(8,128)(2,1)S(1)}, bf16[1456,128]{1,0:T(8,128)(2,1)S(1)}, u32[]{:S(2)}, u32[]{:S(2)}) collective-permute-start(bf16[1456,128]{1,0:T(8,128)(2,1)S(1)} %shard_map.70.refs_1_.refs_0_), channel_id=1, source_target_pairs={{0,2},{1,5},{2,0},{3,7},{4,6},{5,1},{6,4},{7,3},{8,10},{9,13},{10,... | collective-permute-start | bytes 1118216 | tf_op jit(solution)/shard_map/ppermute | solution.py:257
  21.2 14.0 %collective-permute-start.12 = (bf16[1456,128]{1,0:T(8,128)(2,1)S(1)}, bf16[1456,128]{1,0:T(8,128)(2,1)}, u32[]{:S(2)}, u32[]{:S(2)}) collective-permute-start(bf16[1456,128]{1,0:T(8,128)(2,1)S(1)} %collective-permute-done.1.refs_3_), channel_id=1, source_target_pairs={{0,2},{1,5},{2,0},{3,7},{4,6},{5,1},{6,4},{7,3},{8,10},{9,13},{10,... | collective-permute-start | bytes 1118216 | tf_op jit(solution)/shard_map/ppermute | solution.py:257
  21.6 20.6 %collective-permute-start.13 = (bf16[1456,128]{1,0:T(8,128)(2,1)S(1)}, bf16[1456,128]{1,0:T(8,128)(2,1)S(1)}, u32[]{:S(2)}, u32[]{:S(2)}) collective-permute-start(bf16[1456,128]{1,0:T(8,128)(2,1)S(1)} %collective-permute-done.1.refs_3_), channel_id=1, source_target_pairs={{0,4},{1,3},{2,6},{3,1},{4,0},{5,7},{6,2},{7,5},{8,12},{9,11},{10,... | collective-permute-start | bytes 1118216 | tf_op jit(solution)/shard_map/ppermute | solution.py:257
  29.4 13.3 %collective-permute-start.6 = (bf16[1456,128]{1,0:T(8,128)(2,1)S(1)}, bf16[1456,128]{1,0:T(8,128)(2,1)S(1)}, u32[]{:S(2)}, u32[]{:S(2)}) collective-permute-start(bf16[1456,128]{1,0:T(8,128)(2,1)S(1)} %collective-permute-done.2), channel_id=1, source_target_pairs={{8,0},{16,24},{9,1},{17,25},{10,2},{18,26},{11,3},{19,27},{12,4},{... | collective-permute-start | bytes 1118216 | tf_op jit(solution)/shard_map/ppermute | solution.py:265
  35.2 11.1 %collective-permute-start.15 = (bf16[1456,128]{1,0:T(8,128)(2,1)}, bf16[1456,128]{1,0:T(8,128)(2,1)S(1)}, u32[]{:S(2)}, u32[]{:S(2)}) collective-permute-start(bf16[1456,128]{1,0:T(8,128)(2,1)} %broadcast_select_fusion.1.refs_4_), channel_id=1, source_target_pairs={{0,2},{1,5},{2,0},{3,7},{4,6},{5,1},{6,4},{7,3},{8,10},{9,13},{10,... | collective-permute-start | bytes 1118216 | tf_op jit(solution)/shard_map/ppermute | solution.py:257
  36.8 28.1 %copy-start.19 = (s32[128,4]{0,1:T(4,128)S(1)}, s32[128,4]{0,1:T(4,128)}, u32[]{:S(2)}) copy-start(s32[128,4]{0,1:T(4,128)} %param.6) | copy-start | bytes 6148
  37.5 18.0 %collective-permute-start.22 = (bf16[2880,128]{1,0:T(8,128)(2,1)S(1)}, bf16[2880,128]{1,0:T(8,128)(2,1)S(1)}, u32[]{:S(2)}, u32[]{:S(2)}) collective-permute-start(bf16[2880,128]{1,0:T(8,128)(2,1)S(1)} %shard_map.77), channel_id=1, source_target_pairs={{0,1},{1,0},{2,3},{3,2},{4,5},{5,4},{6,7},{7,6},{8,9},{9,8},{10,11... | collective-permute-start | bytes 2211848 | tf_op jit(solution)/shard_map/ppermute | solution.py:257
  39.1 0.8 copy-start.21
  39.9 0.7 copy-start.22
  40.6 24.4 %copy-start.12 = (bf16[1456,128]{1,0:T(8,128)(2,1)}, bf16[1456,128]{1,0:T(8,128)(2,1)S(1)}, u32[]{:S(2)}) copy-start(bf16[1456,128]{1,0:T(8,128)(2,1)S(1)} %collective-permute-done.9.refs_2_.refs_1_) | copy-start | bytes 1118212
  40.6 7.6 %collective-permute-start.10 = (bf16[1456,128]{1,0:T(8,128)(2,1)S(1)}, bf16[1456,128]{1,0:T(8,128)(2,1)S(1)}, u32[]{:S(2)}, u32[]{:S(2)}) collective-permute-start(bf16[1456,128]{1,0:T(8,128)(2,1)S(1)} %shard_map.70.refs_1_.refs_0_), channel_id=1, source_target_pairs={{0,4},{1,3},{2,6},{3,1},{4,0},{5,7},{6,2},{7,5},{8,12},{9,11},{10,... | collective-permute-start | bytes 1118216 | tf_op jit(solution)/shard_map/ppermute | solution.py:257
  42.1 13.4 %copy-start.8 = (bf16[1456,128]{1,0:T(8,128)(2,1)}, bf16[1456,128]{1,0:T(8,128)(2,1)S(1)}, u32[]{:S(2)}) copy-start(bf16[1456,128]{1,0:T(8,128)(2,1)S(1)} %collective-permute-done.13.refs_5_) | copy-start | bytes 1118212
  42.1 22.8 %collective-permute-start.11 = (bf16[1456,128]{1,0:T(8,128)(2,1)S(1)}, bf16[1456,128]{1,0:T(8,128)(2,1)}, u32[]{:S(2)}, u32[]{:S(2)}) collective-permute-start(bf16[1456,128]{1,0:T(8,128)(2,1)S(1)} %collective-permute-done.9.refs_2_.refs_1_), channel_id=1, source_target_pairs={{0,4},{1,3},{2,6},{3,1},{4,0},{5,7},{6,2},{7,5},{8,12},{9,11},{10,... | collective-permute-start | bytes 1118216 | tf_op jit(solution)/shard_map/ppermute | solution.py:257
  42.6 12.4 %collective-permute-start.5 = (bf16[360,512]{1,0:T(8,128)(2,1)S(1)}, bf16[360,512]{1,0:T(8,128)(2,1)S(1)}, u32[]{:S(2)}, u32[]{:S(2)}) collective-permute-start(bf16[360,512]{1,0:T(8,128)(2,1)S(1)} %get-tuple-element.25), channel_id=1, source_target_pairs={{0,24},{8,16},{16,8},{24,0},{1,25},{9,17},{17,9},{25,1},{2,26},{10... | collective-permute-start | bytes 1105928 | tf_op jit(solution)/shard_map/ppermute | solution.py:257
  46.3 18.7 %copy-start.10 = (bf16[1456,128]{1,0:T(8,128)(2,1)}, bf16[1456,128]{1,0:T(8,128)(2,1)S(1)}, u32[]{:S(2)}) copy-start(bf16[1456,128]{1,0:T(8,128)(2,1)S(1)} %collective-permute-done.15.refs_5_) | copy-start | bytes 1118212
  46.3 20.7 %collective-permute-start.16 = (bf16[1456,128]{1,0:T(8,128)(2,1)}, bf16[1456,128]{1,0:T(8,128)(2,1)}, u32[]{:S(2)}, u32[]{:S(2)}) collective-permute-start(bf16[1456,128]{1,0:T(8,128)(2,1)} %broadcast_select_fusion.1.refs_4_), channel_id=1, source_target_pairs={{0,4},{1,3},{2,6},{3,1},{4,0},{5,7},{6,2},{7,5},{8,12},{9,11},{10,... | collective-permute-start | bytes 1118216 | tf_op jit(solution)/shard_map/ppermute | solution.py:257
  48.2 0.7 copy-start.15
  48.9 19.7 %collective-permute-start.14 = (bf16[1456,128]{1,0:T(8,128)(2,1)}, bf16[1456,128]{1,0:T(8,128)(2,1)}, u32[]{:S(2)}, u32[]{:S(2)}) collective-permute-start(bf16[1456,128]{1,0:T(8,128)(2,1)} %collective-permute-done.12.refs_4_), channel_id=1, source_target_pairs={{0,4},{1,3},{2,6},{3,1},{4,0},{5,7},{6,2},{7,5},{8,12},{9,11},{10,... | collective-permute-start | bytes 1118216 | tf_op jit(solution)/shard_map/ppermute | solution.py:257
  55.0 14.1 %collective-permute-start.18 = (bf16[1456,128]{1,0:T(8,128)(2,1)S(1)}, bf16[1456,128]{1,0:T(8,128)(2,1)S(1)}, u32[]{:S(2)}, u32[]{:S(2)}) collective-permute-start(bf16[1456,128]{1,0:T(8,128)(2,1)S(1)} %broadcast_select_fusion.refs_3_), channel_id=1, source_target_pairs={{0,2},{1,5},{2,0},{3,7},{4,6},{5,1},{6,4},{7,3},{8,10},{9,13},{10,... | collective-permute-start | bytes 1118216 | tf_op jit(solution)/shard_map/ppermute | solution.py:257
  55.6 0.9 copy-start.4
  56.4 26.1 %collective-permute-start.8 = (bf16[360,512]{1,0:T(8,128)(2,1)}, bf16[360,512]{1,0:T(8,128)(2,1)}, u32[]{:S(2)}, u32[]{:S(2)}) collective-permute-start(bf16[360,512]{1,0:T(8,128)(2,1)} %get-tuple-element.28), channel_id=1, source_target_pairs={{0,8},{8,0},{16,24},{24,16},{1,9},{9,1},{17,25},{25,17},{2,10},{10... | collective-permute-start | bytes 1105928 | tf_op jit(solution)/shard_map/ppermute | solution.py:257
  65.0 21.1 %collective-permute-start.7 = (bf16[360,512]{1,0:T(8,128)(2,1)}, bf16[360,512]{1,0:T(8,128)(2,1)S(1)}, u32[]{:S(2)}, u32[]{:S(2)}) collective-permute-start(bf16[360,512]{1,0:T(8,128)(2,1)} %copy-done.21), channel_id=1, source_target_pairs={{0,16},{8,24},{16,0},{24,8},{1,17},{9,25},{17,1},{25,9},{2,18},{10... | collective-permute-start | bytes 1105928 | tf_op jit(solution)/shard_map/ppermute | solution.py:257
  67.0 20.7 %collective-permute-start.17 = (bf16[1456,128]{1,0:T(8,128)(2,1)}, bf16[1456,128]{1,0:T(8,128)(2,1)}, u32[]{:S(2)}, u32[]{:S(2)}) collective-permute-start(bf16[1456,128]{1,0:T(8,128)(2,1)} %copy-done.10), channel_id=1, source_target_pairs={{0,4},{1,3},{2,6},{3,1},{4,0},{5,7},{6,2},{7,5},{8,12},{9,11},{10,... | collective-permute-start | bytes 1118216 | tf_op jit(solution)/shard_map/ppermute | solution.py:257
  68.6 23.5 %collective-permute-start.19 = (bf16[1456,128]{1,0:T(8,128)(2,1)S(1)}, bf16[1456,128]{1,0:T(8,128)(2,1)}, u32[]{:S(2)}, u32[]{:S(2)}) collective-permute-start(bf16[1456,128]{1,0:T(8,128)(2,1)S(1)} %broadcast_select_fusion.refs_3_), channel_id=1, source_target_pairs={{0,4},{1,3},{2,6},{3,1},{4,0},{5,7},{6,2},{7,5},{8,12},{9,11},{10,... | collective-permute-start | bytes 1118216 | tf_op jit(solution)/shard_map/ppermute | solution.py:257
  69.1 23.0 %collective-permute-start.20 = (bf16[1456,128]{1,0:T(8,128)(2,1)S(1)}, bf16[1456,128]{1,0:T(8,128)(2,1)}, u32[]{:S(2)}, u32[]{:S(2)}) collective-permute-start(bf16[1456,128]{1,0:T(8,128)(2,1)S(1)} %collective-permute-done.18.refs_4_), channel_id=1, source_target_pairs={{0,4},{1,3},{2,6},{3,1},{4,0},{5,7},{6,2},{7,5},{8,12},{9,11},{10,... | collective-permute-start | bytes 1118216 | tf_op jit(solution)/shard_map/ppermute | solution.py:257
  70.8 1.1 %copy-start.5 = (bf16[2880,128]{1,0:T(8,128)(2,1)S(1)}, bf16[2880,128]{1,0:T(8,128)(2,1)}, u32[]{:S(2)}) copy-start(bf16[2880,128]{1,0:T(8,128)(2,1)} %copy-done.4) | copy-start | bytes 2211844
  71.9 1.0 copy-start.13
  72.9 1.0 copy-start.16
  73.9 2.1 %copy-start.14 = (bf16[1456,128]{1,0:T(8,128)(2,1)S(1)}, bf16[1456,128]{1,0:T(8,128)(2,1)}, u32[]{:S(2)}) copy-start(bf16[1456,128]{1,0:T(8,128)(2,1)} %copy-done.12) | copy-start | bytes 1118212
  73.9 2.1 %copy-start.23 = (bf16[360,512]{1,0:T(8,128)(2,1)S(1)}, bf16[360,512]{1,0:T(8,128)(2,1)}, u32[]{:S(2)}) copy-start(bf16[360,512]{1,0:T(8,128)(2,1)} %copy-done.22) | copy-start | bytes 1105924
  76.0 7.2 %copy-start.7 = (bf16[1456,128]{1,0:T(8,128)(2,1)S(1)}, bf16[1456,128]{1,0:T(8,128)(2,1)}, u32[]{:S(2)}) copy-start(bf16[1456,128]{1,0:T(8,128)(2,1)} %copy-done.6) | copy-start | bytes 1118212
  76.0 7.2 %copy-start.9 = (bf16[1456,128]{1,0:T(8,128)(2,1)S(1)}, bf16[1456,128]{1,0:T(8,128)(2,1)}, u32[]{:S(2)}) copy-start(bf16[1456,128]{1,0:T(8,128)(2,1)} %copy-done.8) | copy-start | bytes 1118212
  82.6 12.4 %collective-permute-start.25 = (f32[8,128]{1,0:T(8,128)S(1)}, f32[8,128]{1,0:T(8,128)S(1)}, u32[]{:S(2)}, u32[]{:S(2)}) collective-permute-start(f32[8,128]{1,0:T(8,128)S(1)} %shard_map.78), channel_id=1, source_target_pairs={{0,6},{1,7},{2,4},{3,5},{4,2},{5,3},{6,0},{7,1},{8,14},{9,15},{10,... | collective-permute-start | bytes 12296 | tf_op jit(solution)/shard_map/ppermute | solution.py:257
  83.1 6.0 %copy-start.11 = (bf16[1456,128]{1,0:T(8,128)(2,1)S(1)}, bf16[1456,128]{1,0:T(8,128)(2,1)}, u32[]{:S(2)}) copy-start(bf16[1456,128]{1,0:T(8,128)(2,1)} %copy-done.10) | copy-start | bytes 1118212
  86.1 8.8 %collective-permute-start.24 = (f32[8,128]{1,0:T(8,128)S(1)}, f32[8,128]{1,0:T(8,128)S(1)}, u32[]{:S(2)}, u32[]{:S(2)}) collective-permute-start(f32[8,128]{1,0:T(8,128)S(1)} %shard_map.78), channel_id=1, source_target_pairs={{0,4},{1,3},{2,6},{3,1},{4,0},{5,7},{6,2},{7,5},{8,12},{9,11},{10,... | collective-permute-start | bytes 12296 | tf_op jit(solution)/shard_map/ppermute | solution.py:257
  87.7 7.3 %collective-permute-start.23 = (f32[8,128]{1,0:T(8,128)S(1)}, f32[8,128]{1,0:T(8,128)S(1)}, u32[]{:S(2)}, u32[]{:S(2)}) collective-permute-start(f32[8,128]{1,0:T(8,128)S(1)} %shard_map.78), channel_id=1, source_target_pairs={{0,2},{1,5},{2,0},{3,7},{4,6},{5,1},{6,4},{7,3},{8,10},{9,13},{10,... | collective-permute-start | bytes 12296 | tf_op jit(solution)/shard_map/ppermute | solution.py:257
  92.1 2.8 %copy-start.1 = (f32[360,1440]{1,0:T(8,128)}, f32[360,1440]{1,0:T(8,128)S(1)}, u32[]{:S(2)}) copy-start(f32[360,1440]{1,0:T(8,128)S(1)} %get-tuple-element.36.refs_2_) | copy-start | bytes 6220804
  94.9 4.6 %collective-permute-start.21 = (bf16[360,1440]{1,0:T(8,128)(2,1)S(1)}, bf16[360,1440]{1,0:T(8,128)(2,1)}, u32[]{:S(2)}, u32[]{:S(2)}) collective-permute-start(bf16[360,1440]{1,0:T(8,128)(2,1)S(1)} %shard_map.75), channel_id=1, source_target_pairs={{0,1},{1,0},{2,3},{3,2},{4,5},{5,4},{6,7},{7,6},{8,9},{9,8},{10,11... | collective-permute-start | bytes 3110408 | tf_op jit(solution)/shard_map/ppermute | solution.py:257
  95.7 1.6 %copy-start.2 = (f32[360,1440]{1,0:T(8,128)S(1)}, f32[360,1440]{1,0:T(8,128)}, u32[]{:S(2)}) copy-start(f32[360,1440]{1,0:T(8,128)} %copy-done.1) | copy-start | bytes 6220804
  (2 other events, 1.4 us)

commit v3 on v2

--- a/solution.py
+++ b/solution.py
@@ -62,28 +62,50 @@
     return (down_grad, route_grad)
 
 
-def pack_kernel(grad_ref, ids_ref, gate_ref, out_ref):
-    width, tokens = grad_ref.shape
-    out_ref[:width, :] = grad_ref[...]
+def pack_kernel(grad_ref, ids_ref, gate_ref, out_ref, ids, gate, sems):
+    width, tokens = grad_ref.shape[2:]
+    copies = [
+        pltpu.make_async_copy(ids_ref.at[0, 0], ids, sems.at[0]),
+        pltpu.make_async_copy(gate_ref.at[0, 0], gate, sems.at[1]),
+        pltpu.make_async_copy(grad_ref.at[0, 0], out_ref.at[:width], sems.at[2]),
+    ]
+    for copy in copies:
+        copy.start()
+    copies[0].wait()
+    copies[1].wait()
     expert = lax.broadcasted_iota(jnp.int32, (META // 2, tokens), 0)
     dense = jnp.zeros((META // 2, tokens), jnp.float32)
-    for k in range(ids_ref.shape[0]):
-        dense = dense + jnp.where(expert == ids_ref[k:k + 1, :], gate_ref[k:k + 1, :], 0.0)
+    for k in range(ids.shape[0]):
+        dense = dense + jnp.where(expert == ids[k:k + 1, :], gate[k:k + 1, :], 0.0)
     high = dense.astype(jnp.bfloat16).astype(jnp.float32)
     out_ref[width:, :] = jnp.concatenate([high, dense - high], axis=0).astype(jnp.bfloat16)
-
-
-def rows_of_core(ref, core, cols):
-    return jnp.concatenate([ref[c, core, :, cols] for c in range(ref.shape[0])], axis=0)
-
-
-def turn_kernel(info_ref, hidden_ref, keep_ref, leave_ref):
+    copies[2].wait()
+
+
+def fetch(source, target, sems, cores):
+    copies = [
+        pltpu.make_async_copy(source.at[c, core], target.at[c, n], sems.at[c, n])
+        for c in range(source.shape[0])
+        for n, core in enumerate(cores)
+    ]
+    for copy in copies:
+        copy.start()
+    for copy in copies:
+        copy.wait()
+
+
+def stacked(ref, n, cols):
+    return jnp.concatenate([ref[c, n, :, cols] for c in range(ref.shape[0])], axis=0)
+
+
+def turn_kernel(info_ref, hidden_ref, keep_ref, leave_ref, here, sems):
     core = info_ref[0] & 1
-    width = hidden_ref.shape[3]
+    fetch(hidden_ref, here, sems, (core, 1 - core))
+    width = here.shape[3]
     for a in range(0, width, LANES):
         cols = slice(a, min(a + LANES, width))
-        keep_ref[cols, :] = rows_of_core(hidden_ref, core, cols).T
-        leave_ref[cols, :] = rows_of_core(hidden_ref, 1 - core, cols).T
+        keep_ref[cols, :] = stacked(here, 0, cols).T
+        leave_ref[cols, :] = stacked(here, 1, cols).T
 
 
 def quarter_kernel(info_ref, keep_ref, got_ref, *rest):
@@ -96,26 +118,49 @@
         outs[o][...] = scratch[info_ref[1] ^ o]
 
 
-def saved_kernel(info_ref, saved_ref, out_ref):
-    theirs = 1 - (info_ref[0] & 1)
-    rows, width = saved_ref.shape[0] * saved_ref.shape[2], saved_ref.shape[3]
+def saved_kernel(info_ref, saved_ref, out_ref, here, sems):
+    fetch(saved_ref, here, sems, (1 - (info_ref[0] & 1),))
+    rows, width = here.shape[0] * here.shape[2], here.shape[3]
     full, rest = width // LANES, width % LANES
     for j in range(full):
-        out_ref[j * rows:(j + 1) * rows, :] = rows_of_core(saved_ref, theirs, slice(j * LANES, (j + 1) * LANES))
-    tail = rows_of_core(saved_ref, theirs, slice(full * LANES, width)).astype(jnp.float32)
+        out_ref[j * rows:(j + 1) * rows, :] = stacked(here, 0, slice(j * LANES, (j + 1) * LANES))
+    tail = stacked(here, 0, slice(full * LANES, width)).astype(jnp.float32)
     step = rows * rest // LANES
     out_ref[full * rows:, :] = jnp.concatenate(
         [tail[a * step:(a + 1) * step] for a in range(LANES // rest)], axis=1
     ).astype(jnp.bfloat16)
 
 
-def block_tables(info_ref, blocks):
+def choose_kernel(info_ref, inner_ref, outer_ref, *refs):
+    out_ref = refs[-1]
+    rows = inner_ref.shape[0]
+    middle = jnp.logical_or(info_ref[1] == 1, info_ref[1] == 2)
+
+    @pl.when(middle)
+    def _():
+        out_ref[:rows, :] = inner_ref[...]
+
+    @pl.when(jnp.logical_not(middle))
+    def _():
+        out_ref[:rows, :] = outer_ref[...]
+
+    if len(refs) > 1:
+        score = refs[0][...]
+        high = score.astype(jnp.bfloat16).astype(jnp.float32)
+        out_ref[rows:, :] = jnp.concatenate([high, score - high], axis=0).astype(jnp.bfloat16)
+
+
+def join_kernel(a_ref, b_ref, out_ref):
+    out_ref[0] = a_ref[...]
+    out_ref[1] = b_ref[...]
+
+
+def block_tables(info_ref, blocks, width):
     me = info_ref[0]
     core, chip = me & 1, me >> 1
     offsets = [0, 1 + core, 2 - core, 3]
-    width = blocks[0].shape[0] - META
     rows = lax.broadcasted_iota(jnp.int32, (META, LANES), 0)
-    metas = [ref[width:, :].astype(jnp.float32) for ref in blocks]
+    metas = [ref[width:width + META, :].astype(jnp.float32) for ref in blocks]
     gates = []
     for expert in (me, me ^ 1):
         picked = jnp.logical_or(rows == expert, rows == expert + META // 2)
@@ -159,8 +204,7 @@
     return jnp.concatenate([ref[a:b, :] for ref in blocks], axis=1)
 
 
-def accumulate(hidden, blocks, acc_refs, out_refs):
-    width = blocks[0].shape[0] - META
+def accumulate(hidden, blocks, width, acc_refs, out_refs):
     rows = out_refs[0].shape[0]
     for a, b in chunks(width):
         total = lax.dot_general(
@@ -173,29 +217,32 @@
             out_ref[:, a:b] = value.astype(out_ref.dtype)
 
 
-def hidden_part(info_ref, hidden_refs, w):
-    half = hidden_refs[0].shape[1] // 2
-    picked = [ref[:, w * half:(w + 1) * half] for ref in hidden_refs]
-    if len(picked) == 1:
-        return picked[0]
-    return jnp.where(info_ref[2] != 0, picked[1], picked[0])
-
-
-def sum_kernel(hiddens, experts, started, info_ref, *refs):
-    hidden_refs, refs = refs[:hiddens], refs[hiddens:]
+def four(refs):
+    own, first, pair = refs
+    return [own, first, pair.at[0], pair.at[1]]
+
+
+def sum_kernel(choices, experts, started, info_ref, *refs):
+    hidden_refs, refs = refs[:choices], refs[choices:]
     number = len(experts)
     outs, refs = refs[-number:], refs[:-number]
-    accs, blocks = (refs[:number], list(refs[number:])) if started else ((), list(refs))
-    tables = block_tables(info_ref, blocks)
-    hidden = [gather_hidden(hidden_part(info_ref, hidden_refs, w), tables[w]) for w in experts]
-    accumulate(hidden[0] if number == 1 else jnp.concatenate(hidden, axis=0), blocks, accs, outs)
+    accs, refs = (refs[:number], refs[number:]) if started else ((), refs)
+    blocks, width = four(refs), outs[0].shape[1]
+    tables = block_tables(info_ref, blocks, width)
+    half = hidden_refs[0].shape[1] // 2
+    middle = jnp.logical_or(info_ref[1] == 1, info_ref[1] == 2)
+    hidden = []
+    for w in experts:
+        parts = [ref[:, w * half:(w + 1) * half] for ref in hidden_refs]
+        hidden.append(gather_hidden(parts[0] if choices == 1 else jnp.where(middle, *parts), tables[w]))
+    accumulate(hidden[0] if number == 1 else jnp.concatenate(hidden, axis=0), blocks, width, accs, outs)
 
 
 def score_kernel(info_ref, saved_ref, got_ref, *refs):
-    blocks, score_ref = list(refs[:-1]), refs[-1]
-    tables = block_tables(info_ref, blocks)
-    core = info_ref[0] & 1
-    rows, width = saved_ref.shape[0] * saved_ref.shape[2], saved_ref.shape[3]
+    blocks, (score_ref, here, sems) = four(refs[:-3]), refs[-3:]
+    fetch(saved_ref, here, sems, (info_ref[0] & 1,))
+    rows, width = here.shape[0] * here.shape[2], here.shape[3]
+    tables = block_tables(info_ref, blocks, width)
     full, rest = width // LANES, width % LANES
     total = jnp.zeros((2 * rows, len(blocks) * LANES), jnp.float32)
     for a, b in chunks(width):
@@ -209,7 +256,7 @@
                     jnp.concatenate([tail[:, n * rest:(n + 1) * rest] for n in range(LANES // rest)], axis=0)
                 )
         theirs = pieces[0] if len(pieces) == 1 else jnp.concatenate(pieces, axis=1)
-        saved = jnp.concatenate([rows_of_core(saved_ref, core, slice(a, b)), theirs], axis=0)
+        saved = jnp.concatenate([stacked(here, 0, slice(a, b)), theirs], axis=0)
         total = total + jnp.dot(saved, tokens_of(blocks, a, b), preferred_element_type=jnp.float32)
     scores = []
     for w in range(2):
@@ -220,26 +267,57 @@
     score_ref[...] = jnp.concatenate(scores, axis=0)
 
 
+def route_kernel(info_ref, ids_ref, score_ref, first_ref, pair_ref, out_ref, ids, sem):
+    copy = pltpu.make_async_copy(ids_ref.at[0, 0], ids, sem)
+    copy.start()
+    half = META // 2
+    parts = [score_ref[...]]
+    for ref in (first_ref, pair_ref.at[0], pair_ref.at[1]):
+        sent = ref[ref.shape[0] - META:, :].astype(jnp.float32)
+        parts.append(sent[:half] + sent[half:])
+    me = info_ref[0]
+    core = me & 1
+    offsets = [0, 2 + 2 * core, 4 - 2 * core, 6]
+    copy.wait()
+    wanted = ids[...] ^ me
+    total = jnp.zeros(wanted.shape, jnp.float32)
+    for w in range(2):
+        for n, part in enumerate(parts):
+            total = total + jnp.where(wanted == offsets[n] ^ w, part[4 * w + n:4 * w + n + 1], 0.0)
+    out_ref[...] = total
+
+
 def add_kernel(a_ref, b_ref, out_ref):
     out_ref[...] = (a_ref[...] + b_ref[...].astype(jnp.float32)).astype(out_ref.dtype)
 
 
-def call(kernel, outs, args, scratch=(), flops=0, limit=16):
-    smem, vmem = pl.BlockSpec(memory_space=pltpu.SMEM), pl.BlockSpec(memory_space=pltpu.VMEM)
-    moved = sum(a.size * a.dtype.itemsize for a in (*args, *outs))
+def call(kernel, outs, args, scratch=(), flops=0, limit=8, aliases=None):
+    smem, vmem, hbm = (pl.BlockSpec(memory_space=space) for space in (pltpu.SMEM, pltpu.VMEM, pltpu.HBM))
+    moved = sum(a.size * a.dtype.itemsize for a in args)
+    specs, operands = [], []
+    for a in args:
+        specs.append(smem if a.ndim == 1 else hbm if a.ndim == 4 else vmem)
+        if a.ndim > 1:
+            a = pltpu.with_memory_space_constraint(a, pltpu.HBM if a.ndim == 4 else pltpu.VMEM)
+        operands.append(a)
     return pl.pallas_call(
         kernel,
         out_shape=outs,
-        in_specs=[smem if a.ndim == 1 else vmem for a in args],
+        in_specs=specs,
         out_specs=[vmem] * len(outs),
         scratch_shapes=list(scratch),
+        input_output_aliases=aliases or {},
         compiler_params=pltpu.CompilerParams(vmem_limit_bytes=limit * 1024 * 1024),
-        cost_estimate=pl.CostEstimate(flops=flops, bytes_accessed=moved, transcendentals=0),
-    )(*args)
+        cost_estimate=pl.CostEstimate(flops=5 * flops, bytes_accessed=5 * moved, transcendentals=0),
+    )(*operands)
+
+
+def phase(*values):
+    return lax.optimization_barrier(values)
 
 
 def after(value, *earlier):
-    return lax.optimization_barrier((value, *earlier))[0]
+    return phase(value, *earlier)[0]
 
 
 def planes4(out_grad, expert_ids, gate_weight, saved_hidden, saved_output):
@@ -250,7 +328,6 @@
     planes = lax.axis_size("dp")
     rows = hidden_width // planes
     me, plane = lax.axis_index("expert"), lax.axis_index("dp")
-    middle = jnp.logical_or(plane == 1, plane == 2)
     bf16 = jnp.bfloat16
 
     def permute(name, target):
@@ -259,82 +336,109 @@
     core = permute("expert", lambda i: i ^ 1)
     first = permute("expert", lambda i: i ^ (4 if i & 1 else 2))
     second = permute("expert", lambda i: i ^ (2 if i & 1 else 4))
-    diagonal = permute("expert", lambda i: i ^ 6)
-    near_plane, far2, far3 = (permute("dp", lambda i, o=o: i ^ o) for o in (1, 2, 3))
+    far1, far2 = (permute("dp", lambda i, o=o: i ^ o) for o in (1, 2))
     inner = lambda x: lax.ppermute(x, "dp", [(1, 2), (2, 1)])
+    outer = lambda x: lax.ppermute(x, "dp", [(0, 3), (3, 0)])
     outward = lambda x: lax.ppermute(x, "dp", [(1, 0), (2, 3)])
-    info = jnp.stack([me, plane, middle.astype(jnp.int32)]).astype(jnp.int32)
-    info_flip = jnp.stack([me, plane, 1 - middle.astype(jnp.int32)]).astype(jnp.int32)
+    info = jnp.stack([me, plane]).astype(jnp.int32)
     hidden4 = saved_hidden.reshape(sources // 2, 2, capacity, hidden_width)
     saved4 = saved_output.reshape(sources // 2, 2, capacity, width)
 
     def shaped(*shape, dtype=bf16):
-        return jax.ShapeDtypeStruct(shape, dtype)
+        return pltpu.VMEM(shape, dtype)
+
+    def fetched(cores):
+        return [
+            pltpu.VMEM((sources // 2, cores, capacity, width), bf16),
+            pltpu.SemaphoreType.DMA((sources // 2, cores)),
+        ]
 
     acc = shaped(rows, width, dtype=jnp.float32)
     flops = 4 * rows * width * 4 * tokens
 
-    (own,) = call(pack_kernel, [shaped(width + META, tokens)], (out_grad.T, expert_ids.T, gate_weight.T))
-    near, across = near_plane(own), inner(own)
-    a0, b0 = first(own), second(own)
-    kept, leaving = call(turn_kernel, [shaped(hidden_width, slots // 2)] * 2, (info, hidden4))
-    hidden = call(
+    def add(hidden, blocks, totals=(), experts=(0, 1), out=acc):
+        return call(
+            functools.partial(sum_kernel, len(hidden), experts, bool(totals)), [out] * len(experts),
+            (info, *hidden, *totals, *blocks), flops=flops * len(experts) // 2,
+            aliases={1 + len(hidden) + n: n for n in range(len(totals))} if out is acc else None,
+        )
+
+    def choose(inner_block, outer_block, *score):
+        extra = META if score else 0
+        return call(
+            choose_kernel, [shaped(width + META + extra, tokens)], (info, inner_block, outer_block, *score)
+        )[0]
+
+    def join(a, b):
+        return call(join_kernel, [shaped(2, *a.shape)], (a, b))[0]
+
+    (own,) = call(
+        pack_kernel,
+        [shaped(width + META, tokens)],
+        tuple(x.T[None, None] for x in (out_grad, expert_ids, gate_weight)),
+        scratch=[
+            pltpu.VMEM(expert_ids.shape[::-1], jnp.int32),
+            pltpu.VMEM(gate_weight.shape[::-1], jnp.float32),
+            pltpu.SemaphoreType.DMA((3,)),
+        ],
+    )
+    kept, leaving = call(
+        turn_kernel, [shaped(hidden_width, slots // 2)] * 2, (info, hidden4), scratch=fetched(2)
+    )
+    own, leaving = phase(own, leaving)
+    near, across, f0, got = far1(own), inner(own), first(own), core(leaving)
+    h0, h1, h2, h3 = call(
         quarter_kernel,
         [shaped(rows, slots)] * planes,
-        (info, kept, core(leaving)),
+        (info, kept, got),
         scratch=[pltpu.VMEM((planes, rows, slots), bf16)],
     )
-    (saved_leaving,) = call(saved_kernel, [shaped(width * slots // 2 // LANES, LANES)], (info, saved4))
+    s0 = second(join(own, f0))
+
+    (saved_leaving,) = call(
+        saved_kernel, [shaped(width * slots // 2 // LANES, LANES)], (after(info, f0), saved4), scratch=fetched(1)
+    )
+    near, across, h0, saved_leaving = phase(near, across, h0, saved_leaving)
+    inside, outside, f1 = inner(near), outward(across), first(near)
     saved_got = core(saved_leaving)
-    second_in, second_out = inner(near), outward(across)
-    d0 = second(a0)
-    a1, b1 = first(near), second(near)
-    totals = call(
-        functools.partial(sum_kernel, 1, (0, 1), False), [acc, acc], (info, hidden[0], own, a0, b0, d0), flops=flops
-    )
+    near, s0 = phase(near, s0)
+    s1 = second(join(near, f1))
+
+    inside, outside, h3, saved_got = phase(inside, outside, h3, saved_got)
+    third, h3_inner = outward(inside), inner(h3)
+    block2 = choose(inside, outside)
+    f2 = first(after(block2, s0))
+    totals = add((h0,), (own, f0, s0))
     (score,) = call(
-        score_kernel, [shaped(8, LANES, dtype=jnp.float32)], (info, saved4, saved_got, own, a0, b0, d0),
-        flops=4 * slots * width * tokens,
-    )
-    third_out = outward(second_in)
-    h3 = far3(after(hidden[3], second_in, second_out))
-    block2 = jnp.where(middle, across, second_out)
-    d1 = second(a1)
-    a2, b2 = first(after(block2, a1)), second(after(block2, b1))
-    block3 = jnp.where(middle, second_in, third_out)
-    h2 = far2(after(hidden[2], h3, third_out))
-    h1 = near_plane(after(hidden[1], h3, third_out))
-    d2 = second(a2)
-    a3, b3 = first(after(block3, a2)), second(after(block3, b2))
-    d3 = second(a3)
-
-    ra, rb, rd = first(score), second(score), diagonal(score)
-
-    totals = call(
-        functools.partial(sum_kernel, 1, (0, 1), True), [acc, acc], (info, h1, *totals, near, a1, b1, d1), flops=flops
-    )
-    own_total, other_total = call(
-        functools.partial(sum_kernel, 2, (0, 1), True), [acc, acc],
-        (info, h2, h3, *totals, block2, a2, b2, d2), flops=flops,
-    )
-    (leaving_part,) = call(
-        functools.partial(sum_kernel, 2, (1,), True), [shaped(rows, width)],
-        (info_flip, h2, h3, other_total, block3, a3, b3, d3), flops=flops // 2,
-    )
+        score_kernel, [shaped(8, LANES, dtype=jnp.float32)], (info, saved4, saved_got, own, f0, s0),
+        scratch=fetched(1), flops=4 * slots * width * tokens,
+    )
+    s2 = second(join(block2, f2))
+
+    third, h3_inner, h1, h2, totals, score = phase(third, h3_inner, h1, h2, totals, score)
+    h1, h2 = far1(h1), far2(h2)
+    block3 = choose(across, third, score)
+    f3 = first(after(block3, s1))
+    s3 = second(join(block3, f3))
+
+    h1, h2, h3 = phase(h1, h2, h3)
+    h3_outer = outer(h3)
+    totals = add((h1,), (near, f1, s1), totals)
+    totals = add((h2,), (block2, f2, s2), totals)
+    blocks3 = (block3, f3, s3)
+    last = (h3_inner, h3_outer)
+    (leaving_part,) = add(last, blocks3, totals[1:], (1,), shaped(rows, width))
     got_part = core(leaving_part)
-    (own_total,) = call(
-        functools.partial(sum_kernel, 2, (0,), True), [acc],
-        (info_flip, h2, h3, own_total, block3, a3, b3, d3), flops=flops // 2,
-    )
-    (down_grad,) = call(add_kernel, [shaped(rows, width)], (own_total, got_part))
-
-    odd = me & 1
-    offsets = jnp.stack([0 * odd, 2 + 2 * odd, 4 - 2 * odd, 6 + 0 * odd])
-    offsets = jnp.concatenate([offsets, offsets ^ 1])
-    back = jnp.stack([r[4 * w + n] for w in range(2) for n, r in enumerate((score, ra, rb, rd))])
-    wanted = (expert_ids.T ^ me)[:, None, :] == offsets[None, :, None]
-    route_grad = jnp.sum(jnp.where(wanted, back[None], 0.0), axis=1).T
-    return (down_grad.reshape(1, rows, width), route_grad)
+    (own_total,) = add(last, blocks3, totals[:1], (0,))
+    (down_grad,) = call(add_kernel, [jax.ShapeDtypeStruct((rows, width), bf16)], (own_total, got_part))
+
+    (route_grad,) = call(
+        route_kernel,
+        [jax.ShapeDtypeStruct((expert_ids.shape[1], tokens), jnp.float32)],
+        (info, expert_ids.T[None, None], score, f3, s3),
+        scratch=[pltpu.VMEM(expert_ids.shape[::-1], jnp.int32), pltpu.SemaphoreType.DMA],
+    )
+    return (down_grad.reshape(1, rows, width), route_grad.T)
 
 
 def fits(mesh, out_grad, expert_ids, gate_weight, saved_hidden, saved_output):

time: 103 us -> 94.8 us (0.920)
  local copies, waits for them, and re-layouts: 11.9 us -> 0 us
  waiting for transfers between devices: 24.9 us -> 35.3 us
  starting transfers between devices: 40.3 us -> 34.2 us
  other arithmetic: 2.74 us -> 0.08 us
  Pallas kernels: 21.3 us -> 23.9 us
    unnamed x48 -> x0, local copies, waits for them, and re-layouts: 11.8 us -> none
    ppermute x22 -> x14, starting transfers between devices: 35.6 us -> 26.4 us  [permute(): lax.ppermute(x, name, [(i, target(i)) for i in range(lax.axis_size(name))])]
    ppermute x22 -> x14, waiting for transfers between devices: 18.8 us -> 27.6 us  [permute(): lax.ppermute(x, name, [(i, target(i)) for i in range(lax.axis_size(name))])]
    ppermute x0 -> x1, starting transfers between devices: none -> 3.24 us  [planes4(): outer = lambda x: lax.ppermute(x, 'dp', [(0, 3), (3, 0)])]
    pallas_call x11 -> x18, Pallas kernels: 21.3 us -> 23.9 us  [call(): pl.pallas_call(kernel, out_shape=outs, in_specs=specs, out_specs=[vmem] *...]
    select_n x2 -> x0, other arithmetic: 1.85 us -> none  [the longest x1 1.8 us: planes4(): block2 = jnp.where(middle, across, second_out)]
    ppermute x2, waiting for transfers between devices: 6.13 us -> 7.72 us  [planes4(): outward = lambda x: lax.ppermute(x, 'dp', [(1, 0), (2, 3)])]
    ppermute x2 -> x3, starting transfers between devices: 2.11 us -> 2.04 us  [planes4(): inner = lambda x: lax.ppermute(x, 'dp', [(1, 2), (2, 1)])]
  transfers between devices with their start and end apart: 26 -> 20, of which waited for: 6 -> 9; matrix products, arithmetic and copies ran while one was open for 3% -> 0% of each run, Pallas kernels for 18% -> 19%
where the time goes in v3:
time: 94.8 us; the launch traced here: 94.4 us
  waiting for transfers between devices  35.3 us (37%)
  starting transfers between devices  34.2 us (36%)
  Pallas kernels  23.9 us (25%)
    ppermute x14, waiting for transfers between devices, permute(): lax.ppermute(x, name, [(i, target(i)) for i in range(lax.axis_size(name))])  27.6 us
    ppermute x14, starting transfers between devices, permute(): lax.ppermute(x, name, [(i, target(i)) for i in range(lax.axis_size(name))])  26.4 us
    pallas_call x18, Pallas kernels, call(): pl.pallas_call(kernel, out_shape=outs, in_specs=specs, out_specs=[vmem] *...  23.9 us
    ppermute x2, waiting for transfers between devices, planes4(): outward = lambda x: lax.ppermute(x, 'dp', [(1, 0), (2, 3)])  7.72 us
    ppermute x1, starting transfers between devices, planes4(): outer = lambda x: lax.ppermute(x, 'dp', [(0, 3), (3, 0)])  3.24 us
    ppermute x2, starting transfers between devices, planes4(): outward = lambda x: lax.ppermute(x, 'dp', [(1, 0), (2, 3)])  2.56 us
    ppermute x3, starting transfers between devices, planes4(): inner = lambda x: lax.ppermute(x, 'dp', [(1, 2), (2, 1)])  2.04 us
  transfers between devices with their start and end apart: 20, of which 9 were waited for; matrix products, arithmetic and copies ran while one was open for 0% of the time, Pallas kernels for 19%

profile of v3, /device:TPU:0, one launch (start us, length us, event | category | flops | bytes accessed | tf_op | source)
XLA Modules:
  0.0 94.4 jit_solution(15757236426629493587)
XLA Ops:
  0.6 0.1 pad_add_fusion.info_ref
  0.7 2.5 %shard_map.69 = (bf16[1440,256]{1,0:T(8,128)(2,1)S(1)}, bf16[1440,256]{1,0:T(8,128)(2,1)S(1)}) custom-call(s32[2]{0:T(128)S(1)} %pad_add_fusion.info_ref, bf16[4,2,64,1440]{3,2,1,0:T(8,128)(2,1)} %bitcast.15), custom_call_target="tpu_custom_call" | custom-call | bytes 7372840 | tf_op jit(solution)/shard_map/pallas_call | solution.py:303
  3.2 1.0 %shard_map.68.a_ref.refs_1_.refs_0_ = bf16[1456,128]{1,0:T(8,128)(2,1)S(1)} custom-call(bf16[1,1,1440,128]{3,2,1,0:T(8,128)(2,1)} %bitcast.19, s32[1,1,4,128]{3,2,1,0:T(4,128)} %bitcast.20, f32[1,1,4,128]{3,2,1,0:T(4,128)} %bitcast.22), custom_call_target="tpu_custom_call" | custom-call | bytes 1863680 | tf_op jit(solution)/shard_map/pallas_call | solution.py:303
  4.3 0.5 collective-permute-start.2
  4.8 2.6 %collective-permute-start.3 = (bf16[1456,128]{1,0:T(8,128)(2,1)S(1)}, bf16[1456,128]{1,0:T(8,128)(2,1)S(1)}, u32[]{:S(2)}, u32[]{:S(2)}) collective-permute-start(bf16[1456,128]{1,0:T(8,128)(2,1)S(1)} %shard_map.68.a_ref.refs_1_.refs_0_), channel_id=1, source_target_pairs={{0,2},{1,5},{2,0},{3,7},{4,6},{5,1},{6,4},{7,3},{8,10},{9,13},{10,... | collective-permute-start | bytes 1118216 | tf_op jit(solution)/shard_map/ppermute | solution.py:334
  7.4 0.7 collective-permute-start.1
  8.1 4.4 %collective-permute-start = (bf16[1456,128]{1,0:T(8,128)(2,1)S(1)}, bf16[1456,128]{1,0:T(8,128)(2,1)S(1)}, u32[]{:S(2)}, u32[]{:S(2)}) collective-permute-start(bf16[1456,128]{1,0:T(8,128)(2,1)S(1)} %shard_map.68.a_ref.refs_1_.refs_0_), channel_id=1, source_target_pairs={{0,8},{8,0},{16,24},{24,16},{1,9},{9,1},{17,25},{25,17},{2,10},{10... | collective-permute-start | bytes 1118216 | tf_op jit(solution)/shard_map/ppermute | solution.py:334
  12.5 0.4 collective-permute-done.3.b_ref.refs_2_.refs_1_
  13.0 2.1 %collective-permute-start.9 = (bf16[2,1456,128]{2,1,0:T(8,128)(2,1)S(1)}, bf16[2,1456,128]{2,1,0:T(8,128)(2,1)S(1)}, u32[]{:S(2)}, u32[]{:S(2)}) collective-permute-start(bf16[2,1456,128]{2,1,0:T(8,128)(2,1)S(1)} %shard_map.72), channel_id=1, source_target_pairs={{0,4},{1,3},{2,6},{3,1},{4,0},{5,7},{6,2},{7,5},{8,12},{9,11},{10,... | collective-permute-start | bytes 2236424 | tf_op jit(solution)/shard_map/ppermute | solution.py:334
  15.1 2.0 %shard_map.71 = bf16[2880,128]{1,0:T(8,128)(2,1)S(1)} custom-call(s32[2]{0:T(128)S(1)} %pad_add_fusion.info_ref, bf16[4,2,64,1440]{3,2,1,0:T(8,128)(2,1)} %bitcast.16), custom_call_target="tpu_custom_call" | custom-call | bytes 7372840 | tf_op jit(solution)/shard_map/pallas_call | solution.py:303
  17.1 0.0 collective-permute-done.2.got_ref
  17.1 0.7 shard_map.70
  17.9 3.4 %collective-permute-done.a_ref.refs_3_ = bf16[1456,128]{1,0:T(8,128)(2,1)S(1)} collective-permute-done((bf16[1456,128]{1,0:T(8,128)(2,1)S(1)}, bf16[1456,128]{1,0:T(8,128)(2,1)S(1)}, u32[]{:S(2)}, u32[]{:S(2)}) %collective-permute-start) | collective-permute-done | bytes 372768 | tf_op jit(solution)/shard_map/ppermute | solution.py:334
  21.2 0.0 collective-permute-start.6
  21.2 1.4 %collective-permute-start.13 = (bf16[1456,128]{1,0:T(8,128)(2,1)S(1)}, bf16[1456,128]{1,0:T(8,128)(2,1)S(1)}, u32[]{:S(2)}, u32[]{:S(2)}) collective-permute-start(bf16[1456,128]{1,0:T(8,128)(2,1)S(1)} %collective-permute-done.a_ref.refs_3_), channel_id=1, source_target_pairs={{0,2},{1,5},{2,0},{3,7},{4,6},{5,1},{6,4},{7,3},{8,10},{9,13},{10,... | collective-permute-start | bytes 1118216 | tf_op jit(solution)/shard_map/ppermute | solution.py:334
  22.7 1.3 %collective-permute-start.5 = (bf16[1456,128]{1,0:T(8,128)(2,1)S(1)}, bf16[1456,128]{1,0:T(8,128)(2,1)S(1)}, u32[]{:S(2)}, u32[]{:S(2)}) collective-permute-start(bf16[1456,128]{1,0:T(8,128)(2,1)S(1)} %collective-permute-done.1.inner_ref), channel_id=1, source_target_pairs={{8,0},{16,24},{9,1},{17,25},{10,2},{18,26},{11,3},{19,27},{12,4},{... | collective-permute-start | bytes 1118216 | tf_op jit(solution)/shard_map/ppermute | solution.py:342
  24.0 0.7 collective-permute-start.4
  24.7 1.2 %collective-permute-done.9.refs_3_.refs_2_ = bf16[2,1456,128]{2,1,0:T(8,128)(2,1)S(1)} collective-permute-done((bf16[2,1456,128]{2,1,0:T(8,128)(2,1)S(1)}, bf16[2,1456,128]{2,1,0:T(8,128)(2,1)S(1)}, u32[]{:S(2)}, u32[]{:S(2)}) %collective-permute-start.9) | collective-permute-done | bytes 745504 | tf_op jit(solution)/shard_map/ppermute | solution.py:334
  25.9 2.9 %collective-permute-done.13.b_ref.refs_4_ = bf16[1456,128]{1,0:T(8,128)(2,1)S(1)} collective-permute-done((bf16[1456,128]{1,0:T(8,128)(2,1)S(1)}, bf16[1456,128]{1,0:T(8,128)(2,1)S(1)}, u32[]{:S(2)}, u32[]{:S(2)}) %collective-permute-start.13) | collective-permute-done | bytes 372768 | tf_op jit(solution)/shard_map/ppermute | solution.py:334
  28.8 0.6 collective-permute-start.14
  29.4 5.0 %collective-permute-done.5.outer_ref = bf16[1456,128]{1,0:T(8,128)(2,1)S(1)} collective-permute-done((bf16[1456,128]{1,0:T(8,128)(2,1)S(1)}, bf16[1456,128]{1,0:T(8,128)(2,1)S(1)}, u32[]{:S(2)}, u32[]{:S(2)}) %collective-permute-start.5) | collective-permute-done | bytes 372768 | tf_op jit(solution)/shard_map/ppermute | solution.py:342
  34.4 0.0 collective-permute-done.4.inner_ref
  34.4 0.0 collective-permute-done.6.got_ref
  34.4 1.3 %collective-permute-start.7 = (bf16[1456,128]{1,0:T(8,128)(2,1)S(1)}, bf16[1456,128]{1,0:T(8,128)(2,1)S(1)}, u32[]{:S(2)}, u32[]{:S(2)}) collective-permute-start(bf16[1456,128]{1,0:T(8,128)(2,1)S(1)} %collective-permute-done.4.inner_ref), channel_id=1, source_target_pairs={{8,0},{16,24},{9,1},{17,25},{10,2},{18,26},{11,3},{19,27},{12,4},{... | collective-permute-start | bytes 1118216 | tf_op jit(solution)/shard_map/ppermute | solution.py:342
  35.7 0.6 shard_map.77.a_ref.refs_3_
  36.3 0.7 collective-permute-start.8
  37.0 1.6 %collective-permute-start.15 = (bf16[1456,128]{1,0:T(8,128)(2,1)S(1)}, bf16[1456,128]{1,0:T(8,128)(2,1)S(1)}, u32[]{:S(2)}, u32[]{:S(2)}) collective-permute-start(bf16[1456,128]{1,0:T(8,128)(2,1)S(1)} %shard_map.77.a_ref.refs_3_), channel_id=1, source_target_pairs={{0,2},{1,5},{2,0},{3,7},{4,6},{5,1},{6,4},{7,3},{8,10},{9,13},{10,... | collective-permute-start | bytes 1118216 | tf_op jit(solution)/shard_map/ppermute | solution.py:334
  38.6 2.2 %shard_map.73 = (f32[360,1440]{1,0:T(8,128)S(1)}, f32[360,1440]{1,0:T(8,128)S(1)}) custom-call(s32[2]{0:T(128)S(1)} %pad_add_fusion.info_ref, bf16[360,512]{1,0:T(8,128)(2,1)S(1)} %get-tuple-element.53.refs_0_, bf16[1456,128]{1,0:T(8,128)(2,1)S(1)} %shard_map.68.a_ref.refs_1_.refs_0_, bf16[1456,128]{1,0:T(8,128)(2,1)S(1)} %collective-permute-done.3.b_ref.refs_2_.refs_1_, ...), custom_call_target="tpu_custom_call" | custom-call | flops 5308416000 | bytes 9297960 | tf_op jit(solution)/shard_map/pallas_call | solution.py:303
  40.8 2.8 %shard_map.74.refs_0_.score_ref = f32[8,128]{1,0:T(8,128)S(1)} custom-call(s32[2]{0:T(128)S(1)} %pad_add_fusion.info_ref, bf16[4,2,64,1440]{3,2,1,0:T(8,128)(2,1)} %bitcast.17, bf16[2880,128]{1,0:T(8,128)(2,1)S(1)} %collective-permute-done.6.got_ref, bf16[1456,128]{1,0:T(8,128)(2,1)S(1)} %shard_map.68.a_ref.refs_1_.refs_0_, ...), custom_call_target="tpu_custom_call" | custom-call | flops 1887436800 | bytes 18513960 | tf_op jit(solution)/shard_map/pallas_call | solution.py:303
  43.6 2.7 %collective-permute-done.7.outer_ref = bf16[1456,128]{1,0:T(8,128)(2,1)S(1)} collective-permute-done((bf16[1456,128]{1,0:T(8,128)(2,1)S(1)}, bf16[1456,128]{1,0:T(8,128)(2,1)S(1)}, u32[]{:S(2)}, u32[]{:S(2)}) %collective-permute-start.7) | collective-permute-done | bytes 372768 | tf_op jit(solution)/shard_map/ppermute | solution.py:342
  46.3 0.6 shard_map.80.a_ref.refs_3_
  46.9 0.0 collective-permute-done.14.refs_5_
  46.9 2.5 %collective-permute-start.17 = (bf16[1472,128]{1,0:T(8,128)(2,1)S(1)}, bf16[1472,128]{1,0:T(8,128)(2,1)S(1)}, u32[]{:S(2)}, u32[]{:S(2)}) collective-permute-start(bf16[1472,128]{1,0:T(8,128)(2,1)S(1)} %shard_map.80.a_ref.refs_3_), channel_id=1, source_target_pairs={{0,2},{1,5},{2,0},{3,7},{4,6},{5,1},{6,4},{7,3},{8,10},{9,13},{10,... | collective-permute-start | bytes 1130504 | tf_op jit(solution)/shard_map/ppermute | solution.py:334
  49.4 4.2 %collective-permute-start.10 = (bf16[360,512]{1,0:T(8,128)(2,1)S(1)}, bf16[360,512]{1,0:T(8,128)(2,1)S(1)}, u32[]{:S(2)}, u32[]{:S(2)}) collective-permute-start(bf16[360,512]{1,0:T(8,128)(2,1)S(1)} %get-tuple-element.59), channel_id=1, source_target_pairs={{0,8},{8,0},{16,24},{24,16},{1,9},{9,1},{17,25},{25,17},{2,10},{10... | collective-permute-start | bytes 1105928 | tf_op jit(solution)/shard_map/ppermute | solution.py:334
  53.7 2.0 %collective-permute-start.16 = (bf16[2,1456,128]{2,1,0:T(8,128)(2,1)S(1)}, bf16[2,1456,128]{2,1,0:T(8,128)(2,1)S(1)}, u32[]{:S(2)}, u32[]{:S(2)}) collective-permute-start(bf16[2,1456,128]{2,1,0:T(8,128)(2,1)S(1)} %shard_map.78), channel_id=1, source_target_pairs={{0,4},{1,3},{2,6},{3,1},{4,0},{5,7},{6,2},{7,5},{8,12},{9,11},{10,... | collective-permute-start | bytes 2236424 | tf_op jit(solution)/shard_map/ppermute | solution.py:334
  55.7 11.3 %collective-permute-done.10.refs_0_ = bf16[360,512]{1,0:T(8,128)(2,1)S(1)} collective-permute-done((bf16[360,512]{1,0:T(8,128)(2,1)S(1)}, bf16[360,512]{1,0:T(8,128)(2,1)S(1)}, u32[]{:S(2)}, u32[]{:S(2)}) %collective-permute-start.10) | collective-permute-done | bytes 368672 | tf_op jit(solution)/shard_map/ppermute | solution.py:334
  67.0 3.6 %collective-permute-done.11.refs_0_ = bf16[360,512]{1,0:T(8,128)(2,1)S(1)} collective-permute-done((bf16[360,512]{1,0:T(8,128)(2,1)S(1)}, bf16[360,512]{1,0:T(8,128)(2,1)S(1)}, u32[]{:S(2)}, u32[]{:S(2)}) %collective-permute-start.11) | collective-permute-done | bytes 368672 | tf_op jit(solution)/shard_map/ppermute | solution.py:334
  70.7 3.2 %collective-permute-start.12 = (bf16[360,512]{1,0:T(8,128)(2,1)S(1)}, bf16[360,512]{1,0:T(8,128)(2,1)S(1)}, u32[]{:S(2)}, u32[]{:S(2)}) collective-permute-start(bf16[360,512]{1,0:T(8,128)(2,1)S(1)} %get-tuple-element.61), channel_id=1, source_target_pairs={{0,24},{24,0},{1,25},{25,1},{2,26},{26,2},{3,27},{27,3},{4,28},{28... | collective-permute-start | bytes 1105928 | tf_op jit(solution)/shard_map/ppermute | solution.py:341
  73.9 0.1 shard_map.81
  74.0 4.4 %collective-permute-start.18 = (bf16[2,1472,128]{2,1,0:T(8,128)(2,1)S(1)}, bf16[2,1472,128]{2,1,0:T(8,128)(2,1)S(1)}, u32[]{:S(2)}, u32[]{:S(2)}) collective-permute-start(bf16[2,1472,128]{2,1,0:T(8,128)(2,1)S(1)} %shard_map.81), channel_id=1, source_target_pairs={{0,4},{1,3},{2,6},{3,1},{4,0},{5,7},{6,2},{7,5},{8,12},{9,11},{10,... | collective-permute-start | bytes 2261000 | tf_op jit(solution)/shard_map/ppermute | solution.py:334
  78.4 2.5 %shard_map.76 = (f32[360,1440]{1,0:T(8,128)S(1)}, f32[360,1440]{1,0:T(8,128)S(1)}) custom-call(s32[2]{0:T(128)S(1)} %pad_add_fusion.info_ref, bf16[360,512]{1,0:T(8,128)(2,1)S(1)} %collective-permute-done.10.refs_0_, f32[360,1440]{1,0:T(8,128)S(1)} %get-tuple-element.64.refs_1_, ...), custom_call_target="tpu_custom_call", output_to_operand_aliasing={{0}: (2, {}), {1}: (3, {})} | custom-call | flops 5308416000 | bytes 30033960 | tf_op jit(solution)/shard_map/pallas_call | solution.py:303
  80.9 2.5 %shard_map.79 = (f32[360,1440]{1,0:T(8,128)S(1)}, f32[360,1440]{1,0:T(8,128)S(1)}) custom-call(s32[2]{0:T(128)S(1)} %pad_add_fusion.info_ref, bf16[360,512]{1,0:T(8,128)(2,1)S(1)} %collective-permute-done.11.refs_0_, f32[360,1440]{1,0:T(8,128)S(1)} %get-tuple-element.67.refs_1_, ...), custom_call_target="tpu_custom_call", output_to_operand_aliasing={{0}: (2, {}), {1}: (3, {})} | custom-call | flops 5308416000 | bytes 30033960 | tf_op jit(solution)/shard_map/pallas_call | solution.py:303
  83.4 4.6 %collective-permute-done.18.refs_5_.pair_ref = bf16[2,1472,128]{2,1,0:T(8,128)(2,1)S(1)} collective-permute-done((bf16[2,1472,128]{2,1,0:T(8,128)(2,1)S(1)}, bf16[2,1472,128]{2,1,0:T(8,128)(2,1)S(1)}, u32[]{:S(2)}, u32[]{:S(2)}) %collective-permute-start.18) | collective-permute-done | bytes 753696 | tf_op jit(solution)/shard_map/ppermute | solution.py:334
  88.0 1.6 %shard_map.83 = bf16[360,1440]{1,0:T(8,128)(2,1)S(1)} custom-call(s32[2]{0:T(128)S(1)} %pad_add_fusion.info_ref, bf16[360,512]{1,0:T(8,128)(2,1)S(1)} %collective-permute-done.8.refs_0_, bf16[360,512]{1,0:T(8,128)(2,1)S(1)} %collective-permute-done.12.refs_1_, f32[360,1440]{1,0:T(8,128)S(1)} %get-tuple-element.75.refs_2_, ...), custom_call_target="tpu_custom_call" | custom-call | flops 2654208000 | bytes 21591080 | tf_op jit(solution)/shard_map/pallas_call | solution.py:303
  89.6 0.1 collective-permute-start.19
  89.7 1.8 %shard_map.85 = f32[4,128]{1,0:T(4,128)} custom-call(s32[2]{0:T(128)S(1)} %pad_add_fusion.info_ref, s32[1,1,4,128]{3,2,1,0:T(4,128)} %bitcast.21, f32[8,128]{1,0:T(8,128)S(1)} %shard_map.74.refs_0_.score_ref, bf16[1472,128]{1,0:T(8,128)(2,1)S(1)} %collective-permute-done.17.b_ref.refs_4_.first_ref, ...), custom_call_target="tpu_custom_call" | custom-call | bytes 5683240 | tf_op jit(solution)/shard_map/pallas_call | solution.py:303
  91.5 1.6 %shard_map.82.a_ref = f32[360,1440]{1,0:T(8,128)S(1)} custom-call(s32[2]{0:T(128)S(1)} %pad_add_fusion.info_ref, bf16[360,512]{1,0:T(8,128)(2,1)S(1)} %collective-permute-done.8.refs_0_, bf16[360,512]{1,0:T(8,128)(2,1)S(1)} %collective-permute-done.12.refs_1_, f32[360,1440]{1,0:T(8,128)S(1)} %get-tuple-element.71.refs_2_, ...), custom_call_target="tpu_custom_call", output_to_operand_aliasing={{}: (3, {})} | custom-call | flops 2654208000 | bytes 21591080 | tf_op jit(solution)/shard_map/pallas_call | solution.py:303
  93.1 1.3 %shard_map.84 = bf16[360,1440]{1,0:T(8,128)(2,1)} custom-call(f32[360,1440]{1,0:T(8,128)S(1)} %shard_map.82.a_ref, bf16[360,1440]{1,0:T(8,128)(2,1)S(1)} %collective-permute-done.19.b_ref), custom_call_target="tpu_custom_call" | custom-call | bytes 15552000 | tf_op jit(solution)/shard_map/pallas_call | solution.py:303
  (11 shorter events, 0.2 us)
Async XLA Ops:
  4.3 12.8 %collective-permute-start.2 = (bf16[1440,256]{1,0:T(8,128)(2,1)S(1)}, bf16[1440,256]{1,0:T(8,128)(2,1)S(1)}, u32[]{:S(2)}, u32[]{:S(2)}) collective-permute-start(bf16[1440,256]{1,0:T(8,128)(2,1)S(1)} %get-tuple-element.42), channel_id=1, source_target_pairs={{0,1},{1,0},{2,3},{3,2},{4,5},{5,4},{6,7},{7,6},{8,9},{9,8},{10,11... | collective-permute-start | bytes 2211848 | tf_op jit(solution)/shard_map/ppermute | solution.py:334
  4.8 8.1 %collective-permute-start.3 = (bf16[1456,128]{1,0:T(8,128)(2,1)S(1)}, bf16[1456,128]{1,0:T(8,128)(2,1)S(1)}, u32[]{:S(2)}, u32[]{:S(2)}) collective-permute-start(bf16[1456,128]{1,0:T(8,128)(2,1)S(1)} %shard_map.68.a_ref.refs_1_.refs_0_), channel_id=1, source_target_pairs={{0,2},{1,5},{2,0},{3,7},{4,6},{5,1},{6,4},{7,3},{8,10},{9,13},{10,... | collective-permute-start | bytes 1118216 | tf_op jit(solution)/shard_map/ppermute | solution.py:334
  7.4 10.5 %collective-permute-start.1 = (bf16[1456,128]{1,0:T(8,128)(2,1)S(1)}, bf16[1456,128]{1,0:T(8,128)(2,1)S(1)}, u32[]{:S(2)}, u32[]{:S(2)}) collective-permute-start(bf16[1456,128]{1,0:T(8,128)(2,1)S(1)} %shard_map.68.a_ref.refs_1_.refs_0_), channel_id=1, source_target_pairs={{8,16},{16,8},{9,17},{17,9},{10,18},{18,10},{11,19},{19,11},{12,20... | collective-permute-start | bytes 1118216 | tf_op jit(solution)/shard_map/ppermute | solution.py:340
  8.1 13.2 %collective-permute-start = (bf16[1456,128]{1,0:T(8,128)(2,1)S(1)}, bf16[1456,128]{1,0:T(8,128)(2,1)S(1)}, u32[]{:S(2)}, u32[]{:S(2)}) collective-permute-start(bf16[1456,128]{1,0:T(8,128)(2,1)S(1)} %shard_map.68.a_ref.refs_1_.refs_0_), channel_id=1, source_target_pairs={{0,8},{8,0},{16,24},{24,16},{1,9},{9,1},{17,25},{25,17},{2,10},{10... | collective-permute-start | bytes 1118216 | tf_op jit(solution)/shard_map/ppermute | solution.py:334
  13.0 12.9 %collective-permute-start.9 = (bf16[2,1456,128]{2,1,0:T(8,128)(2,1)S(1)}, bf16[2,1456,128]{2,1,0:T(8,128)(2,1)S(1)}, u32[]{:S(2)}, u32[]{:S(2)}) collective-permute-start(bf16[2,1456,128]{2,1,0:T(8,128)(2,1)S(1)} %shard_map.72), channel_id=1, source_target_pairs={{0,4},{1,3},{2,6},{3,1},{4,0},{5,7},{6,2},{7,5},{8,12},{9,11},{10,... | collective-permute-start | bytes 2236424 | tf_op jit(solution)/shard_map/ppermute | solution.py:334
  21.2 13.2 %collective-permute-start.6 = (bf16[2880,128]{1,0:T(8,128)(2,1)S(1)}, bf16[2880,128]{1,0:T(8,128)(2,1)S(1)}, u32[]{:S(2)}, u32[]{:S(2)}) collective-permute-start(bf16[2880,128]{1,0:T(8,128)(2,1)S(1)} %shard_map.71), channel_id=1, source_target_pairs={{0,1},{1,0},{2,3},{3,2},{4,5},{5,4},{6,7},{7,6},{8,9},{9,8},{10,11... | collective-permute-start | bytes 2211848 | tf_op jit(solution)/shard_map/ppermute | solution.py:334
  21.2 7.6 %collective-permute-start.13 = (bf16[1456,128]{1,0:T(8,128)(2,1)S(1)}, bf16[1456,128]{1,0:T(8,128)(2,1)S(1)}, u32[]{:S(2)}, u32[]{:S(2)}) collective-permute-start(bf16[1456,128]{1,0:T(8,128)(2,1)S(1)} %collective-permute-done.a_ref.refs_3_), channel_id=1, source_target_pairs={{0,2},{1,5},{2,0},{3,7},{4,6},{5,1},{6,4},{7,3},{8,10},{9,13},{10,... | collective-permute-start | bytes 1118216 | tf_op jit(solution)/shard_map/ppermute | solution.py:334
  22.7 11.8 %collective-permute-start.5 = (bf16[1456,128]{1,0:T(8,128)(2,1)S(1)}, bf16[1456,128]{1,0:T(8,128)(2,1)S(1)}, u32[]{:S(2)}, u32[]{:S(2)}) collective-permute-start(bf16[1456,128]{1,0:T(8,128)(2,1)S(1)} %collective-permute-done.1.inner_ref), channel_id=1, source_target_pairs={{8,0},{16,24},{9,1},{17,25},{10,2},{18,26},{11,3},{19,27},{12,4},{... | collective-permute-start | bytes 1118216 | tf_op jit(solution)/shard_map/ppermute | solution.py:342
  24.0 10.5 %collective-permute-start.4 = (bf16[1456,128]{1,0:T(8,128)(2,1)S(1)}, bf16[1456,128]{1,0:T(8,128)(2,1)S(1)}, u32[]{:S(2)}, u32[]{:S(2)}) collective-permute-start(bf16[1456,128]{1,0:T(8,128)(2,1)S(1)} %collective-permute-done.a_ref.refs_3_), channel_id=1, source_target_pairs={{8,16},{16,8},{9,17},{17,9},{10,18},{18,10},{11,19},{19,11},{12,20... | collective-permute-start | bytes 1118216 | tf_op jit(solution)/shard_map/ppermute | solution.py:340
  28.8 18.1 %collective-permute-start.14 = (bf16[2,1456,128]{2,1,0:T(8,128)(2,1)S(1)}, bf16[2,1456,128]{2,1,0:T(8,128)(2,1)S(1)}, u32[]{:S(2)}, u32[]{:S(2)}) collective-permute-start(bf16[2,1456,128]{2,1,0:T(8,128)(2,1)S(1)} %shard_map.75), channel_id=1, source_target_pairs={{0,4},{1,3},{2,6},{3,1},{4,0},{5,7},{6,2},{7,5},{8,12},{9,11},{10,... | collective-permute-start | bytes 2236424 | tf_op jit(solution)/shard_map/ppermute | solution.py:334
  34.4 11.9 %collective-permute-start.7 = (bf16[1456,128]{1,0:T(8,128)(2,1)S(1)}, bf16[1456,128]{1,0:T(8,128)(2,1)S(1)}, u32[]{:S(2)}, u32[]{:S(2)}) collective-permute-start(bf16[1456,128]{1,0:T(8,128)(2,1)S(1)} %collective-permute-done.4.inner_ref), channel_id=1, source_target_pairs={{8,0},{16,24},{9,1},{17,25},{10,2},{18,26},{11,3},{19,27},{12,4},{... | collective-permute-start | bytes 1118216 | tf_op jit(solution)/shard_map/ppermute | solution.py:342
  36.3 7.3 %collective-permute-start.8 = (bf16[360,512]{1,0:T(8,128)(2,1)S(1)}, bf16[360,512]{1,0:T(8,128)(2,1)S(1)}, u32[]{:S(2)}, u32[]{:S(2)}) collective-permute-start(bf16[360,512]{1,0:T(8,128)(2,1)S(1)} %get-tuple-element.61), channel_id=1, source_target_pairs={{8,16},{16,8},{9,17},{17,9},{10,18},{18,10},{11,19},{19,11},{12,20... | collective-permute-start | bytes 1105928 | tf_op jit(solution)/shard_map/ppermute | solution.py:340
  37.0 16.6 %collective-permute-start.15 = (bf16[1456,128]{1,0:T(8,128)(2,1)S(1)}, bf16[1456,128]{1,0:T(8,128)(2,1)S(1)}, u32[]{:S(2)}, u32[]{:S(2)}) collective-permute-start(bf16[1456,128]{1,0:T(8,128)(2,1)S(1)} %shard_map.77.a_ref.refs_3_), channel_id=1, source_target_pairs={{0,2},{1,5},{2,0},{3,7},{4,6},{5,1},{6,4},{7,3},{8,10},{9,13},{10,... | collective-permute-start | bytes 1118216 | tf_op jit(solution)/shard_map/ppermute | solution.py:334
  46.9 27.0 %collective-permute-start.17 = (bf16[1472,128]{1,0:T(8,128)(2,1)S(1)}, bf16[1472,128]{1,0:T(8,128)(2,1)S(1)}, u32[]{:S(2)}, u32[]{:S(2)}) collective-permute-start(bf16[1472,128]{1,0:T(8,128)(2,1)S(1)} %shard_map.80.a_ref.refs_3_), channel_id=1, source_target_pairs={{0,2},{1,5},{2,0},{3,7},{4,6},{5,1},{6,4},{7,3},{8,10},{9,13},{10,... | collective-permute-start | bytes 1130504 | tf_op jit(solution)/shard_map/ppermute | solution.py:334
  49.4 17.6 %collective-permute-start.10 = (bf16[360,512]{1,0:T(8,128)(2,1)S(1)}, bf16[360,512]{1,0:T(8,128)(2,1)S(1)}, u32[]{:S(2)}, u32[]{:S(2)}) collective-permute-start(bf16[360,512]{1,0:T(8,128)(2,1)S(1)} %get-tuple-element.59), channel_id=1, source_target_pairs={{0,8},{8,0},{16,24},{24,16},{1,9},{9,1},{17,25},{25,17},{2,10},{10... | collective-permute-start | bytes 1105928 | tf_op jit(solution)/shard_map/ppermute | solution.py:334
  53.6 17.1 %collective-permute-start.11 = (bf16[360,512]{1,0:T(8,128)(2,1)S(1)}, bf16[360,512]{1,0:T(8,128)(2,1)S(1)}, u32[]{:S(2)}, u32[]{:S(2)}) collective-permute-start(bf16[360,512]{1,0:T(8,128)(2,1)S(1)} %get-tuple-element.60), channel_id=1, source_target_pairs={{0,16},{8,24},{16,0},{24,8},{1,17},{9,25},{17,1},{25,9},{2,18},{10... | collective-permute-start | bytes 1105928 | tf_op jit(solution)/shard_map/ppermute | solution.py:334
  53.7 27.2 %collective-permute-start.16 = (bf16[2,1456,128]{2,1,0:T(8,128)(2,1)S(1)}, bf16[2,1456,128]{2,1,0:T(8,128)(2,1)S(1)}, u32[]{:S(2)}, u32[]{:S(2)}) collective-permute-start(bf16[2,1456,128]{2,1,0:T(8,128)(2,1)S(1)} %shard_map.78), channel_id=1, source_target_pairs={{0,4},{1,3},{2,6},{3,1},{4,0},{5,7},{6,2},{7,5},{8,12},{9,11},{10,... | collective-permute-start | bytes 2236424 | tf_op jit(solution)/shard_map/ppermute | solution.py:334
  70.7 12.7 %collective-permute-start.12 = (bf16[360,512]{1,0:T(8,128)(2,1)S(1)}, bf16[360,512]{1,0:T(8,128)(2,1)S(1)}, u32[]{:S(2)}, u32[]{:S(2)}) collective-permute-start(bf16[360,512]{1,0:T(8,128)(2,1)S(1)} %get-tuple-element.61), channel_id=1, source_target_pairs={{0,24},{24,0},{1,25},{25,1},{2,26},{26,2},{3,27},{27,3},{4,28},{28... | collective-permute-start | bytes 1105928 | tf_op jit(solution)/shard_map/ppermute | solution.py:341
  74.0 14.0 %collective-permute-start.18 = (bf16[2,1472,128]{2,1,0:T(8,128)(2,1)S(1)}, bf16[2,1472,128]{2,1,0:T(8,128)(2,1)S(1)}, u32[]{:S(2)}, u32[]{:S(2)}) collective-permute-start(bf16[2,1472,128]{2,1,0:T(8,128)(2,1)S(1)} %shard_map.81), channel_id=1, source_target_pairs={{0,4},{1,3},{2,6},{3,1},{4,0},{5,7},{6,2},{7,5},{8,12},{9,11},{10,... | collective-permute-start | bytes 2261000 | tf_op jit(solution)/shard_map/ppermute | solution.py:334
  89.6 3.5 %collective-permute-start.19 = (bf16[360,1440]{1,0:T(8,128)(2,1)S(1)}, bf16[360,1440]{1,0:T(8,128)(2,1)S(1)}, u32[]{:S(2)}, u32[]{:S(2)}) collective-permute-start(bf16[360,1440]{1,0:T(8,128)(2,1)S(1)} %shard_map.83), channel_id=1, source_target_pairs={{0,1},{1,0},{2,3},{3,2},{4,5},{5,4},{6,7},{7,6},{8,9},{9,8},{10,11... | collective-permute-start | bytes 3110408 | tf_op jit(solution)/shard_map/ppermute | solution.py:334

commit v4 on v3

--- a/solution.py
+++ b/solution.py
@@ -9,6 +9,25 @@
 
 LANES = 128
 META = 16
+AFTER = {
+    "saved": ("f0",),
+    "inside": ("quarters", "saved",),
+    "outside": ("near", "saved",),
+    "f1": ("across", "saved",),
+    "j1": ("s0",),
+    "third": ("outside", "saved_swapped",),
+    "h3_inner": ("inside", "outside", "saved_swapped", "across",),
+    "f2": ("s0",),
+    "h1": ("third",),
+    "h2": ("h3_inner",),
+    "f3": ("s1",),
+    "h3_outer": ("h1", "h2",),
+    "j3": ("h1",),
+    "turned": ("own",),
+}
+SCALE, SCALES = 3, {"t2": 0.5, "turned": 2, "t0": 0.5}
+TOTALS = ("t0", "t1", "t2")
+H3 = ("h3_inner", "h3_outer")
 
 
 def slot_numbers(ids, experts, capacity):
@@ -98,8 +117,8 @@
     return jnp.concatenate([ref[c, n, :, cols] for c in range(ref.shape[0])], axis=0)
 
 
-def turn_kernel(info_ref, hidden_ref, keep_ref, leave_ref, here, sems):
-    core = info_ref[0] & 1
+def turn_kernel(hidden_ref, keep_ref, leave_ref, here, sems):
+    core = lax.axis_index("expert") & 1
     fetch(hidden_ref, here, sems, (core, 1 - core))
     width = here.shape[3]
     for a in range(0, width, LANES):
@@ -108,18 +127,18 @@
         leave_ref[cols, :] = stacked(here, 1, cols).T
 
 
-def quarter_kernel(info_ref, keep_ref, got_ref, *rest):
+def quarter_kernel(keep_ref, got_ref, *rest):
     outs, scratch = rest[:-1], rest[-1]
     planes, rows, half = len(outs), outs[0].shape[0], keep_ref.shape[1]
     for q in range(planes):
         scratch[q, :, :half] = keep_ref[q * rows:(q + 1) * rows, :]
         scratch[q, :, half:] = got_ref[q * rows:(q + 1) * rows, :]
     for o in range(planes):
-        outs[o][...] = scratch[info_ref[1] ^ o]
-
-
-def saved_kernel(info_ref, saved_ref, out_ref, here, sems):
-    fetch(saved_ref, here, sems, (1 - (info_ref[0] & 1),))
+        outs[o][...] = scratch[lax.axis_index("dp") ^ o]
+
+
+def saved_kernel(saved_ref, out_ref, here, sems):
+    fetch(saved_ref, here, sems, (1 - (lax.axis_index("expert") & 1),))
     rows, width = here.shape[0] * here.shape[2], here.shape[3]
     full, rest = width // LANES, width % LANES
     for j in range(full):
@@ -131,10 +150,11 @@
     ).astype(jnp.bfloat16)
 
 
-def choose_kernel(info_ref, inner_ref, outer_ref, *refs):
+def choose_kernel(inner_ref, outer_ref, *refs):
     out_ref = refs[-1]
     rows = inner_ref.shape[0]
-    middle = jnp.logical_or(info_ref[1] == 1, info_ref[1] == 2)
+    plane = lax.axis_index("dp")
+    middle = jnp.logical_or(plane == 1, plane == 2)
 
     @pl.when(middle)
     def _():
@@ -155,8 +175,8 @@
     out_ref[1] = b_ref[...]
 
 
-def block_tables(info_ref, blocks, width):
-    me = info_ref[0]
+def block_tables(blocks, width):
+    me = lax.axis_index("expert")
     core, chip = me & 1, me >> 1
     offsets = [0, 1 + core, 2 - core, 3]
     rows = lax.broadcasted_iota(jnp.int32, (META, LANES), 0)
@@ -204,45 +224,47 @@
     return jnp.concatenate([ref[a:b, :] for ref in blocks], axis=1)
 
 
-def accumulate(hidden, blocks, width, acc_refs, out_refs):
-    rows = out_refs[0].shape[0]
-    for a, b in chunks(width):
-        total = lax.dot_general(
-            hidden, tokens_of(blocks, a, b), (((1,), (1,)), ((), ())), preferred_element_type=jnp.float32
-        )
-        for w, out_ref in enumerate(out_refs):
-            value = total[w * rows:(w + 1) * rows]
-            if acc_refs:
-                value = value + acc_refs[w][:, a:b]
-            out_ref[:, a:b] = value.astype(out_ref.dtype)
-
-
 def four(refs):
     own, first, pair = refs
     return [own, first, pair.at[0], pair.at[1]]
 
 
-def sum_kernel(choices, experts, started, info_ref, *refs):
-    hidden_refs, refs = refs[:choices], refs[choices:]
+def sum_kernel(choices, experts, started, *refs):
     number = len(experts)
     outs, refs = refs[-number:], refs[:-number]
     accs, refs = (refs[:number], refs[number:]) if started else ((), refs)
-    blocks, width = four(refs), outs[0].shape[1]
-    tables = block_tables(info_ref, blocks, width)
-    half = hidden_refs[0].shape[1] // 2
-    middle = jnp.logical_or(info_ref[1] == 1, info_ref[1] == 2)
-    hidden = []
-    for w in experts:
-        parts = [ref[:, w * half:(w + 1) * half] for ref in hidden_refs]
-        hidden.append(gather_hidden(parts[0] if choices == 1 else jnp.where(middle, *parts), tables[w]))
-    accumulate(hidden[0] if number == 1 else jnp.concatenate(hidden, axis=0), blocks, width, accs, outs)
-
-
-def score_kernel(info_ref, saved_ref, got_ref, *refs):
+    rows, width = outs[0].shape
+    plane = lax.axis_index("dp")
+    middle = jnp.logical_or(plane == 1, plane == 2)
+    replicas = []
+    for many in choices:
+        hidden_refs, blocks, refs = refs[:many], four(refs[many:many + 3]), refs[many + 3:]
+        tables = block_tables(blocks, width)
+        half = hidden_refs[0].shape[1] // 2
+        hidden = []
+        for w in experts:
+            parts = [ref[:, w * half:(w + 1) * half] for ref in hidden_refs]
+            hidden.append(gather_hidden(parts[0] if many == 1 else jnp.where(middle, *parts), tables[w]))
+        replicas.append((hidden[0] if number == 1 else jnp.concatenate(hidden, axis=0), blocks))
+    for a, b in chunks(width):
+        total = None
+        for hidden, blocks in replicas:
+            product = lax.dot_general(
+                hidden, tokens_of(blocks, a, b), (((1,), (1,)), ((), ())), preferred_element_type=jnp.float32
+            )
+            total = product if total is None else total + product
+        for w, out_ref in enumerate(outs):
+            value = total[w * rows:(w + 1) * rows]
+            if started:
+                value = value + accs[w][:, a:b]
+            out_ref[:, a:b] = value.astype(out_ref.dtype)
+
+
+def score_kernel(saved_ref, got_ref, *refs):
     blocks, (score_ref, here, sems) = four(refs[:-3]), refs[-3:]
-    fetch(saved_ref, here, sems, (info_ref[0] & 1,))
+    fetch(saved_ref, here, sems, (lax.axis_index("expert") & 1,))
     rows, width = here.shape[0] * here.shape[2], here.shape[3]
-    tables = block_tables(info_ref, blocks, width)
+    tables = block_tables(blocks, width)
     full, rest = width // LANES, width % LANES
     total = jnp.zeros((2 * rows, len(blocks) * LANES), jnp.float32)
     for a, b in chunks(width):
@@ -267,7 +289,7 @@
     score_ref[...] = jnp.concatenate(scores, axis=0)
 
 
-def route_kernel(info_ref, ids_ref, score_ref, first_ref, pair_ref, out_ref, ids, sem):
+def route_kernel(ids_ref, score_ref, first_ref, pair_ref, out_ref, ids, sem):
     copy = pltpu.make_async_copy(ids_ref.at[0, 0], ids, sem)
     copy.start()
     half = META // 2
@@ -275,7 +297,7 @@
     for ref in (first_ref, pair_ref.at[0], pair_ref.at[1]):
         sent = ref[ref.shape[0] - META:, :].astype(jnp.float32)
         parts.append(sent[:half] + sent[half:])
-    me = info_ref[0]
+    me = lax.axis_index("expert")
     core = me & 1
     offsets = [0, 2 + 2 * core, 4 - 2 * core, 6]
     copy.wait()
@@ -291,12 +313,13 @@
     out_ref[...] = (a_ref[...] + b_ref[...].astype(jnp.float32)).astype(out_ref.dtype)
 
 
-def call(kernel, outs, args, scratch=(), flops=0, limit=8, aliases=None):
+def call(kernel, outs, args, scratch=(), flops=0, limit=8, aliases=None, name=None):
     smem, vmem, hbm = (pl.BlockSpec(memory_space=space) for space in (pltpu.SMEM, pltpu.VMEM, pltpu.HBM))
     moved = sum(a.size * a.dtype.itemsize for a in args)
+    scale = SCALES.get(name, SCALE)
     specs, operands = [], []
     for a in args:
-        specs.append(smem if a.ndim == 1 else hbm if a.ndim == 4 else vmem)
+        specs.append(hbm if a.ndim == 4 else vmem)
         if a.ndim > 1:
             a = pltpu.with_memory_space_constraint(a, pltpu.HBM if a.ndim == 4 else pltpu.VMEM)
         operands.append(a)
@@ -308,7 +331,7 @@
         scratch_shapes=list(scratch),
         input_output_aliases=aliases or {},
         compiler_params=pltpu.CompilerParams(vmem_limit_bytes=limit * 1024 * 1024),
-        cost_estimate=pl.CostEstimate(flops=5 * flops, bytes_accessed=5 * moved, transcendentals=0),
+        cost_estimate=pl.CostEstimate(flops=int(scale * flops), bytes_accessed=int(scale * moved), transcendentals=0),
     )(*operands)
 
 
@@ -327,7 +350,6 @@
     slots = sources * capacity
     planes = lax.axis_size("dp")
     rows = hidden_width // planes
-    me, plane = lax.axis_index("expert"), lax.axis_index("dp")
     bf16 = jnp.bfloat16
 
     def permute(name, target):
@@ -336,11 +358,10 @@
     core = permute("expert", lambda i: i ^ 1)
     first = permute("expert", lambda i: i ^ (4 if i & 1 else 2))
     second = permute("expert", lambda i: i ^ (2 if i & 1 else 4))
-    far1, far2 = (permute("dp", lambda i, o=o: i ^ o) for o in (1, 2))
+    far1, far2, far3 = (permute("dp", lambda i, o=o: i ^ o) for o in (1, 2, 3))
     inner = lambda x: lax.ppermute(x, "dp", [(1, 2), (2, 1)])
     outer = lambda x: lax.ppermute(x, "dp", [(0, 3), (3, 0)])
     outward = lambda x: lax.ppermute(x, "dp", [(1, 0), (2, 3)])
-    info = jnp.stack([me, plane]).astype(jnp.int32)
     hidden4 = saved_hidden.reshape(sources // 2, 2, capacity, hidden_width)
     saved4 = saved_output.reshape(sources // 2, 2, capacity, width)
 
@@ -356,89 +377,153 @@
     acc = shaped(rows, width, dtype=jnp.float32)
     flops = 4 * rows * width * 4 * tokens
 
-    def add(hidden, blocks, totals=(), experts=(0, 1), out=acc):
+    def add(replicas, totals=(), experts=(0, 1), out=acc, name=None):
+        arrays = [x for hidden, blocks in replicas for x in (*hidden, *blocks)]
         return call(
-            functools.partial(sum_kernel, len(hidden), experts, bool(totals)), [out] * len(experts),
-            (info, *hidden, *totals, *blocks), flops=flops * len(experts) // 2,
-            aliases={1 + len(hidden) + n: n for n in range(len(totals))} if out is acc else None,
+            functools.partial(sum_kernel, [len(hidden) for hidden, blocks in replicas], experts, bool(totals)),
+            [out] * len(experts),
+            (*totals, *arrays), flops=flops * len(replicas) * len(experts) // 2, name=name,
+            aliases={n: n for n in range(len(totals))} if out is acc else None,
         )
 
     def choose(inner_block, outer_block, *score):
         extra = META if score else 0
         return call(
-            choose_kernel, [shaped(width + META + extra, tokens)], (info, inner_block, outer_block, *score)
+            choose_kernel, [shaped(width + META + extra, tokens)], (inner_block, outer_block, *score)
         )[0]
 
     def join(a, b):
         return call(join_kernel, [shaped(2, *a.shape)], (a, b))[0]
 
-    (own,) = call(
-        pack_kernel,
-        [shaped(width + META, tokens)],
-        tuple(x.T[None, None] for x in (out_grad, expert_ids, gate_weight)),
-        scratch=[
-            pltpu.VMEM(expert_ids.shape[::-1], jnp.int32),
-            pltpu.VMEM(gate_weight.shape[::-1], jnp.float32),
-            pltpu.SemaphoreType.DMA((3,)),
-        ],
-    )
-    kept, leaving = call(
-        turn_kernel, [shaped(hidden_width, slots // 2)] * 2, (info, hidden4), scratch=fetched(2)
-    )
-    own, leaving = phase(own, leaving)
-    near, across, f0, got = far1(own), inner(own), first(own), core(leaving)
-    h0, h1, h2, h3 = call(
-        quarter_kernel,
-        [shaped(rows, slots)] * planes,
-        (info, kept, got),
-        scratch=[pltpu.VMEM((planes, rows, slots), bf16)],
-    )
-    s0 = second(join(own, f0))
-
-    (saved_leaving,) = call(
-        saved_kernel, [shaped(width * slots // 2 // LANES, LANES)], (after(info, f0), saved4), scratch=fetched(1)
-    )
-    near, across, h0, saved_leaving = phase(near, across, h0, saved_leaving)
-    inside, outside, f1 = inner(near), outward(across), first(near)
-    saved_got = core(saved_leaving)
-    near, s0 = phase(near, s0)
-    s1 = second(join(near, f1))
-
-    inside, outside, h3, saved_got = phase(inside, outside, h3, saved_got)
-    third, h3_inner = outward(inside), inner(h3)
-    block2 = choose(inside, outside)
-    f2 = first(after(block2, s0))
-    totals = add((h0,), (own, f0, s0))
-    (score,) = call(
-        score_kernel, [shaped(8, LANES, dtype=jnp.float32)], (info, saved4, saved_got, own, f0, s0),
-        scratch=fetched(1), flops=4 * slots * width * tokens,
-    )
-    s2 = second(join(block2, f2))
-
-    third, h3_inner, h1, h2, totals, score = phase(third, h3_inner, h1, h2, totals, score)
-    h1, h2 = far1(h1), far2(h2)
-    block3 = choose(across, third, score)
-    f3 = first(after(block3, s1))
-    s3 = second(join(block3, f3))
-
-    h1, h2, h3 = phase(h1, h2, h3)
-    h3_outer = outer(h3)
-    totals = add((h1,), (near, f1, s1), totals)
-    totals = add((h2,), (block2, f2, s2), totals)
-    blocks3 = (block3, f3, s3)
-    last = (h3_inner, h3_outer)
-    (leaving_part,) = add(last, blocks3, totals[1:], (1,), shaped(rows, width))
-    got_part = core(leaving_part)
-    (own_total,) = add(last, blocks3, totals[:1], (0,))
-    (down_grad,) = call(add_kernel, [jax.ShapeDtypeStruct((rows, width), bf16)], (own_total, got_part))
-
-    (route_grad,) = call(
-        route_kernel,
-        [jax.ShapeDtypeStruct((expert_ids.shape[1], tokens), jnp.float32)],
-        (info, expert_ids.T[None, None], score, f3, s3),
-        scratch=[pltpu.VMEM(expert_ids.shape[::-1], jnp.int32), pltpu.SemaphoreType.DMA],
-    )
-    return (down_grad.reshape(1, rows, width), route_grad.T)
+    steps = {
+        "hidden": (lambda: hidden4,),
+        "outputs": (lambda: saved4,),
+        "own": (
+            lambda: call(
+                pack_kernel,
+                [shaped(width + META, tokens)],
+                tuple(x.T[None, None] for x in (out_grad, expert_ids, gate_weight)),
+                scratch=[
+                    pltpu.VMEM(expert_ids.shape[::-1], jnp.int32),
+                    pltpu.VMEM(gate_weight.shape[::-1], jnp.float32),
+                    pltpu.SemaphoreType.DMA((3,)),
+                ],
+                name="own",
+            )[0],
+        ),
+        "turned": (
+            lambda x: call(
+                turn_kernel, [shaped(hidden_width, slots // 2)] * 2, (x,), scratch=fetched(2), name="turned"
+            ),
+            "hidden",
+        ),
+        "swapped": (lambda t: core(t[1]), "turned"),
+        "quarters": (
+            lambda t, got: call(
+                quarter_kernel,
+                [shaped(rows, slots)] * planes,
+                (t[0], got),
+                scratch=[pltpu.VMEM((planes, rows, slots), bf16)],
+                name="quarters",
+            ),
+            "turned", "swapped",
+        ),
+        "h1": (lambda h: far1(h[1]), "quarters"),
+        "h2": (lambda h: far2(h[2]), "quarters"),
+        "h3": (lambda h: far3(h[3]), "quarters"),
+        "h3_inner": (lambda h: inner(h[3]), "quarters"),
+        "h3_outer": (lambda h: outer(h[3]), "quarters"),
+        "near": (far1, "own"),
+        "across": (inner, "own"),
+        "inside": (inner, "near"),
+        "outside": (outward, "across"),
+        "third": (outward, "inside"),
+        "block2": (choose, "inside", "outside"),
+        "block3": (choose, "across", "third", "score"),
+        "f0": (first, "own"),
+        "j0": (join, "own", "f0"),
+        "s0": (second, "j0"),
+        "f1": (first, "near"),
+        "j1": (join, "near", "f1"),
+        "s1": (second, "j1"),
+        "f2": (first, "block2"),
+        "j2": (join, "block2", "f2"),
+        "s2": (second, "j2"),
+        "f3": (first, "block3"),
+        "j3": (join, "block3", "f3"),
+        "s3": (second, "j3"),
+        "saved": (
+            lambda x: call(
+                saved_kernel, [shaped(width * slots // 2 // LANES, LANES)], (x,), scratch=fetched(1), name="saved"
+            )[0],
+            "outputs",
+        ),
+        "saved_swapped": (core, "saved"),
+        "score": (
+            lambda got, *blocks: call(
+                score_kernel, [shaped(8, LANES, dtype=jnp.float32)], (saved4, got, *blocks),
+                scratch=fetched(1), flops=4 * slots * width * tokens, name="score",
+            )[0],
+            "saved_swapped", "own", "f0", "s0",
+        ),
+        "part_swapped": (core, "part"),
+        "down": (
+            lambda a, b: call(add_kernel, [jax.ShapeDtypeStruct((rows, width), bf16)], (a, b), name="down")[0],
+            "mine", "part_swapped",
+        ),
+        "route": (
+            lambda *scores: call(
+                route_kernel,
+                [jax.ShapeDtypeStruct((expert_ids.shape[1], tokens), jnp.float32)],
+                (expert_ids.T[None, None], *scores),
+                scratch=[pltpu.VMEM(expert_ids.shape[::-1], jnp.int32), pltpu.SemaphoreType.DMA],
+                name="route",
+            )[0],
+            "score", "f3", "s3",
+        ),
+    }
+    sums = {
+        "t0": ("quarters", "own", "f0", "s0"),
+        "t1": ("h1", "near", "f1", "s1"),
+        "t2": ("h2", "block2", "f2", "s2"),
+        "t3": (*H3, "block3", "f3", "s3"),
+    }
+
+    def split(names, values):
+        replicas = []
+        for n in names:
+            many = len(sums[n]) - 3
+            hidden = (values[0][0],) if n == "t0" else values[:many]
+            replicas.append((hidden, values[many:many + 3]))
+            values = values[many + 3:]
+        return replicas
+
+    before = None
+    for n in TOTALS:
+        build = lambda *values, n=n, started=before is not None: add(
+            split([n], values[1:] if started else values), values[0] if started else (), name=n
+        )
+        steps[n] = (build, *([before] if before else []), *sums[n])
+        before = n
+    late = [n for n in sums if n not in TOTALS]
+    for n, experts, out in (("part", (1,), shaped(rows, width)), ("mine", (0,), acc)):
+        build = lambda t, *values, n=n, experts=experts, out=out: add(
+            split(late, values), [t[w] for w in experts], experts, out, name=n
+        )[0]
+        steps[n] = (build, before, *(x for m in late for x in sums[m]))
+    made = {}
+
+    def get(name):
+        if name not in made:
+            build, *needs = steps[name]
+            values = [get(other) for other in needs]
+            earlier = [get(other) for other in AFTER.get(name, ())]
+            if earlier:
+                values = phase(*values, *earlier)[:len(values)]
+            made[name] = build(*values)
+        return made[name]
+
+    return (get("down").reshape(1, rows, width), get("route").T)
 
 
 def fits(mesh, out_grad, expert_ids, gate_weight, saved_hidden, saved_output):

time: 94.8 us -> 81.4 us (0.86)
  Pallas kernels: 23.9 us -> 17.4 us
  starting transfers between devices: 34.2 us -> 28.5 us
    ppermute x14, waiting for transfers between devices: 27.6 us -> 20 us  [permute(): lax.ppermute(x, name, [(i, target(i)) for i in range(lax.axis_size(name))])]
    ppermute x14, starting transfers between devices: 26.4 us -> 19.8 us  [permute(): lax.ppermute(x, name, [(i, target(i)) for i in range(lax.axis_size(name))])]
    pallas_call x18, Pallas kernels: 23.9 us -> 17.4 us  [call(): pl.pallas_call(kernel, out_shape=outs, in_specs=specs, out_specs=[vmem] *...]
    ppermute x2, waiting for transfers between devices: 7.72 us -> 12.9 us  [planes4(): outward = lambda x: lax.ppermute(x, 'dp', [(1, 0), (2, 3)])]
    ppermute x1, waiting for transfers between devices: 0.01 us -> 1.53 us  [planes4(): outer = lambda x: lax.ppermute(x, 'dp', [(0, 3), (3, 0)])]
  transfers between devices with their start and end apart: 20 -> 20, of which waited for: 9 -> 9; matrix products, arithmetic and copies ran while one was open for 0% -> 0% of each run, Pallas kernels for 19% -> 17%
where the time goes in v4:
time: 81.4 us; the launch traced here: 81.1 us
  waiting for transfers between devices  34.4 us (42%)
  starting transfers between devices  28.5 us (35%)
  Pallas kernels  17.4 us (21%)
  between operations  0.85 us (1%)
    ppermute x14, waiting for transfers between devices, permute(): lax.ppermute(x, name, [(i, target(i)) for i in range(lax.axis_size(name))])  20 us
    ppermute x14, starting transfers between devices, permute(): lax.ppermute(x, name, [(i, target(i)) for i in range(lax.axis_size(name))])  19.8 us
    pallas_call x18, Pallas kernels, call(): pl.pallas_call(kernel, out_shape=outs, in_specs=specs, out_specs=[vmem] *...  17.4 us
    ppermute x2, waiting for transfers between devices, planes4(): outward = lambda x: lax.ppermute(x, 'dp', [(1, 0), (2, 3)])  12.9 us
    ppermute x1, starting transfers between devices, planes4(): outer = lambda x: lax.ppermute(x, 'dp', [(0, 3), (3, 0)])  4.06 us
    ppermute x2, starting transfers between devices, planes4(): outward = lambda x: lax.ppermute(x, 'dp', [(1, 0), (2, 3)])  2.56 us
    ppermute x3, starting transfers between devices, planes4(): inner = lambda x: lax.ppermute(x, 'dp', [(1, 2), (2, 1)])  2.04 us
  transfers between devices with their start and end apart: 20, of which 9 were waited for; matrix products, arithmetic and copies ran while one was open for 0% of the time, Pallas kernels for 17%

profile of v4, /device:TPU:0, one launch (start us, length us, event | category | flops | bytes accessed | tf_op | source)
XLA Modules:
  0.0 81.1 jit_solution(15916167896173747047)
XLA Ops:
  0.6 1.0 %shard_map.68.a_ref.refs_1_.refs_0_ = bf16[1456,128]{1,0:T(8,128)(2,1)S(1)} custom-call(bf16[1,1,1440,128]{3,2,1,0:T(8,128)(2,1)} %bitcast.17, s32[1,1,4,128]{3,2,1,0:T(4,128)} %bitcast.18, f32[1,1,4,128]{3,2,1,0:T(4,128)} %bitcast.20), custom_call_target="tpu_custom_call" | custom-call | bytes 1118208 | tf_op jit(solution)/shard_map/pallas_call | solution.py:326
  1.7 3.0 %collective-permute-start.1 = (bf16[1456,128]{1,0:T(8,128)(2,1)S(1)}, bf16[1456,128]{1,0:T(8,128)(2,1)S(1)}, u32[]{:S(2)}, u32[]{:S(2)}) collective-permute-start(bf16[1456,128]{1,0:T(8,128)(2,1)S(1)} %shard_map.68.a_ref.refs_1_.refs_0_), channel_id=1, source_target_pairs={{0,2},{1,5},{2,0},{3,7},{4,6},{5,1},{6,4},{7,3},{8,10},{9,13},{10,... | collective-permute-start | bytes 1118216 | tf_op jit(solution)/shard_map/ppermute | solution.py:356
  4.7 0.7 collective-permute-start.5
  5.4 4.4 %collective-permute-start.3 = (bf16[1456,128]{1,0:T(8,128)(2,1)S(1)}, bf16[1456,128]{1,0:T(8,128)(2,1)S(1)}, u32[]{:S(2)}, u32[]{:S(2)}) collective-permute-start(bf16[1456,128]{1,0:T(8,128)(2,1)S(1)} %shard_map.68.a_ref.refs_1_.refs_0_), channel_id=1, source_target_pairs={{0,8},{8,0},{16,24},{24,16},{1,9},{9,1},{17,25},{25,17},{2,10},{10... | collective-permute-start | bytes 1118216 | tf_op jit(solution)/shard_map/ppermute | solution.py:356
  9.8 0.4 collective-permute-done.1.b_ref.refs_2_.refs_1_
  10.3 2.1 %collective-permute-start.2 = (bf16[2,1456,128]{2,1,0:T(8,128)(2,1)S(1)}, bf16[2,1456,128]{2,1,0:T(8,128)(2,1)S(1)}, u32[]{:S(2)}, u32[]{:S(2)}) collective-permute-start(bf16[2,1456,128]{2,1,0:T(8,128)(2,1)S(1)} %shard_map.71), channel_id=1, source_target_pairs={{0,4},{1,3},{2,6},{3,1},{4,0},{5,7},{6,2},{7,5},{8,12},{9,11},{10,... | collective-permute-start | bytes 2236424 | tf_op jit(solution)/shard_map/ppermute | solution.py:356
  12.4 2.0 %shard_map.69 = (bf16[1440,256]{1,0:T(8,128)(2,1)S(1)}, bf16[1440,256]{1,0:T(8,128)(2,1)S(1)}) custom-call(bf16[4,2,64,1440]{3,2,1,0:T(8,128)(2,1)} %bitcast.13), custom_call_target="tpu_custom_call" | custom-call | bytes 2949120 | tf_op jit(solution)/shard_map/pallas_call | solution.py:326
  14.4 0.1 collective-permute-start
  14.4 1.5 %shard_map.73 = bf16[2880,128]{1,0:T(8,128)(2,1)S(1)} custom-call(bf16[4,2,64,1440]{3,2,1,0:T(8,128)(2,1)} %bitcast.14), custom_call_target="tpu_custom_call" | custom-call | bytes 4423680 | tf_op jit(solution)/shard_map/pallas_call | solution.py:326
  15.9 0.0 collective-permute-done.5.inner_ref
  15.9 2.0 %collective-permute-done.3.a_ref.refs_3_ = bf16[1456,128]{1,0:T(8,128)(2,1)S(1)} collective-permute-done((bf16[1456,128]{1,0:T(8,128)(2,1)S(1)}, bf16[1456,128]{1,0:T(8,128)(2,1)S(1)}, u32[]{:S(2)}, u32[]{:S(2)}) %collective-permute-start.3) | collective-permute-done | bytes 372768 | tf_op jit(solution)/shard_map/ppermute | solution.py:356
  18.0 1.5 %collective-permute-start.10 = (bf16[1456,128]{1,0:T(8,128)(2,1)S(1)}, bf16[1456,128]{1,0:T(8,128)(2,1)S(1)}, u32[]{:S(2)}, u32[]{:S(2)}) collective-permute-start(bf16[1456,128]{1,0:T(8,128)(2,1)S(1)} %collective-permute-done.3.a_ref.refs_3_), channel_id=1, source_target_pairs={{0,2},{1,5},{2,0},{3,7},{4,6},{5,1},{6,4},{7,3},{8,10},{9,13},{10,... | collective-permute-start | bytes 1118216 | tf_op jit(solution)/shard_map/ppermute | solution.py:356
  19.4 0.0 collective-permute-start.7
  19.5 1.3 %collective-permute-start.6 = (bf16[1456,128]{1,0:T(8,128)(2,1)S(1)}, bf16[1456,128]{1,0:T(8,128)(2,1)S(1)}, u32[]{:S(2)}, u32[]{:S(2)}) collective-permute-start(bf16[1456,128]{1,0:T(8,128)(2,1)S(1)} %collective-permute-done.5.inner_ref), channel_id=1, source_target_pairs={{8,0},{16,24},{9,1},{17,25},{10,2},{18,26},{11,3},{19,27},{12,4},{... | collective-permute-start | bytes 1118216 | tf_op jit(solution)/shard_map/ppermute | solution.py:364
  20.7 0.0 collective-permute-done.got_ref
  20.7 0.2 shard_map.70
  21.0 0.7 collective-permute-start.4
  21.6 3.9 %collective-permute-done.10.b_ref.refs_4_ = bf16[1456,128]{1,0:T(8,128)(2,1)S(1)} collective-permute-done((bf16[1456,128]{1,0:T(8,128)(2,1)S(1)}, bf16[1456,128]{1,0:T(8,128)(2,1)S(1)}, u32[]{:S(2)}, u32[]{:S(2)}) %collective-permute-start.10) | collective-permute-done | bytes 372768 | tf_op jit(solution)/shard_map/ppermute | solution.py:356
  25.5 0.0 collective-permute-done.2.refs_3_.refs_2_
  25.6 2.5 %collective-permute-start.11 = (bf16[2,1456,128]{2,1,0:T(8,128)(2,1)S(1)}, bf16[2,1456,128]{2,1,0:T(8,128)(2,1)S(1)}, u32[]{:S(2)}, u32[]{:S(2)}) collective-permute-start(bf16[2,1456,128]{2,1,0:T(8,128)(2,1)S(1)} %shard_map.74), channel_id=1, source_target_pairs={{0,4},{1,3},{2,6},{3,1},{4,0},{5,7},{6,2},{7,5},{8,12},{9,11},{10,... | collective-permute-start | bytes 2236424 | tf_op jit(solution)/shard_map/ppermute | solution.py:356
  28.1 4.4 %collective-permute-done.6.outer_ref = bf16[1456,128]{1,0:T(8,128)(2,1)S(1)} collective-permute-done((bf16[1456,128]{1,0:T(8,128)(2,1)S(1)}, bf16[1456,128]{1,0:T(8,128)(2,1)S(1)}, u32[]{:S(2)}, u32[]{:S(2)}) %collective-permute-start.6) | collective-permute-done | bytes 372768 | tf_op jit(solution)/shard_map/ppermute | solution.py:364
  32.4 0.0 collective-permute-done.7.got_ref
  32.4 0.0 collective-permute-done.4.inner_ref
  32.4 1.3 %collective-permute-start.8 = (bf16[1456,128]{1,0:T(8,128)(2,1)S(1)}, bf16[1456,128]{1,0:T(8,128)(2,1)S(1)}, u32[]{:S(2)}, u32[]{:S(2)}) collective-permute-start(bf16[1456,128]{1,0:T(8,128)(2,1)S(1)} %collective-permute-done.4.inner_ref), channel_id=1, source_target_pairs={{8,0},{16,24},{9,1},{17,25},{10,2},{18,26},{11,3},{19,27},{12,4},{... | collective-permute-start | bytes 1118216 | tf_op jit(solution)/shard_map/ppermute | solution.py:364
  33.7 0.7 collective-permute-start.12
  34.5 0.6 collective-permute-start.14
  35.1 2.2 %shard_map.79.refs_0_.score_ref = f32[8,128]{1,0:T(8,128)S(1)} custom-call(bf16[4,2,64,1440]{3,2,1,0:T(8,128)(2,1)} %bitcast.15, bf16[2880,128]{1,0:T(8,128)(2,1)S(1)} %collective-permute-done.7.got_ref, bf16[1456,128]{1,0:T(8,128)(2,1)S(1)} %shard_map.68.a_ref.refs_1_.refs_0_, bf16[1456,128]{1,0:T(8,128)(2,1)S(1)} %collective-permute-done.1.b_ref.refs_2_.refs_1_, ...), custom_call_target="tpu_custom_call" | custom-call | flops 1132462080 | bytes 11108352 | tf_op jit(solution)/shard_map/pallas_call | solution.py:326
  37.3 8.5 %collective-permute-done.8.outer_ref = bf16[1456,128]{1,0:T(8,128)(2,1)S(1)} collective-permute-done((bf16[1456,128]{1,0:T(8,128)(2,1)S(1)}, bf16[1456,128]{1,0:T(8,128)(2,1)S(1)}, u32[]{:S(2)}, u32[]{:S(2)}) %collective-permute-start.8) | collective-permute-done | bytes 372768 | tf_op jit(solution)/shard_map/ppermute | solution.py:364
  45.9 0.0 collective-permute-done.11.refs_5_
  45.9 0.6 collective-permute-start.17
  46.5 0.1 collective-permute-start.15
  46.7 2.9 %collective-permute-start.13 = (bf16[360,512]{1,0:T(8,128)(2,1)S(1)}, bf16[360,512]{1,0:T(8,128)(2,1)S(1)}, u32[]{:S(2)}, u32[]{:S(2)}) collective-permute-start(bf16[360,512]{1,0:T(8,128)(2,1)S(1)} %get-tuple-element.50), channel_id=1, source_target_pairs={{0,16},{8,24},{16,0},{24,8},{1,17},{9,25},{17,1},{25,9},{2,18},{10... | collective-permute-start | bytes 1105928 | tf_op jit(solution)/shard_map/ppermute | solution.py:356
  49.6 12.2 %collective-permute-done.9.refs_2_ = bf16[360,512]{1,0:T(8,128)(2,1)S(1)} collective-permute-done((bf16[360,512]{1,0:T(8,128)(2,1)S(1)}, bf16[360,512]{1,0:T(8,128)(2,1)S(1)}, u32[]{:S(2)}, u32[]{:S(2)}) %collective-permute-start.9) | collective-permute-done | bytes 368672 | tf_op jit(solution)/shard_map/ppermute | solution.py:356
  61.8 0.0 collective-permute-done.17.b_ref.refs_4_.first_ref
  61.8 1.8 %collective-permute-start.18 = (bf16[2,1472,128]{2,1,0:T(8,128)(2,1)S(1)}, bf16[2,1472,128]{2,1,0:T(8,128)(2,1)S(1)}, u32[]{:S(2)}, u32[]{:S(2)}) collective-permute-start(bf16[2,1472,128]{2,1,0:T(8,128)(2,1)S(1)} %shard_map.81), channel_id=1, source_target_pairs={{0,4},{1,3},{2,6},{3,1},{4,0},{5,7},{6,2},{7,5},{8,12},{9,11},{10,... | collective-permute-start | bytes 2261000 | tf_op jit(solution)/shard_map/ppermute | solution.py:356
  63.7 1.1 %collective-permute-done.13.refs_2_ = bf16[360,512]{1,0:T(8,128)(2,1)S(1)} collective-permute-done((bf16[360,512]{1,0:T(8,128)(2,1)S(1)}, bf16[360,512]{1,0:T(8,128)(2,1)S(1)}, u32[]{:S(2)}, u32[]{:S(2)}) %collective-permute-start.13) | collective-permute-done | bytes 368672 | tf_op jit(solution)/shard_map/ppermute | solution.py:356
  64.8 4.1 %collective-permute-start.16 = (bf16[360,512]{1,0:T(8,128)(2,1)S(1)}, bf16[360,512]{1,0:T(8,128)(2,1)S(1)}, u32[]{:S(2)}, u32[]{:S(2)}) collective-permute-start(bf16[360,512]{1,0:T(8,128)(2,1)S(1)} %get-tuple-element.53), channel_id=1, source_target_pairs={{0,24},{24,0},{1,25},{25,1},{2,26},{26,2},{3,27},{27,3},{4,28},{28... | collective-permute-start | bytes 1105928 | tf_op jit(solution)/shard_map/ppermute | solution.py:363
  68.9 1.7 %shard_map.72 = (f32[360,1440]{1,0:T(8,128)S(1)}, f32[360,1440]{1,0:T(8,128)S(1)}) custom-call(bf16[360,512]{1,0:T(8,128)(2,1)S(1)} %get-tuple-element.33.refs_0_, bf16[1456,128]{1,0:T(8,128)(2,1)S(1)} %shard_map.68.a_ref.refs_1_.refs_0_, bf16[1456,128]{1,0:T(8,128)(2,1)S(1)} %collective-permute-done.1.b_ref.refs_2_.refs_1_, ...), custom_call_target="tpu_custom_call" | custom-call | flops 530841600 | bytes 929792 | tf_op jit(solution)/shard_map/pallas_call | solution.py:326
  70.6 1.9 %shard_map.75 = (f32[360,1440]{1,0:T(8,128)S(1)}, f32[360,1440]{1,0:T(8,128)S(1)}) custom-call(f32[360,1440]{1,0:T(8,128)S(1)} %get-tuple-element.34.refs_0_, f32[360,1440]{1,0:T(8,128)S(1)} %get-tuple-element.35.refs_1_, bf16[360,512]{1,0:T(8,128)(2,1)S(1)} %collective-permute-done.9.refs_2_, ...), custom_call_target="tpu_custom_call", output_to_operand_aliasing={{0}: (0, {}), {1}: (1, {})} | custom-call | flops 3185049600 | bytes 18020352 | tf_op jit(solution)/shard_map/pallas_call | solution.py:326
  72.5 1.9 %shard_map.78 = (f32[360,1440]{1,0:T(8,128)S(1)}, f32[360,1440]{1,0:T(8,128)S(1)}) custom-call(f32[360,1440]{1,0:T(8,128)S(1)} %get-tuple-element.47.refs_0_, f32[360,1440]{1,0:T(8,128)S(1)} %get-tuple-element.48.refs_1_, bf16[360,512]{1,0:T(8,128)(2,1)S(1)} %collective-permute-done.13.refs_2_, ...), custom_call_target="tpu_custom_call", output_to_operand_aliasing={{0}: (0, {}), {1}: (1, {})} | custom-call | flops 530841600 | bytes 3003392 | tf_op jit(solution)/shard_map/pallas_call | solution.py:326
  74.5 1.5 %collective-permute-done.16.refs_2_ = bf16[360,512]{1,0:T(8,128)(2,1)S(1)} collective-permute-done((bf16[360,512]{1,0:T(8,128)(2,1)S(1)}, bf16[360,512]{1,0:T(8,128)(2,1)S(1)}, u32[]{:S(2)}, u32[]{:S(2)}) %collective-permute-start.16) | collective-permute-done | bytes 368672 | tf_op jit(solution)/shard_map/ppermute | solution.py:363
  76.0 0.0 collective-permute-done.18.refs_5_.pair_ref
  76.0 1.0 %shard_map.83 = bf16[360,1440]{1,0:T(8,128)(2,1)S(1)} custom-call(f32[360,1440]{1,0:T(8,128)S(1)} %get-tuple-element.57.refs_0_, bf16[360,512]{1,0:T(8,128)(2,1)S(1)} %collective-permute-done.12.refs_1_, bf16[360,512]{1,0:T(8,128)(2,1)S(1)} %collective-permute-done.16.refs_2_, bf16[1472,128]{1,0:T(8,128)(2,1)S(1)} %shard_map.80.a_ref.refs_3_, ...), custom_call_target="tpu_custom_call" | custom-call | flops 1592524800 | bytes 12954624 | tf_op jit(solution)/shard_map/pallas_call | solution.py:326
  77.0 0.1 collective-permute-start.19
  77.1 1.3 %shard_map.85 = f32[4,128]{1,0:T(4,128)} custom-call(s32[1,1,4,128]{3,2,1,0:T(4,128)} %bitcast.19, f32[8,128]{1,0:T(8,128)S(1)} %shard_map.79.refs_0_.score_ref, bf16[1472,128]{1,0:T(8,128)(2,1)S(1)} %collective-permute-done.17.b_ref.refs_4_.first_ref, bf16[2,1472,128]{2,1,0:T(8,128)(2,1)S(1)} %collective-permute-done.18.refs_5_.pair_ref), custom_call_target="tpu_custom_call" | custom-call | bytes 3409920 | tf_op jit(solution)/shard_map/pallas_call | solution.py:326
  78.4 1.1 %shard_map.82.a_ref = f32[360,1440]{1,0:T(8,128)S(1)} custom-call(f32[360,1440]{1,0:T(8,128)S(1)} %get-tuple-element.52.refs_0_, bf16[360,512]{1,0:T(8,128)(2,1)S(1)} %collective-permute-done.12.refs_1_, bf16[360,512]{1,0:T(8,128)(2,1)S(1)} %collective-permute-done.16.refs_2_, ...), custom_call_target="tpu_custom_call", output_to_operand_aliasing={{}: (0, {})} | custom-call | flops 1592524800 | bytes 12954624 | tf_op jit(solution)/shard_map/pallas_call | solution.py:326
  79.5 0.4 collective-permute-done.19.b_ref
  79.9 1.2 %shard_map.84 = bf16[360,1440]{1,0:T(8,128)(2,1)} custom-call(f32[360,1440]{1,0:T(8,128)S(1)} %shard_map.82.a_ref, bf16[360,1440]{1,0:T(8,128)(2,1)S(1)} %collective-permute-done.19.b_ref), custom_call_target="tpu_custom_call" | custom-call | bytes 9331200 | tf_op jit(solution)/shard_map/pallas_call | solution.py:326
  (10 shorter events, 0.3 us)
Async XLA Ops:
  1.7 8.5 %collective-permute-start.1 = (bf16[1456,128]{1,0:T(8,128)(2,1)S(1)}, bf16[1456,128]{1,0:T(8,128)(2,1)S(1)}, u32[]{:S(2)}, u32[]{:S(2)}) collective-permute-start(bf16[1456,128]{1,0:T(8,128)(2,1)S(1)} %shard_map.68.a_ref.refs_1_.refs_0_), channel_id=1, source_target_pairs={{0,2},{1,5},{2,0},{3,7},{4,6},{5,1},{6,4},{7,3},{8,10},{9,13},{10,... | collective-permute-start | bytes 1118216 | tf_op jit(solution)/shard_map/ppermute | solution.py:356
  4.7 11.2 %collective-permute-start.5 = (bf16[1456,128]{1,0:T(8,128)(2,1)S(1)}, bf16[1456,128]{1,0:T(8,128)(2,1)S(1)}, u32[]{:S(2)}, u32[]{:S(2)}) collective-permute-start(bf16[1456,128]{1,0:T(8,128)(2,1)S(1)} %shard_map.68.a_ref.refs_1_.refs_0_), channel_id=1, source_target_pairs={{8,16},{16,8},{9,17},{17,9},{10,18},{18,10},{11,19},{19,11},{12,20... | collective-permute-start | bytes 1118216 | tf_op jit(solution)/shard_map/ppermute | solution.py:362
  5.4 12.6 %collective-permute-start.3 = (bf16[1456,128]{1,0:T(8,128)(2,1)S(1)}, bf16[1456,128]{1,0:T(8,128)(2,1)S(1)}, u32[]{:S(2)}, u32[]{:S(2)}) collective-permute-start(bf16[1456,128]{1,0:T(8,128)(2,1)S(1)} %shard_map.68.a_ref.refs_1_.refs_0_), channel_id=1, source_target_pairs={{0,8},{8,0},{16,24},{24,16},{1,9},{9,1},{17,25},{25,17},{2,10},{10... | collective-permute-start | bytes 1118216 | tf_op jit(solution)/shard_map/ppermute | solution.py:356
  10.3 15.2 %collective-permute-start.2 = (bf16[2,1456,128]{2,1,0:T(8,128)(2,1)S(1)}, bf16[2,1456,128]{2,1,0:T(8,128)(2,1)S(1)}, u32[]{:S(2)}, u32[]{:S(2)}) collective-permute-start(bf16[2,1456,128]{2,1,0:T(8,128)(2,1)S(1)} %shard_map.71), channel_id=1, source_target_pairs={{0,4},{1,3},{2,6},{3,1},{4,0},{5,7},{6,2},{7,5},{8,12},{9,11},{10,... | collective-permute-start | bytes 2236424 | tf_op jit(solution)/shard_map/ppermute | solution.py:356
  14.4 6.4 %collective-permute-start = (bf16[1440,256]{1,0:T(8,128)(2,1)S(1)}, bf16[1440,256]{1,0:T(8,128)(2,1)S(1)}, u32[]{:S(2)}, u32[]{:S(2)}) collective-permute-start(bf16[1440,256]{1,0:T(8,128)(2,1)S(1)} %get-tuple-element.32), channel_id=1, source_target_pairs={{0,1},{1,0},{2,3},{3,2},{4,5},{5,4},{6,7},{7,6},{8,9},{9,8},{10,11... | collective-permute-start | bytes 2211848 | tf_op jit(solution)/shard_map/ppermute | solution.py:356
  18.0 7.6 %collective-permute-start.10 = (bf16[1456,128]{1,0:T(8,128)(2,1)S(1)}, bf16[1456,128]{1,0:T(8,128)(2,1)S(1)}, u32[]{:S(2)}, u32[]{:S(2)}) collective-permute-start(bf16[1456,128]{1,0:T(8,128)(2,1)S(1)} %collective-permute-done.3.a_ref.refs_3_), channel_id=1, source_target_pairs={{0,2},{1,5},{2,0},{3,7},{4,6},{5,1},{6,4},{7,3},{8,10},{9,13},{10,... | collective-permute-start | bytes 1118216 | tf_op jit(solution)/shard_map/ppermute | solution.py:356
  19.4 13.0 %collective-permute-start.7 = (bf16[2880,128]{1,0:T(8,128)(2,1)S(1)}, bf16[2880,128]{1,0:T(8,128)(2,1)S(1)}, u32[]{:S(2)}, u32[]{:S(2)}) collective-permute-start(bf16[2880,128]{1,0:T(8,128)(2,1)S(1)} %shard_map.73), channel_id=1, source_target_pairs={{0,1},{1,0},{2,3},{3,2},{4,5},{5,4},{6,7},{7,6},{8,9},{9,8},{10,11... | collective-permute-start | bytes 2211848 | tf_op jit(solution)/shard_map/ppermute | solution.py:356
  19.5 13.0 %collective-permute-start.6 = (bf16[1456,128]{1,0:T(8,128)(2,1)S(1)}, bf16[1456,128]{1,0:T(8,128)(2,1)S(1)}, u32[]{:S(2)}, u32[]{:S(2)}) collective-permute-start(bf16[1456,128]{1,0:T(8,128)(2,1)S(1)} %collective-permute-done.5.inner_ref), channel_id=1, source_target_pairs={{8,0},{16,24},{9,1},{17,25},{10,2},{18,26},{11,3},{19,27},{12,4},{... | collective-permute-start | bytes 1118216 | tf_op jit(solution)/shard_map/ppermute | solution.py:364
  21.0 11.5 %collective-permute-start.4 = (bf16[1456,128]{1,0:T(8,128)(2,1)S(1)}, bf16[1456,128]{1,0:T(8,128)(2,1)S(1)}, u32[]{:S(2)}, u32[]{:S(2)}) collective-permute-start(bf16[1456,128]{1,0:T(8,128)(2,1)S(1)} %collective-permute-done.3.a_ref.refs_3_), channel_id=1, source_target_pairs={{8,16},{16,8},{9,17},{17,9},{10,18},{18,10},{11,19},{19,11},{12,20... | collective-permute-start | bytes 1118216 | tf_op jit(solution)/shard_map/ppermute | solution.py:362
  25.6 20.3 %collective-permute-start.11 = (bf16[2,1456,128]{2,1,0:T(8,128)(2,1)S(1)}, bf16[2,1456,128]{2,1,0:T(8,128)(2,1)S(1)}, u32[]{:S(2)}, u32[]{:S(2)}) collective-permute-start(bf16[2,1456,128]{2,1,0:T(8,128)(2,1)S(1)} %shard_map.74), channel_id=1, source_target_pairs={{0,4},{1,3},{2,6},{3,1},{4,0},{5,7},{6,2},{7,5},{8,12},{9,11},{10,... | collective-permute-start | bytes 2236424 | tf_op jit(solution)/shard_map/ppermute | solution.py:356
  32.4 13.4 %collective-permute-start.8 = (bf16[1456,128]{1,0:T(8,128)(2,1)S(1)}, bf16[1456,128]{1,0:T(8,128)(2,1)S(1)}, u32[]{:S(2)}, u32[]{:S(2)}) collective-permute-start(bf16[1456,128]{1,0:T(8,128)(2,1)S(1)} %collective-permute-done.4.inner_ref), channel_id=1, source_target_pairs={{8,0},{16,24},{9,1},{17,25},{10,2},{18,26},{11,3},{19,27},{12,4},{... | collective-permute-start | bytes 1118216 | tf_op jit(solution)/shard_map/ppermute | solution.py:364
  33.7 13.0 %collective-permute-start.12 = (bf16[360,512]{1,0:T(8,128)(2,1)S(1)}, bf16[360,512]{1,0:T(8,128)(2,1)S(1)}, u32[]{:S(2)}, u32[]{:S(2)}) collective-permute-start(bf16[360,512]{1,0:T(8,128)(2,1)S(1)} %get-tuple-element.53), channel_id=1, source_target_pairs={{8,16},{16,8},{9,17},{17,9},{10,18},{18,10},{11,19},{19,11},{12,20... | collective-permute-start | bytes 1105928 | tf_op jit(solution)/shard_map/ppermute | solution.py:362
  34.5 12.0 %collective-permute-start.14 = (bf16[1456,128]{1,0:T(8,128)(2,1)S(1)}, bf16[1456,128]{1,0:T(8,128)(2,1)S(1)}, u32[]{:S(2)}, u32[]{:S(2)}) collective-permute-start(bf16[1456,128]{1,0:T(8,128)(2,1)S(1)} %shard_map.76.a_ref.refs_3_), channel_id=1, source_target_pairs={{0,2},{1,5},{2,0},{3,7},{4,6},{5,1},{6,4},{7,3},{8,10},{9,13},{10,... | collective-permute-start | bytes 1118216 | tf_op jit(solution)/shard_map/ppermute | solution.py:356
  45.9 15.9 %collective-permute-start.17 = (bf16[1472,128]{1,0:T(8,128)(2,1)S(1)}, bf16[1472,128]{1,0:T(8,128)(2,1)S(1)}, u32[]{:S(2)}, u32[]{:S(2)}) collective-permute-start(bf16[1472,128]{1,0:T(8,128)(2,1)S(1)} %shard_map.80.a_ref.refs_3_), channel_id=1, source_target_pairs={{0,2},{1,5},{2,0},{3,7},{4,6},{5,1},{6,4},{7,3},{8,10},{9,13},{10,... | collective-permute-start | bytes 1130504 | tf_op jit(solution)/shard_map/ppermute | solution.py:356
  46.5 15.3 %collective-permute-start.9 = (bf16[360,512]{1,0:T(8,128)(2,1)S(1)}, bf16[360,512]{1,0:T(8,128)(2,1)S(1)}, u32[]{:S(2)}, u32[]{:S(2)}) collective-permute-start(bf16[360,512]{1,0:T(8,128)(2,1)S(1)} %get-tuple-element.43), channel_id=1, source_target_pairs={{0,8},{8,0},{16,24},{24,16},{1,9},{9,1},{17,25},{25,17},{2,10},{10... | collective-permute-start | bytes 1105928 | tf_op jit(solution)/shard_map/ppermute | solution.py:356
  46.5 26.0 %collective-permute-start.15 = (bf16[2,1456,128]{2,1,0:T(8,128)(2,1)S(1)}, bf16[2,1456,128]{2,1,0:T(8,128)(2,1)S(1)}, u32[]{:S(2)}, u32[]{:S(2)}) collective-permute-start(bf16[2,1456,128]{2,1,0:T(8,128)(2,1)S(1)} %shard_map.77), channel_id=1, source_target_pairs={{0,4},{1,3},{2,6},{3,1},{4,0},{5,7},{6,2},{7,5},{8,12},{9,11},{10,... | collective-permute-start | bytes 2236424 | tf_op jit(solution)/shard_map/ppermute | solution.py:356
  46.7 18.1 %collective-permute-start.13 = (bf16[360,512]{1,0:T(8,128)(2,1)S(1)}, bf16[360,512]{1,0:T(8,128)(2,1)S(1)}, u32[]{:S(2)}, u32[]{:S(2)}) collective-permute-start(bf16[360,512]{1,0:T(8,128)(2,1)S(1)} %get-tuple-element.50), channel_id=1, source_target_pairs={{0,16},{8,24},{16,0},{24,8},{1,17},{9,25},{17,1},{25,9},{2,18},{10... | collective-permute-start | bytes 1105928 | tf_op jit(solution)/shard_map/ppermute | solution.py:356
  61.8 14.2 %collective-permute-start.18 = (bf16[2,1472,128]{2,1,0:T(8,128)(2,1)S(1)}, bf16[2,1472,128]{2,1,0:T(8,128)(2,1)S(1)}, u32[]{:S(2)}, u32[]{:S(2)}) collective-permute-start(bf16[2,1472,128]{2,1,0:T(8,128)(2,1)S(1)} %shard_map.81), channel_id=1, source_target_pairs={{0,4},{1,3},{2,6},{3,1},{4,0},{5,7},{6,2},{7,5},{8,12},{9,11},{10,... | collective-permute-start | bytes 2261000 | tf_op jit(solution)/shard_map/ppermute | solution.py:356
  64.8 11.2 %collective-permute-start.16 = (bf16[360,512]{1,0:T(8,128)(2,1)S(1)}, bf16[360,512]{1,0:T(8,128)(2,1)S(1)}, u32[]{:S(2)}, u32[]{:S(2)}) collective-permute-start(bf16[360,512]{1,0:T(8,128)(2,1)S(1)} %get-tuple-element.53), channel_id=1, source_target_pairs={{0,24},{24,0},{1,25},{25,1},{2,26},{26,2},{3,27},{27,3},{4,28},{28... | collective-permute-start | bytes 1105928 | tf_op jit(solution)/shard_map/ppermute | solution.py:363
  77.0 2.8 %collective-permute-start.19 = (bf16[360,1440]{1,0:T(8,128)(2,1)S(1)}, bf16[360,1440]{1,0:T(8,128)(2,1)S(1)}, u32[]{:S(2)}, u32[]{:S(2)}) collective-permute-start(bf16[360,1440]{1,0:T(8,128)(2,1)S(1)} %shard_map.83), channel_id=1, source_target_pairs={{0,1},{1,0},{2,3},{3,2},{4,5},{5,4},{6,7},{7,6},{8,9},{9,8},{10,11... | collective-permute-start | bytes 3110408 | tf_op jit(solution)/shard_map/ppermute | solution.py:356

commit v5 on v4

--- a/solution.py
+++ b/solution.py
@@ -16,7 +16,7 @@
     "f1": ("across", "saved",),
     "j1": ("s0",),
     "third": ("outside", "saved_swapped",),
-    "h3_inner": ("inside", "outside", "saved_swapped", "across",),
+    "h3_inner": ("inside", "outside", "across",),
     "f2": ("s0",),
     "h1": ("third",),
     "h2": ("h3_inner",),
@@ -25,7 +25,7 @@
     "j3": ("h1",),
     "turned": ("own",),
 }
-SCALE, SCALES = 3, {"t2": 0.5, "turned": 2, "t0": 0.5}
+SCALE, SCALES = 3, {"t2": 0.5, "turned": 2, "t0": 0.5, "own": 40}
 TOTALS = ("t0", "t1", "t2")
 H3 = ("h3_inner", "h3_outer")
 
@@ -103,28 +103,36 @@
 
 def fetch(source, target, sems, cores):
     copies = [
-        pltpu.make_async_copy(source.at[c, core], target.at[c, n], sems.at[c, n])
+        [pltpu.make_async_copy(source.at[c, core], target.at[c, n], sems.at[c, n]) for n, core in enumerate(cores)]
         for c in range(source.shape[0])
-        for n, core in enumerate(cores)
     ]
-    for copy in copies:
-        copy.start()
-    for copy in copies:
-        copy.wait()
-
-
-def stacked(ref, n, cols):
-    return jnp.concatenate([ref[c, n, :, cols] for c in range(ref.shape[0])], axis=0)
+    for chip in copies:
+        for copy in chip:
+            copy.start()
+    return copies
+
+
+def arrive(copies):
+    for chip in copies:
+        for copy in chip:
+            copy.wait()
+
+
+def stacked(ref, n, cols, chips):
+    return jnp.concatenate([ref[c, n, :, cols] for c in chips], axis=0)
 
 
 def turn_kernel(hidden_ref, keep_ref, leave_ref, here, sems):
     core = lax.axis_index("expert") & 1
-    fetch(hidden_ref, here, sems, (core, 1 - core))
-    width = here.shape[3]
-    for a in range(0, width, LANES):
-        cols = slice(a, min(a + LANES, width))
-        keep_ref[cols, :] = stacked(here, 0, cols).T
-        leave_ref[cols, :] = stacked(here, 1, cols).T
+    copies = fetch(hidden_ref, here, sems, (core, 1 - core))
+    width, pair = here.shape[3], 2 * here.shape[2]
+    for c in range(0, here.shape[0], 2):
+        arrive(copies[c:c + 2])
+        to = slice(c // 2 * pair, (c // 2 + 1) * pair)
+        for a in range(0, width, LANES):
+            cols = slice(a, min(a + LANES, width))
+            keep_ref[cols, to] = stacked(here, 0, cols, (c, c + 1)).T
+            leave_ref[cols, to] = stacked(here, 1, cols, (c, c + 1)).T
 
 
 def quarter_kernel(keep_ref, got_ref, *rest):
@@ -138,12 +146,13 @@
 
 
 def saved_kernel(saved_ref, out_ref, here, sems):
-    fetch(saved_ref, here, sems, (1 - (lax.axis_index("expert") & 1),))
+    arrive(fetch(saved_ref, here, sems, (1 - (lax.axis_index("expert") & 1),)))
+    chips = range(here.shape[0])
     rows, width = here.shape[0] * here.shape[2], here.shape[3]
     full, rest = width // LANES, width % LANES
     for j in range(full):
-        out_ref[j * rows:(j + 1) * rows, :] = stacked(here, 0, slice(j * LANES, (j + 1) * LANES))
-    tail = stacked(here, 0, slice(full * LANES, width)).astype(jnp.float32)
+        out_ref[j * rows:(j + 1) * rows, :] = stacked(here, 0, slice(j * LANES, (j + 1) * LANES), chips)
+    tail = stacked(here, 0, slice(full * LANES, width), chips).astype(jnp.float32)
     step = rows * rest // LANES
     out_ref[full * rows:, :] = jnp.concatenate(
         [tail[a * step:(a + 1) * step] for a in range(LANES // rest)], axis=1
@@ -262,9 +271,11 @@
 
 def score_kernel(saved_ref, got_ref, *refs):
     blocks, (score_ref, here, sems) = four(refs[:-3]), refs[-3:]
-    fetch(saved_ref, here, sems, (lax.axis_index("expert") & 1,))
+    copies = fetch(saved_ref, here, sems, (lax.axis_index("expert") & 1,))
+    chips = range(here.shape[0])
     rows, width = here.shape[0] * here.shape[2], here.shape[3]
     tables = block_tables(blocks, width)
+    arrive(copies)
     full, rest = width // LANES, width % LANES
     total = jnp.zeros((2 * rows, len(blocks) * LANES), jnp.float32)
     for a, b in chunks(width):
@@ -278,7 +289,7 @@
                     jnp.concatenate([tail[:, n * rest:(n + 1) * rest] for n in range(LANES // rest)], axis=0)
                 )
         theirs = pieces[0] if len(pieces) == 1 else jnp.concatenate(pieces, axis=1)
-        saved = jnp.concatenate([stacked(here, 0, slice(a, b)), theirs], axis=0)
+        saved = jnp.concatenate([stacked(here, 0, slice(a, b), chips), theirs], axis=0)
         total = total + jnp.dot(saved, tokens_of(blocks, a, b), preferred_element_type=jnp.float32)
     scores = []
     for w in range(2):
@@ -309,12 +320,18 @@
     out_ref[...] = total
 
 
-def add_kernel(a_ref, b_ref, out_ref):
-    out_ref[...] = (a_ref[...] + b_ref[...].astype(jnp.float32)).astype(out_ref.dtype)
-
-
-def call(kernel, outs, args, scratch=(), flops=0, limit=8, aliases=None, name=None):
-    smem, vmem, hbm = (pl.BlockSpec(memory_space=space) for space in (pltpu.SMEM, pltpu.VMEM, pltpu.HBM))
+def add_kernel(a_ref, b_ref, out_ref, total, sems):
+    copies = []
+    for n, (a, b) in enumerate(chunks(a_ref.shape[1], 4 * LANES)):
+        total[:, a:b] = (a_ref[:, a:b] + b_ref[:, a:b].astype(jnp.float32)).astype(total.dtype)
+        copies.append(pltpu.make_async_copy(total.at[:, a:b], out_ref.at[:, a:b], sems.at[n]))
+        copies[-1].start()
+    for copy in copies:
+        copy.wait()
+
+
+def call(kernel, outs, args, scratch=(), flops=0, limit=8, aliases=None, name=None, out_space=pltpu.VMEM):
+    vmem, hbm = (pl.BlockSpec(memory_space=space) for space in (pltpu.VMEM, pltpu.HBM))
     moved = sum(a.size * a.dtype.itemsize for a in args)
     scale = SCALES.get(name, SCALE)
     specs, operands = [], []
@@ -327,7 +344,7 @@
         kernel,
         out_shape=outs,
         in_specs=specs,
-        out_specs=[vmem] * len(outs),
+        out_specs=[pl.BlockSpec(memory_space=out_space)] * len(outs),
         scratch_shapes=list(scratch),
         input_output_aliases=aliases or {},
         compiler_params=pltpu.CompilerParams(vmem_limit_bytes=limit * 1024 * 1024),
@@ -468,7 +485,10 @@
         ),
         "part_swapped": (core, "part"),
         "down": (
-            lambda a, b: call(add_kernel, [jax.ShapeDtypeStruct((rows, width), bf16)], (a, b), name="down")[0],
+            lambda a, b: call(
+                add_kernel, [jax.ShapeDtypeStruct((rows, width), bf16)], (a, b), name="down", out_space=pltpu.HBM,
+                scratch=[pltpu.VMEM((rows, width), bf16), pltpu.SemaphoreType.DMA((len(chunks(width, 4 * LANES)),))],
+            )[0],
             "mine", "part_swapped",
         ),
         "route": (

time: 81.4 us -> 81.2 us (level)
  no operation moved by 1% of the time
where the time goes in v5:
time: 81.2 us; the launch traced here: 80.9 us
  waiting for transfers between devices  34.6 us (43%)
  starting transfers between devices  28.3 us (35%)
  Pallas kernels  17.1 us (21%)
  between operations  0.85 us (1%)
    ppermute x14, waiting for transfers between devices, permute(): lax.ppermute(x, name, [(i, target(i)) for i in range(lax.axis_size(name))])  20.3 us
    ppermute x14, starting transfers between devices, permute(): lax.ppermute(x, name, [(i, target(i)) for i in range(lax.axis_size(name))])  19.5 us
    pallas_call x18, Pallas kernels, call(): pl.pallas_call(kernel, out_shape=outs, in_specs=specs, out_specs=[pl.Bloc...  17.1 us
    ppermute x2, waiting for transfers between devices, planes4(): outward = lambda x: lax.ppermute(x, 'dp', [(1, 0), (2, 3)])  12.9 us
    ppermute x1, starting transfers between devices, planes4(): outer = lambda x: lax.ppermute(x, 'dp', [(0, 3), (3, 0)])  4.16 us
    ppermute x2, starting transfers between devices, planes4(): outward = lambda x: lax.ppermute(x, 'dp', [(1, 0), (2, 3)])  2.56 us
    ppermute x3, starting transfers between devices, planes4(): inner = lambda x: lax.ppermute(x, 'dp', [(1, 2), (2, 1)])  2.04 us
  transfers between devices with their start and end apart: 20, of which 9 were waited for; matrix products, arithmetic and copies ran while one was open for 0% of the time, Pallas kernels for 17%

profile of v5, /device:TPU:0, one launch (start us, length us, event | category | flops | bytes accessed | tf_op | source)
XLA Modules:
  0.0 80.9 jit_solution(16959769336740839471)
XLA Ops:
  0.6 1.0 %shard_map.68.a_ref.refs_1_.refs_0_ = bf16[1456,128]{1,0:T(8,128)(2,1)S(1)} custom-call(bf16[1,1,1440,128]{3,2,1,0:T(8,128)(2,1)} %bitcast.17, s32[1,1,4,128]{3,2,1,0:T(4,128)} %bitcast.18, f32[1,1,4,128]{3,2,1,0:T(4,128)} %bitcast.20), custom_call_target="tpu_custom_call" | custom-call | bytes 14909440 | tf_op jit(solution)/shard_map/pallas_call | solution.py:343
  1.7 3.0 %collective-permute-start.1 = (bf16[1456,128]{1,0:T(8,128)(2,1)S(1)}, bf16[1456,128]{1,0:T(8,128)(2,1)S(1)}, u32[]{:S(2)}, u32[]{:S(2)}) collective-permute-start(bf16[1456,128]{1,0:T(8,128)(2,1)S(1)} %shard_map.68.a_ref.refs_1_.refs_0_), channel_id=1, source_target_pairs={{0,2},{1,5},{2,0},{3,7},{4,6},{5,1},{6,4},{7,3},{8,10},{9,13},{10,... | collective-permute-start | bytes 1118216 | tf_op jit(solution)/shard_map/ppermute | solution.py:373
  4.7 0.7 collective-permute-start.5
  5.4 4.4 %collective-permute-start.3 = (bf16[1456,128]{1,0:T(8,128)(2,1)S(1)}, bf16[1456,128]{1,0:T(8,128)(2,1)S(1)}, u32[]{:S(2)}, u32[]{:S(2)}) collective-permute-start(bf16[1456,128]{1,0:T(8,128)(2,1)S(1)} %shard_map.68.a_ref.refs_1_.refs_0_), channel_id=1, source_target_pairs={{0,8},{8,0},{16,24},{24,16},{1,9},{9,1},{17,25},{25,17},{2,10},{10... | collective-permute-start | bytes 1118216 | tf_op jit(solution)/shard_map/ppermute | solution.py:373
  9.8 0.4 collective-permute-done.1.b_ref.refs_2_.refs_1_
  10.3 2.1 %collective-permute-start.2 = (bf16[2,1456,128]{2,1,0:T(8,128)(2,1)S(1)}, bf16[2,1456,128]{2,1,0:T(8,128)(2,1)S(1)}, u32[]{:S(2)}, u32[]{:S(2)}) collective-permute-start(bf16[2,1456,128]{2,1,0:T(8,128)(2,1)S(1)} %shard_map.71), channel_id=1, source_target_pairs={{0,4},{1,3},{2,6},{3,1},{4,0},{5,7},{6,2},{7,5},{8,12},{9,11},{10,... | collective-permute-start | bytes 2236424 | tf_op jit(solution)/shard_map/ppermute | solution.py:373
  12.4 1.8 %shard_map.69 = (bf16[1440,256]{1,0:T(8,128)(2,1)S(1)}, bf16[1440,256]{1,0:T(8,128)(2,1)S(1)}) custom-call(bf16[4,2,64,1440]{3,2,1,0:T(8,128)(2,1)} %bitcast.13), custom_call_target="tpu_custom_call" | custom-call | bytes 2949120 | tf_op jit(solution)/shard_map/pallas_call | solution.py:343
  14.2 0.1 collective-permute-start
  14.3 1.5 %shard_map.73 = bf16[2880,128]{1,0:T(8,128)(2,1)S(1)} custom-call(bf16[4,2,64,1440]{3,2,1,0:T(8,128)(2,1)} %bitcast.14), custom_call_target="tpu_custom_call" | custom-call | bytes 4423680 | tf_op jit(solution)/shard_map/pallas_call | solution.py:343
  15.7 0.0 collective-permute-done.5.inner_ref
  15.7 2.2 %collective-permute-done.3.a_ref.refs_3_ = bf16[1456,128]{1,0:T(8,128)(2,1)S(1)} collective-permute-done((bf16[1456,128]{1,0:T(8,128)(2,1)S(1)}, bf16[1456,128]{1,0:T(8,128)(2,1)S(1)}, u32[]{:S(2)}, u32[]{:S(2)}) %collective-permute-start.3) | collective-permute-done | bytes 372768 | tf_op jit(solution)/shard_map/ppermute | solution.py:373
  18.0 1.5 %collective-permute-start.10 = (bf16[1456,128]{1,0:T(8,128)(2,1)S(1)}, bf16[1456,128]{1,0:T(8,128)(2,1)S(1)}, u32[]{:S(2)}, u32[]{:S(2)}) collective-permute-start(bf16[1456,128]{1,0:T(8,128)(2,1)S(1)} %collective-permute-done.3.a_ref.refs_3_), channel_id=1, source_target_pairs={{0,2},{1,5},{2,0},{3,7},{4,6},{5,1},{6,4},{7,3},{8,10},{9,13},{10,... | collective-permute-start | bytes 1118216 | tf_op jit(solution)/shard_map/ppermute | solution.py:373
  19.4 0.0 collective-permute-start.7
  19.5 1.3 %collective-permute-start.6 = (bf16[1456,128]{1,0:T(8,128)(2,1)S(1)}, bf16[1456,128]{1,0:T(8,128)(2,1)S(1)}, u32[]{:S(2)}, u32[]{:S(2)}) collective-permute-start(bf16[1456,128]{1,0:T(8,128)(2,1)S(1)} %collective-permute-done.5.inner_ref), channel_id=1, source_target_pairs={{8,0},{16,24},{9,1},{17,25},{10,2},{18,26},{11,3},{19,27},{12,4},{... | collective-permute-start | bytes 1118216 | tf_op jit(solution)/shard_map/ppermute | solution.py:381
  20.7 0.0 collective-permute-done.got_ref
  20.7 0.2 shard_map.70
  21.0 0.7 collective-permute-start.4
  21.6 3.9 %collective-permute-done.10.b_ref.refs_4_ = bf16[1456,128]{1,0:T(8,128)(2,1)S(1)} collective-permute-done((bf16[1456,128]{1,0:T(8,128)(2,1)S(1)}, bf16[1456,128]{1,0:T(8,128)(2,1)S(1)}, u32[]{:S(2)}, u32[]{:S(2)}) %collective-permute-start.10) | collective-permute-done | bytes 372768 | tf_op jit(solution)/shard_map/ppermute | solution.py:373
  25.5 0.0 collective-permute-done.2.refs_3_.refs_2_
  25.6 2.5 %collective-permute-start.11 = (bf16[2,1456,128]{2,1,0:T(8,128)(2,1)S(1)}, bf16[2,1456,128]{2,1,0:T(8,128)(2,1)S(1)}, u32[]{:S(2)}, u32[]{:S(2)}) collective-permute-start(bf16[2,1456,128]{2,1,0:T(8,128)(2,1)S(1)} %shard_map.74), channel_id=1, source_target_pairs={{0,4},{1,3},{2,6},{3,1},{4,0},{5,7},{6,2},{7,5},{8,12},{9,11},{10,... | collective-permute-start | bytes 2236424 | tf_op jit(solution)/shard_map/ppermute | solution.py:373
  28.1 4.4 %collective-permute-done.6.outer_ref = bf16[1456,128]{1,0:T(8,128)(2,1)S(1)} collective-permute-done((bf16[1456,128]{1,0:T(8,128)(2,1)S(1)}, bf16[1456,128]{1,0:T(8,128)(2,1)S(1)}, u32[]{:S(2)}, u32[]{:S(2)}) %collective-permute-start.6) | collective-permute-done | bytes 372768 | tf_op jit(solution)/shard_map/ppermute | solution.py:381
  32.4 0.0 collective-permute-done.4.inner_ref
  32.4 1.3 %collective-permute-start.8 = (bf16[1456,128]{1,0:T(8,128)(2,1)S(1)}, bf16[1456,128]{1,0:T(8,128)(2,1)S(1)}, u32[]{:S(2)}, u32[]{:S(2)}) collective-permute-start(bf16[1456,128]{1,0:T(8,128)(2,1)S(1)} %collective-permute-done.4.inner_ref), channel_id=1, source_target_pairs={{8,0},{16,24},{9,1},{17,25},{10,2},{18,26},{11,3},{19,27},{12,4},{... | collective-permute-start | bytes 1118216 | tf_op jit(solution)/shard_map/ppermute | solution.py:381
  33.7 0.7 collective-permute-start.12
  34.5 0.6 collective-permute-start.14
  35.1 2.3 %shard_map.79.refs_0_.score_ref = f32[8,128]{1,0:T(8,128)S(1)} custom-call(bf16[4,2,64,1440]{3,2,1,0:T(8,128)(2,1)} %bitcast.15, bf16[2880,128]{1,0:T(8,128)(2,1)S(1)} %collective-permute-done.7.got_ref, bf16[1456,128]{1,0:T(8,128)(2,1)S(1)} %shard_map.68.a_ref.refs_1_.refs_0_, bf16[1456,128]{1,0:T(8,128)(2,1)S(1)} %collective-permute-done.1.b_ref.refs_2_.refs_1_, ...), custom_call_target="tpu_custom_call" | custom-call | flops 1132462080 | bytes 11108352 | tf_op jit(solution)/shard_map/pallas_call | solution.py:343
  37.3 8.5 %collective-permute-done.8.outer_ref = bf16[1456,128]{1,0:T(8,128)(2,1)S(1)} collective-permute-done((bf16[1456,128]{1,0:T(8,128)(2,1)S(1)}, bf16[1456,128]{1,0:T(8,128)(2,1)S(1)}, u32[]{:S(2)}, u32[]{:S(2)}) %collective-permute-start.8) | collective-permute-done | bytes 372768 | tf_op jit(solution)/shard_map/ppermute | solution.py:381
  45.9 0.6 collective-permute-start.17
  46.5 0.0 collective-permute-start.9
  46.5 0.0 collective-permute-done.14.b_ref.refs_4_
  46.5 0.1 collective-permute-start.15
  46.7 0.0 collective-permute-done.12.refs_1_
  46.7 2.8 %collective-permute-start.13 = (bf16[360,512]{1,0:T(8,128)(2,1)S(1)}, bf16[360,512]{1,0:T(8,128)(2,1)S(1)}, u32[]{:S(2)}, u32[]{:S(2)}) collective-permute-start(bf16[360,512]{1,0:T(8,128)(2,1)S(1)} %get-tuple-element.50), channel_id=1, source_target_pairs={{0,16},{8,24},{16,0},{24,8},{1,17},{9,25},{17,1},{25,9},{2,18},{10... | collective-permute-start | bytes 1105928 | tf_op jit(solution)/shard_map/ppermute | solution.py:373
  49.4 12.2 %collective-permute-done.9.refs_2_ = bf16[360,512]{1,0:T(8,128)(2,1)S(1)} collective-permute-done((bf16[360,512]{1,0:T(8,128)(2,1)S(1)}, bf16[360,512]{1,0:T(8,128)(2,1)S(1)}, u32[]{:S(2)}, u32[]{:S(2)}) %collective-permute-start.9) | collective-permute-done | bytes 368672 | tf_op jit(solution)/shard_map/ppermute | solution.py:373
  61.7 1.8 %collective-permute-start.18 = (bf16[2,1472,128]{2,1,0:T(8,128)(2,1)S(1)}, bf16[2,1472,128]{2,1,0:T(8,128)(2,1)S(1)}, u32[]{:S(2)}, u32[]{:S(2)}) collective-permute-start(bf16[2,1472,128]{2,1,0:T(8,128)(2,1)S(1)} %shard_map.81), channel_id=1, source_target_pairs={{0,4},{1,3},{2,6},{3,1},{4,0},{5,7},{6,2},{7,5},{8,12},{9,11},{10,... | collective-permute-start | bytes 2261000 | tf_op jit(solution)/shard_map/ppermute | solution.py:373
  63.5 1.2 %collective-permute-done.13.refs_2_ = bf16[360,512]{1,0:T(8,128)(2,1)S(1)} collective-permute-done((bf16[360,512]{1,0:T(8,128)(2,1)S(1)}, bf16[360,512]{1,0:T(8,128)(2,1)S(1)}, u32[]{:S(2)}, u32[]{:S(2)}) %collective-permute-start.13) | collective-permute-done | bytes 368672 | tf_op jit(solution)/shard_map/ppermute | solution.py:373
  64.7 4.2 %collective-permute-start.16 = (bf16[360,512]{1,0:T(8,128)(2,1)S(1)}, bf16[360,512]{1,0:T(8,128)(2,1)S(1)}, u32[]{:S(2)}, u32[]{:S(2)}) collective-permute-start(bf16[360,512]{1,0:T(8,128)(2,1)S(1)} %get-tuple-element.53), channel_id=1, source_target_pairs={{0,24},{24,0},{1,25},{25,1},{2,26},{26,2},{3,27},{27,3},{4,28},{28... | collective-permute-start | bytes 1105928 | tf_op jit(solution)/shard_map/ppermute | solution.py:380
  68.9 1.7 %shard_map.72 = (f32[360,1440]{1,0:T(8,128)S(1)}, f32[360,1440]{1,0:T(8,128)S(1)}) custom-call(bf16[360,512]{1,0:T(8,128)(2,1)S(1)} %get-tuple-element.33.refs_0_, bf16[1456,128]{1,0:T(8,128)(2,1)S(1)} %shard_map.68.a_ref.refs_1_.refs_0_, bf16[1456,128]{1,0:T(8,128)(2,1)S(1)} %collective-permute-done.1.b_ref.refs_2_.refs_1_, ...), custom_call_target="tpu_custom_call" | custom-call | flops 530841600 | bytes 929792 | tf_op jit(solution)/shard_map/pallas_call | solution.py:343
  70.6 1.9 %shard_map.75 = (f32[360,1440]{1,0:T(8,128)S(1)}, f32[360,1440]{1,0:T(8,128)S(1)}) custom-call(f32[360,1440]{1,0:T(8,128)S(1)} %get-tuple-element.34.refs_0_, f32[360,1440]{1,0:T(8,128)S(1)} %get-tuple-element.35.refs_1_, bf16[360,512]{1,0:T(8,128)(2,1)S(1)} %collective-permute-done.9.refs_2_, ...), custom_call_target="tpu_custom_call", output_to_operand_aliasing={{0}: (0, {}), {1}: (1, {})} | custom-call | flops 3185049600 | bytes 18020352 | tf_op jit(solution)/shard_map/pallas_call | solution.py:343
  72.5 0.0 collective-permute-done.15.refs_5_
  72.5 1.9 %shard_map.78 = (f32[360,1440]{1,0:T(8,128)S(1)}, f32[360,1440]{1,0:T(8,128)S(1)}) custom-call(f32[360,1440]{1,0:T(8,128)S(1)} %get-tuple-element.47.refs_0_, f32[360,1440]{1,0:T(8,128)S(1)} %get-tuple-element.48.refs_1_, bf16[360,512]{1,0:T(8,128)(2,1)S(1)} %collective-permute-done.13.refs_2_, ...), custom_call_target="tpu_custom_call", output_to_operand_aliasing={{0}: (0, {}), {1}: (1, {})} | custom-call | flops 530841600 | bytes 3003392 | tf_op jit(solution)/shard_map/pallas_call | solution.py:343
  74.5 1.4 %collective-permute-done.16.refs_2_ = bf16[360,512]{1,0:T(8,128)(2,1)S(1)} collective-permute-done((bf16[360,512]{1,0:T(8,128)(2,1)S(1)}, bf16[360,512]{1,0:T(8,128)(2,1)S(1)}, u32[]{:S(2)}, u32[]{:S(2)}) %collective-permute-start.16) | collective-permute-done | bytes 368672 | tf_op jit(solution)/shard_map/ppermute | solution.py:380
  75.9 1.1 %shard_map.83 = bf16[360,1440]{1,0:T(8,128)(2,1)S(1)} custom-call(f32[360,1440]{1,0:T(8,128)S(1)} %get-tuple-element.57.refs_0_, bf16[360,512]{1,0:T(8,128)(2,1)S(1)} %collective-permute-done.12.refs_1_, bf16[360,512]{1,0:T(8,128)(2,1)S(1)} %collective-permute-done.16.refs_2_, bf16[1472,128]{1,0:T(8,128)(2,1)S(1)} %shard_map.80.a_ref.refs_3_, ...), custom_call_target="tpu_custom_call" | custom-call | flops 1592524800 | bytes 12954624 | tf_op jit(solution)/shard_map/pallas_call | solution.py:343
  77.0 0.1 collective-permute-start.19
  77.0 1.3 %shard_map.85 = f32[4,128]{1,0:T(4,128)} custom-call(s32[1,1,4,128]{3,2,1,0:T(4,128)} %bitcast.19, f32[8,128]{1,0:T(8,128)S(1)} %shard_map.79.refs_0_.score_ref, bf16[1472,128]{1,0:T(8,128)(2,1)S(1)} %collective-permute-done.17.b_ref.refs_4_.first_ref, bf16[2,1472,128]{2,1,0:T(8,128)(2,1)S(1)} %collective-permute-done.18.refs_5_.pair_ref), custom_call_target="tpu_custom_call" | custom-call | bytes 3409920 | tf_op jit(solution)/shard_map/pallas_call | solution.py:343
  78.3 1.1 %shard_map.82.a_ref = f32[360,1440]{1,0:T(8,128)S(1)} custom-call(f32[360,1440]{1,0:T(8,128)S(1)} %get-tuple-element.52.refs_0_, bf16[360,512]{1,0:T(8,128)(2,1)S(1)} %collective-permute-done.12.refs_1_, bf16[360,512]{1,0:T(8,128)(2,1)S(1)} %collective-permute-done.16.refs_2_, ...), custom_call_target="tpu_custom_call", output_to_operand_aliasing={{}: (0, {})} | custom-call | flops 1592524800 | bytes 12954624 | tf_op jit(solution)/shard_map/pallas_call | solution.py:343
  79.4 0.4 collective-permute-done.19.b_ref
  79.8 1.1 %shard_map.84 = bf16[360,1440]{1,0:T(8,128)(2,1)} custom-call(f32[360,1440]{1,0:T(8,128)S(1)} %shard_map.82.a_ref, bf16[360,1440]{1,0:T(8,128)(2,1)S(1)} %collective-permute-done.19.b_ref), custom_call_target="tpu_custom_call" | custom-call | bytes 9331200 | tf_op jit(solution)/shard_map/pallas_call | solution.py:343
  (10 shorter events, 0.3 us)
Async XLA Ops:
  1.7 8.5 %collective-permute-start.1 = (bf16[1456,128]{1,0:T(8,128)(2,1)S(1)}, bf16[1456,128]{1,0:T(8,128)(2,1)S(1)}, u32[]{:S(2)}, u32[]{:S(2)}) collective-permute-start(bf16[1456,128]{1,0:T(8,128)(2,1)S(1)} %shard_map.68.a_ref.refs_1_.refs_0_), channel_id=1, source_target_pairs={{0,2},{1,5},{2,0},{3,7},{4,6},{5,1},{6,4},{7,3},{8,10},{9,13},{10,... | collective-permute-start | bytes 1118216 | tf_op jit(solution)/shard_map/ppermute | solution.py:373
  4.7 11.1 %collective-permute-start.5 = (bf16[1456,128]{1,0:T(8,128)(2,1)S(1)}, bf16[1456,128]{1,0:T(8,128)(2,1)S(1)}, u32[]{:S(2)}, u32[]{:S(2)}) collective-permute-start(bf16[1456,128]{1,0:T(8,128)(2,1)S(1)} %shard_map.68.a_ref.refs_1_.refs_0_), channel_id=1, source_target_pairs={{8,16},{16,8},{9,17},{17,9},{10,18},{18,10},{11,19},{19,11},{12,20... | collective-permute-start | bytes 1118216 | tf_op jit(solution)/shard_map/ppermute | solution.py:379
  5.4 12.6 %collective-permute-start.3 = (bf16[1456,128]{1,0:T(8,128)(2,1)S(1)}, bf16[1456,128]{1,0:T(8,128)(2,1)S(1)}, u32[]{:S(2)}, u32[]{:S(2)}) collective-permute-start(bf16[1456,128]{1,0:T(8,128)(2,1)S(1)} %shard_map.68.a_ref.refs_1_.refs_0_), channel_id=1, source_target_pairs={{0,8},{8,0},{16,24},{24,16},{1,9},{9,1},{17,25},{25,17},{2,10},{10... | collective-permute-start | bytes 1118216 | tf_op jit(solution)/shard_map/ppermute | solution.py:373
  10.3 15.2 %collective-permute-start.2 = (bf16[2,1456,128]{2,1,0:T(8,128)(2,1)S(1)}, bf16[2,1456,128]{2,1,0:T(8,128)(2,1)S(1)}, u32[]{:S(2)}, u32[]{:S(2)}) collective-permute-start(bf16[2,1456,128]{2,1,0:T(8,128)(2,1)S(1)} %shard_map.71), channel_id=1, source_target_pairs={{0,4},{1,3},{2,6},{3,1},{4,0},{5,7},{6,2},{7,5},{8,12},{9,11},{10,... | collective-permute-start | bytes 2236424 | tf_op jit(solution)/shard_map/ppermute | solution.py:373
  14.2 6.6 %collective-permute-start = (bf16[1440,256]{1,0:T(8,128)(2,1)S(1)}, bf16[1440,256]{1,0:T(8,128)(2,1)S(1)}, u32[]{:S(2)}, u32[]{:S(2)}) collective-permute-start(bf16[1440,256]{1,0:T(8,128)(2,1)S(1)} %get-tuple-element.32), channel_id=1, source_target_pairs={{0,1},{1,0},{2,3},{3,2},{4,5},{5,4},{6,7},{7,6},{8,9},{9,8},{10,11... | collective-permute-start | bytes 2211848 | tf_op jit(solution)/shard_map/ppermute | solution.py:373
  18.0 7.6 %collective-permute-start.10 = (bf16[1456,128]{1,0:T(8,128)(2,1)S(1)}, bf16[1456,128]{1,0:T(8,128)(2,1)S(1)}, u32[]{:S(2)}, u32[]{:S(2)}) collective-permute-start(bf16[1456,128]{1,0:T(8,128)(2,1)S(1)} %collective-permute-done.3.a_ref.refs_3_), channel_id=1, source_target_pairs={{0,2},{1,5},{2,0},{3,7},{4,6},{5,1},{6,4},{7,3},{8,10},{9,13},{10,... | collective-permute-start | bytes 1118216 | tf_op jit(solution)/shard_map/ppermute | solution.py:373
  19.4 13.0 %collective-permute-start.7 = (bf16[2880,128]{1,0:T(8,128)(2,1)S(1)}, bf16[2880,128]{1,0:T(8,128)(2,1)S(1)}, u32[]{:S(2)}, u32[]{:S(2)}) collective-permute-start(bf16[2880,128]{1,0:T(8,128)(2,1)S(1)} %shard_map.73), channel_id=1, source_target_pairs={{0,1},{1,0},{2,3},{3,2},{4,5},{5,4},{6,7},{7,6},{8,9},{9,8},{10,11... | collective-permute-start | bytes 2211848 | tf_op jit(solution)/shard_map/ppermute | solution.py:373
  19.5 13.0 %collective-permute-start.6 = (bf16[1456,128]{1,0:T(8,128)(2,1)S(1)}, bf16[1456,128]{1,0:T(8,128)(2,1)S(1)}, u32[]{:S(2)}, u32[]{:S(2)}) collective-permute-start(bf16[1456,128]{1,0:T(8,128)(2,1)S(1)} %collective-permute-done.5.inner_ref), channel_id=1, source_target_pairs={{8,0},{16,24},{9,1},{17,25},{10,2},{18,26},{11,3},{19,27},{12,4},{... | collective-permute-start | bytes 1118216 | tf_op jit(solution)/shard_map/ppermute | solution.py:381
  21.0 11.5 %collective-permute-start.4 = (bf16[1456,128]{1,0:T(8,128)(2,1)S(1)}, bf16[1456,128]{1,0:T(8,128)(2,1)S(1)}, u32[]{:S(2)}, u32[]{:S(2)}) collective-permute-start(bf16[1456,128]{1,0:T(8,128)(2,1)S(1)} %collective-permute-done.3.a_ref.refs_3_), channel_id=1, source_target_pairs={{8,16},{16,8},{9,17},{17,9},{10,18},{18,10},{11,19},{19,11},{12,20... | collective-permute-start | bytes 1118216 | tf_op jit(solution)/shard_map/ppermute | solution.py:379
  25.6 20.3 %collective-permute-start.11 = (bf16[2,1456,128]{2,1,0:T(8,128)(2,1)S(1)}, bf16[2,1456,128]{2,1,0:T(8,128)(2,1)S(1)}, u32[]{:S(2)}, u32[]{:S(2)}) collective-permute-start(bf16[2,1456,128]{2,1,0:T(8,128)(2,1)S(1)} %shard_map.74), channel_id=1, source_target_pairs={{0,4},{1,3},{2,6},{3,1},{4,0},{5,7},{6,2},{7,5},{8,12},{9,11},{10,... | collective-permute-start | bytes 2236424 | tf_op jit(solution)/shard_map/ppermute | solution.py:373
  32.4 13.4 %collective-permute-start.8 = (bf16[1456,128]{1,0:T(8,128)(2,1)S(1)}, bf16[1456,128]{1,0:T(8,128)(2,1)S(1)}, u32[]{:S(2)}, u32[]{:S(2)}) collective-permute-start(bf16[1456,128]{1,0:T(8,128)(2,1)S(1)} %collective-permute-done.4.inner_ref), channel_id=1, source_target_pairs={{8,0},{16,24},{9,1},{17,25},{10,2},{18,26},{11,3},{19,27},{12,4},{... | collective-permute-start | bytes 1118216 | tf_op jit(solution)/shard_map/ppermute | solution.py:381
  33.7 13.0 %collective-permute-start.12 = (bf16[360,512]{1,0:T(8,128)(2,1)S(1)}, bf16[360,512]{1,0:T(8,128)(2,1)S(1)}, u32[]{:S(2)}, u32[]{:S(2)}) collective-permute-start(bf16[360,512]{1,0:T(8,128)(2,1)S(1)} %get-tuple-element.53), channel_id=1, source_target_pairs={{8,16},{16,8},{9,17},{17,9},{10,18},{18,10},{11,19},{19,11},{12,20... | collective-permute-start | bytes 1105928 | tf_op jit(solution)/shard_map/ppermute | solution.py:379
  34.5 12.0 %collective-permute-start.14 = (bf16[1456,128]{1,0:T(8,128)(2,1)S(1)}, bf16[1456,128]{1,0:T(8,128)(2,1)S(1)}, u32[]{:S(2)}, u32[]{:S(2)}) collective-permute-start(bf16[1456,128]{1,0:T(8,128)(2,1)S(1)} %shard_map.76.a_ref.refs_3_), channel_id=1, source_target_pairs={{0,2},{1,5},{2,0},{3,7},{4,6},{5,1},{6,4},{7,3},{8,10},{9,13},{10,... | collective-permute-start | bytes 1118216 | tf_op jit(solution)/shard_map/ppermute | solution.py:373
  45.9 15.8 %collective-permute-start.17 = (bf16[1472,128]{1,0:T(8,128)(2,1)S(1)}, bf16[1472,128]{1,0:T(8,128)(2,1)S(1)}, u32[]{:S(2)}, u32[]{:S(2)}) collective-permute-start(bf16[1472,128]{1,0:T(8,128)(2,1)S(1)} %shard_map.80.a_ref.refs_3_), channel_id=1, source_target_pairs={{0,2},{1,5},{2,0},{3,7},{4,6},{5,1},{6,4},{7,3},{8,10},{9,13},{10,... | collective-permute-start | bytes 1130504 | tf_op jit(solution)/shard_map/ppermute | solution.py:373
  46.5 15.2 %collective-permute-start.9 = (bf16[360,512]{1,0:T(8,128)(2,1)S(1)}, bf16[360,512]{1,0:T(8,128)(2,1)S(1)}, u32[]{:S(2)}, u32[]{:S(2)}) collective-permute-start(bf16[360,512]{1,0:T(8,128)(2,1)S(1)} %get-tuple-element.43), channel_id=1, source_target_pairs={{0,8},{8,0},{16,24},{24,16},{1,9},{9,1},{17,25},{25,17},{2,10},{10... | collective-permute-start | bytes 1105928 | tf_op jit(solution)/shard_map/ppermute | solution.py:373
  46.5 26.0 %collective-permute-start.15 = (bf16[2,1456,128]{2,1,0:T(8,128)(2,1)S(1)}, bf16[2,1456,128]{2,1,0:T(8,128)(2,1)S(1)}, u32[]{:S(2)}, u32[]{:S(2)}) collective-permute-start(bf16[2,1456,128]{2,1,0:T(8,128)(2,1)S(1)} %shard_map.77), channel_id=1, source_target_pairs={{0,4},{1,3},{2,6},{3,1},{4,0},{5,7},{6,2},{7,5},{8,12},{9,11},{10,... | collective-permute-start | bytes 2236424 | tf_op jit(solution)/shard_map/ppermute | solution.py:373
  46.7 18.0 %collective-permute-start.13 = (bf16[360,512]{1,0:T(8,128)(2,1)S(1)}, bf16[360,512]{1,0:T(8,128)(2,1)S(1)}, u32[]{:S(2)}, u32[]{:S(2)}) collective-permute-start(bf16[360,512]{1,0:T(8,128)(2,1)S(1)} %get-tuple-element.50), channel_id=1, source_target_pairs={{0,16},{8,24},{16,0},{24,8},{1,17},{9,25},{17,1},{25,9},{2,18},{10... | collective-permute-start | bytes 1105928 | tf_op jit(solution)/shard_map/ppermute | solution.py:373
  61.7 14.2 %collective-permute-start.18 = (bf16[2,1472,128]{2,1,0:T(8,128)(2,1)S(1)}, bf16[2,1472,128]{2,1,0:T(8,128)(2,1)S(1)}, u32[]{:S(2)}, u32[]{:S(2)}) collective-permute-start(bf16[2,1472,128]{2,1,0:T(8,128)(2,1)S(1)} %shard_map.81), channel_id=1, source_target_pairs={{0,4},{1,3},{2,6},{3,1},{4,0},{5,7},{6,2},{7,5},{8,12},{9,11},{10,... | collective-permute-start | bytes 2261000 | tf_op jit(solution)/shard_map/ppermute | solution.py:373
  64.7 11.2 %collective-permute-start.16 = (bf16[360,512]{1,0:T(8,128)(2,1)S(1)}, bf16[360,512]{1,0:T(8,128)(2,1)S(1)}, u32[]{:S(2)}, u32[]{:S(2)}) collective-permute-start(bf16[360,512]{1,0:T(8,128)(2,1)S(1)} %get-tuple-element.53), channel_id=1, source_target_pairs={{0,24},{24,0},{1,25},{25,1},{2,26},{26,2},{3,27},{27,3},{4,28},{28... | collective-permute-start | bytes 1105928 | tf_op jit(solution)/shard_map/ppermute | solution.py:380
  77.0 2.8 %collective-permute-start.19 = (bf16[360,1440]{1,0:T(8,128)(2,1)S(1)}, bf16[360,1440]{1,0:T(8,128)(2,1)S(1)}, u32[]{:S(2)}, u32[]{:S(2)}) collective-permute-start(bf16[360,1440]{1,0:T(8,128)(2,1)S(1)} %shard_map.83), channel_id=1, source_target_pairs={{0,1},{1,0},{2,3},{3,2},{4,5},{5,4},{6,7},{7,6},{8,9},{9,8},{10,11... | collective-permute-start | bytes 3110408 | tf_op jit(solution)/shard_map/ppermute | solution.py:373

commit v6 on v5

--- a/solution.py
+++ b/solution.py
@@ -10,9 +10,8 @@
 LANES = 128
 META = 16
 AFTER = {
-    "saved": ("f0",),
     "inside": ("quarters", "saved",),
-    "outside": ("near", "saved",),
+    "outside": ("saved",),
     "f1": ("across", "saved",),
     "j1": ("s0",),
     "third": ("outside", "saved_swapped",),
@@ -25,7 +24,7 @@
     "j3": ("h1",),
     "turned": ("own",),
 }
-SCALE, SCALES = 3, {"t2": 0.5, "turned": 2, "t0": 0.5, "own": 40}
+SCALE, SCALES = 3, {"t2": 0.5, "turned": 2, "t0": 0.5, "own": 40, "saved": 16}
 TOTALS = ("t0", "t1", "t2")
 H3 = ("h3_inner", "h3_outer")
 

time: 81.2 us -> 81.2 us (level)
  no operation moved by 1% of the time
where the time goes in v6:
time: 81.2 us; the launch traced here: 80.9 us
  waiting for transfers between devices  34.6 us (43%)
  starting transfers between devices  28.3 us (35%)
  Pallas kernels  17.1 us (21%)
  between operations  0.85 us (1%)
    ppermute x14, waiting for transfers between devices, permute(): lax.ppermute(x, name, [(i, target(i)) for i in range(lax.axis_size(name))])  20.3 us
    ppermute x14, starting transfers between devices, permute(): lax.ppermute(x, name, [(i, target(i)) for i in range(lax.axis_size(name))])  19.5 us
    pallas_call x18, Pallas kernels, call(): pl.pallas_call(kernel, out_shape=outs, in_specs=specs, out_specs=[pl.Bloc...  17.1 us
    ppermute x2, waiting for transfers between devices, planes4(): outward = lambda x: lax.ppermute(x, 'dp', [(1, 0), (2, 3)])  12.9 us
    ppermute x1, starting transfers between devices, planes4(): outer = lambda x: lax.ppermute(x, 'dp', [(0, 3), (3, 0)])  4.16 us
    ppermute x2, starting transfers between devices, planes4(): outward = lambda x: lax.ppermute(x, 'dp', [(1, 0), (2, 3)])  2.56 us
    ppermute x3, starting transfers between devices, planes4(): inner = lambda x: lax.ppermute(x, 'dp', [(1, 2), (2, 1)])  2.04 us
  transfers between devices with their start and end apart: 20, of which 9 were waited for; matrix products, arithmetic and copies ran while one was open for 0% of the time, Pallas kernels for 17%

profile of v6, /device:TPU:0, one launch (start us, length us, event | category | flops | bytes accessed | tf_op | source)
XLA Modules:
  0.0 80.9 jit_solution(1258760679624620506)
XLA Ops:
  0.6 1.0 %shard_map.68.a_ref.refs_1_.refs_0_ = bf16[1456,128]{1,0:T(8,128)(2,1)S(1)} custom-call(bf16[1,1,1440,128]{3,2,1,0:T(8,128)(2,1)} %bitcast.17, s32[1,1,4,128]{3,2,1,0:T(4,128)} %bitcast.18, f32[1,1,4,128]{3,2,1,0:T(4,128)} %bitcast.20), custom_call_target="tpu_custom_call" | custom-call | bytes 14909440 | tf_op jit(solution)/shard_map/pallas_call | solution.py:342
  1.7 3.0 %collective-permute-start.1 = (bf16[1456,128]{1,0:T(8,128)(2,1)S(1)}, bf16[1456,128]{1,0:T(8,128)(2,1)S(1)}, u32[]{:S(2)}, u32[]{:S(2)}) collective-permute-start(bf16[1456,128]{1,0:T(8,128)(2,1)S(1)} %shard_map.68.a_ref.refs_1_.refs_0_), channel_id=1, source_target_pairs={{0,2},{1,5},{2,0},{3,7},{4,6},{5,1},{6,4},{7,3},{8,10},{9,13},{10,... | collective-permute-start | bytes 1118216 | tf_op jit(solution)/shard_map/ppermute | solution.py:372
  4.7 0.7 collective-permute-start.5
  5.4 4.4 %collective-permute-start.3 = (bf16[1456,128]{1,0:T(8,128)(2,1)S(1)}, bf16[1456,128]{1,0:T(8,128)(2,1)S(1)}, u32[]{:S(2)}, u32[]{:S(2)}) collective-permute-start(bf16[1456,128]{1,0:T(8,128)(2,1)S(1)} %shard_map.68.a_ref.refs_1_.refs_0_), channel_id=1, source_target_pairs={{0,8},{8,0},{16,24},{24,16},{1,9},{9,1},{17,25},{25,17},{2,10},{10... | collective-permute-start | bytes 1118216 | tf_op jit(solution)/shard_map/ppermute | solution.py:372
  9.8 0.4 collective-permute-done.1.b_ref.refs_2_.refs_1_
  10.3 2.1 %collective-permute-start.2 = (bf16[2,1456,128]{2,1,0:T(8,128)(2,1)S(1)}, bf16[2,1456,128]{2,1,0:T(8,128)(2,1)S(1)}, u32[]{:S(2)}, u32[]{:S(2)}) collective-permute-start(bf16[2,1456,128]{2,1,0:T(8,128)(2,1)S(1)} %shard_map.71), channel_id=1, source_target_pairs={{0,4},{1,3},{2,6},{3,1},{4,0},{5,7},{6,2},{7,5},{8,12},{9,11},{10,... | collective-permute-start | bytes 2236424 | tf_op jit(solution)/shard_map/ppermute | solution.py:372
  12.4 1.8 %shard_map.69 = (bf16[1440,256]{1,0:T(8,128)(2,1)S(1)}, bf16[1440,256]{1,0:T(8,128)(2,1)S(1)}) custom-call(bf16[4,2,64,1440]{3,2,1,0:T(8,128)(2,1)} %bitcast.13), custom_call_target="tpu_custom_call" | custom-call | bytes 2949120 | tf_op jit(solution)/shard_map/pallas_call | solution.py:342
  14.2 0.1 collective-permute-start
  14.3 1.5 %shard_map.73 = bf16[2880,128]{1,0:T(8,128)(2,1)S(1)} custom-call(bf16[4,2,64,1440]{3,2,1,0:T(8,128)(2,1)} %bitcast.14), custom_call_target="tpu_custom_call" | custom-call | bytes 23592960 | tf_op jit(solution)/shard_map/pallas_call | solution.py:342
  15.7 0.0 collective-permute-done.5.inner_ref
  15.7 2.2 %collective-permute-done.3.a_ref.refs_3_ = bf16[1456,128]{1,0:T(8,128)(2,1)S(1)} collective-permute-done((bf16[1456,128]{1,0:T(8,128)(2,1)S(1)}, bf16[1456,128]{1,0:T(8,128)(2,1)S(1)}, u32[]{:S(2)}, u32[]{:S(2)}) %collective-permute-start.3) | collective-permute-done | bytes 372768 | tf_op jit(solution)/shard_map/ppermute | solution.py:372
  18.0 1.5 %collective-permute-start.10 = (bf16[1456,128]{1,0:T(8,128)(2,1)S(1)}, bf16[1456,128]{1,0:T(8,128)(2,1)S(1)}, u32[]{:S(2)}, u32[]{:S(2)}) collective-permute-start(bf16[1456,128]{1,0:T(8,128)(2,1)S(1)} %collective-permute-done.3.a_ref.refs_3_), channel_id=1, source_target_pairs={{0,2},{1,5},{2,0},{3,7},{4,6},{5,1},{6,4},{7,3},{8,10},{9,13},{10,... | collective-permute-start | bytes 1118216 | tf_op jit(solution)/shard_map/ppermute | solution.py:372
  19.4 0.0 collective-permute-start.7
  19.5 1.3 %collective-permute-start.6 = (bf16[1456,128]{1,0:T(8,128)(2,1)S(1)}, bf16[1456,128]{1,0:T(8,128)(2,1)S(1)}, u32[]{:S(2)}, u32[]{:S(2)}) collective-permute-start(bf16[1456,128]{1,0:T(8,128)(2,1)S(1)} %collective-permute-done.5.inner_ref), channel_id=1, source_target_pairs={{8,0},{16,24},{9,1},{17,25},{10,2},{18,26},{11,3},{19,27},{12,4},{... | collective-permute-start | bytes 1118216 | tf_op jit(solution)/shard_map/ppermute | solution.py:380
  20.7 0.0 collective-permute-done.got_ref
  20.7 0.2 shard_map.70
  21.0 0.7 collective-permute-start.4
  21.6 3.9 %collective-permute-done.10.b_ref.refs_4_ = bf16[1456,128]{1,0:T(8,128)(2,1)S(1)} collective-permute-done((bf16[1456,128]{1,0:T(8,128)(2,1)S(1)}, bf16[1456,128]{1,0:T(8,128)(2,1)S(1)}, u32[]{:S(2)}, u32[]{:S(2)}) %collective-permute-start.10) | collective-permute-done | bytes 372768 | tf_op jit(solution)/shard_map/ppermute | solution.py:372
  25.5 0.0 collective-permute-done.2.refs_3_.refs_2_
  25.6 2.5 %collective-permute-start.11 = (bf16[2,1456,128]{2,1,0:T(8,128)(2,1)S(1)}, bf16[2,1456,128]{2,1,0:T(8,128)(2,1)S(1)}, u32[]{:S(2)}, u32[]{:S(2)}) collective-permute-start(bf16[2,1456,128]{2,1,0:T(8,128)(2,1)S(1)} %shard_map.74), channel_id=1, source_target_pairs={{0,4},{1,3},{2,6},{3,1},{4,0},{5,7},{6,2},{7,5},{8,12},{9,11},{10,... | collective-permute-start | bytes 2236424 | tf_op jit(solution)/shard_map/ppermute | solution.py:372
  28.1 4.4 %collective-permute-done.6.outer_ref = bf16[1456,128]{1,0:T(8,128)(2,1)S(1)} collective-permute-done((bf16[1456,128]{1,0:T(8,128)(2,1)S(1)}, bf16[1456,128]{1,0:T(8,128)(2,1)S(1)}, u32[]{:S(2)}, u32[]{:S(2)}) %collective-permute-start.6) | collective-permute-done | bytes 372768 | tf_op jit(solution)/shard_map/ppermute | solution.py:380
  32.4 1.3 %collective-permute-start.8 = (bf16[1456,128]{1,0:T(8,128)(2,1)S(1)}, bf16[1456,128]{1,0:T(8,128)(2,1)S(1)}, u32[]{:S(2)}, u32[]{:S(2)}) collective-permute-start(bf16[1456,128]{1,0:T(8,128)(2,1)S(1)} %collective-permute-done.4.inner_ref), channel_id=1, source_target_pairs={{8,0},{16,24},{9,1},{17,25},{10,2},{18,26},{11,3},{19,27},{12,4},{... | collective-permute-start | bytes 1118216 | tf_op jit(solution)/shard_map/ppermute | solution.py:380
  33.7 0.7 collective-permute-start.12
  34.5 0.6 collective-permute-start.14
  35.1 2.3 %shard_map.79.refs_0_.score_ref = f32[8,128]{1,0:T(8,128)S(1)} custom-call(bf16[4,2,64,1440]{3,2,1,0:T(8,128)(2,1)} %bitcast.15, bf16[2880,128]{1,0:T(8,128)(2,1)S(1)} %collective-permute-done.7.got_ref, bf16[1456,128]{1,0:T(8,128)(2,1)S(1)} %shard_map.68.a_ref.refs_1_.refs_0_, bf16[1456,128]{1,0:T(8,128)(2,1)S(1)} %collective-permute-done.1.b_ref.refs_2_.refs_1_, ...), custom_call_target="tpu_custom_call" | custom-call | flops 1132462080 | bytes 11108352 | tf_op jit(solution)/shard_map/pallas_call | solution.py:342
  37.3 8.5 %collective-permute-done.8.outer_ref = bf16[1456,128]{1,0:T(8,128)(2,1)S(1)} collective-permute-done((bf16[1456,128]{1,0:T(8,128)(2,1)S(1)}, bf16[1456,128]{1,0:T(8,128)(2,1)S(1)}, u32[]{:S(2)}, u32[]{:S(2)}) %collective-permute-start.8) | collective-permute-done | bytes 372768 | tf_op jit(solution)/shard_map/ppermute | solution.py:380
  45.9 0.6 collective-permute-start.17
  46.5 0.0 collective-permute-start.9
  46.5 0.0 collective-permute-done.14.b_ref.refs_4_
  46.5 0.1 collective-permute-start.15
  46.7 0.0 collective-permute-done.12.refs_1_
  46.7 2.8 %collective-permute-start.13 = (bf16[360,512]{1,0:T(8,128)(2,1)S(1)}, bf16[360,512]{1,0:T(8,128)(2,1)S(1)}, u32[]{:S(2)}, u32[]{:S(2)}) collective-permute-start(bf16[360,512]{1,0:T(8,128)(2,1)S(1)} %get-tuple-element.48), channel_id=1, source_target_pairs={{0,16},{8,24},{16,0},{24,8},{1,17},{9,25},{17,1},{25,9},{2,18},{10... | collective-permute-start | bytes 1105928 | tf_op jit(solution)/shard_map/ppermute | solution.py:372
  49.4 12.2 %collective-permute-done.9.refs_2_ = bf16[360,512]{1,0:T(8,128)(2,1)S(1)} collective-permute-done((bf16[360,512]{1,0:T(8,128)(2,1)S(1)}, bf16[360,512]{1,0:T(8,128)(2,1)S(1)}, u32[]{:S(2)}, u32[]{:S(2)}) %collective-permute-start.9) | collective-permute-done | bytes 368672 | tf_op jit(solution)/shard_map/ppermute | solution.py:372
  61.7 1.8 %collective-permute-start.18 = (bf16[2,1472,128]{2,1,0:T(8,128)(2,1)S(1)}, bf16[2,1472,128]{2,1,0:T(8,128)(2,1)S(1)}, u32[]{:S(2)}, u32[]{:S(2)}) collective-permute-start(bf16[2,1472,128]{2,1,0:T(8,128)(2,1)S(1)} %shard_map.81), channel_id=1, source_target_pairs={{0,4},{1,3},{2,6},{3,1},{4,0},{5,7},{6,2},{7,5},{8,12},{9,11},{10,... | collective-permute-start | bytes 2261000 | tf_op jit(solution)/shard_map/ppermute | solution.py:372
  63.5 1.2 %collective-permute-done.13.refs_2_ = bf16[360,512]{1,0:T(8,128)(2,1)S(1)} collective-permute-done((bf16[360,512]{1,0:T(8,128)(2,1)S(1)}, bf16[360,512]{1,0:T(8,128)(2,1)S(1)}, u32[]{:S(2)}, u32[]{:S(2)}) %collective-permute-start.13) | collective-permute-done | bytes 368672 | tf_op jit(solution)/shard_map/ppermute | solution.py:372
  64.7 4.2 %collective-permute-start.16 = (bf16[360,512]{1,0:T(8,128)(2,1)S(1)}, bf16[360,512]{1,0:T(8,128)(2,1)S(1)}, u32[]{:S(2)}, u32[]{:S(2)}) collective-permute-start(bf16[360,512]{1,0:T(8,128)(2,1)S(1)} %get-tuple-element.51), channel_id=1, source_target_pairs={{0,24},{24,0},{1,25},{25,1},{2,26},{26,2},{3,27},{27,3},{4,28},{28... | collective-permute-start | bytes 1105928 | tf_op jit(solution)/shard_map/ppermute | solution.py:379
  68.9 1.7 %shard_map.72 = (f32[360,1440]{1,0:T(8,128)S(1)}, f32[360,1440]{1,0:T(8,128)S(1)}) custom-call(bf16[360,512]{1,0:T(8,128)(2,1)S(1)} %get-tuple-element.32.refs_0_, bf16[1456,128]{1,0:T(8,128)(2,1)S(1)} %shard_map.68.a_ref.refs_1_.refs_0_, bf16[1456,128]{1,0:T(8,128)(2,1)S(1)} %collective-permute-done.1.b_ref.refs_2_.refs_1_, ...), custom_call_target="tpu_custom_call" | custom-call | flops 530841600 | bytes 929792 | tf_op jit(solution)/shard_map/pallas_call | solution.py:342
  70.6 1.9 %shard_map.75 = (f32[360,1440]{1,0:T(8,128)S(1)}, f32[360,1440]{1,0:T(8,128)S(1)}) custom-call(f32[360,1440]{1,0:T(8,128)S(1)} %get-tuple-element.33.refs_0_, f32[360,1440]{1,0:T(8,128)S(1)} %get-tuple-element.34.refs_1_, bf16[360,512]{1,0:T(8,128)(2,1)S(1)} %collective-permute-done.9.refs_2_, ...), custom_call_target="tpu_custom_call", output_to_operand_aliasing={{0}: (0, {}), {1}: (1, {})} | custom-call | flops 3185049600 | bytes 18020352 | tf_op jit(solution)/shard_map/pallas_call | solution.py:342
  72.5 0.0 collective-permute-done.15.refs_5_
  72.5 1.9 %shard_map.78 = (f32[360,1440]{1,0:T(8,128)S(1)}, f32[360,1440]{1,0:T(8,128)S(1)}) custom-call(f32[360,1440]{1,0:T(8,128)S(1)} %get-tuple-element.45.refs_0_, f32[360,1440]{1,0:T(8,128)S(1)} %get-tuple-element.46.refs_1_, bf16[360,512]{1,0:T(8,128)(2,1)S(1)} %collective-permute-done.13.refs_2_, ...), custom_call_target="tpu_custom_call", output_to_operand_aliasing={{0}: (0, {}), {1}: (1, {})} | custom-call | flops 530841600 | bytes 3003392 | tf_op jit(solution)/shard_map/pallas_call | solution.py:342
  74.5 1.4 %collective-permute-done.16.refs_2_ = bf16[360,512]{1,0:T(8,128)(2,1)S(1)} collective-permute-done((bf16[360,512]{1,0:T(8,128)(2,1)S(1)}, bf16[360,512]{1,0:T(8,128)(2,1)S(1)}, u32[]{:S(2)}, u32[]{:S(2)}) %collective-permute-start.16) | collective-permute-done | bytes 368672 | tf_op jit(solution)/shard_map/ppermute | solution.py:379
  75.9 0.0 collective-permute-done.18.refs_5_.pair_ref
  75.9 1.1 %shard_map.83 = bf16[360,1440]{1,0:T(8,128)(2,1)S(1)} custom-call(f32[360,1440]{1,0:T(8,128)S(1)} %get-tuple-element.55.refs_0_, bf16[360,512]{1,0:T(8,128)(2,1)S(1)} %collective-permute-done.12.refs_1_, bf16[360,512]{1,0:T(8,128)(2,1)S(1)} %collective-permute-done.16.refs_2_, bf16[1472,128]{1,0:T(8,128)(2,1)S(1)} %shard_map.80.a_ref.refs_3_, ...), custom_call_target="tpu_custom_call" | custom-call | flops 1592524800 | bytes 12954624 | tf_op jit(solution)/shard_map/pallas_call | solution.py:342
  77.0 0.1 collective-permute-start.19
  77.0 1.3 %shard_map.85 = f32[4,128]{1,0:T(4,128)} custom-call(s32[1,1,4,128]{3,2,1,0:T(4,128)} %bitcast.19, f32[8,128]{1,0:T(8,128)S(1)} %shard_map.79.refs_0_.score_ref, bf16[1472,128]{1,0:T(8,128)(2,1)S(1)} %collective-permute-done.17.b_ref.refs_4_.first_ref, bf16[2,1472,128]{2,1,0:T(8,128)(2,1)S(1)} %collective-permute-done.18.refs_5_.pair_ref), custom_call_target="tpu_custom_call" | custom-call | bytes 3409920 | tf_op jit(solution)/shard_map/pallas_call | solution.py:342
  78.3 1.1 %shard_map.82.a_ref = f32[360,1440]{1,0:T(8,128)S(1)} custom-call(f32[360,1440]{1,0:T(8,128)S(1)} %get-tuple-element.50.refs_0_, bf16[360,512]{1,0:T(8,128)(2,1)S(1)} %collective-permute-done.12.refs_1_, bf16[360,512]{1,0:T(8,128)(2,1)S(1)} %collective-permute-done.16.refs_2_, ...), custom_call_target="tpu_custom_call", output_to_operand_aliasing={{}: (0, {})} | custom-call | flops 1592524800 | bytes 12954624 | tf_op jit(solution)/shard_map/pallas_call | solution.py:342
  79.4 0.4 collective-permute-done.19.b_ref
  79.8 1.1 %shard_map.84 = bf16[360,1440]{1,0:T(8,128)(2,1)} custom-call(f32[360,1440]{1,0:T(8,128)S(1)} %shard_map.82.a_ref, bf16[360,1440]{1,0:T(8,128)(2,1)S(1)} %collective-permute-done.19.b_ref), custom_call_target="tpu_custom_call" | custom-call | bytes 9331200 | tf_op jit(solution)/shard_map/pallas_call | solution.py:342
  (10 shorter events, 0.3 us)
Async XLA Ops:
  1.7 8.5 %collective-permute-start.1 = (bf16[1456,128]{1,0:T(8,128)(2,1)S(1)}, bf16[1456,128]{1,0:T(8,128)(2,1)S(1)}, u32[]{:S(2)}, u32[]{:S(2)}) collective-permute-start(bf16[1456,128]{1,0:T(8,128)(2,1)S(1)} %shard_map.68.a_ref.refs_1_.refs_0_), channel_id=1, source_target_pairs={{0,2},{1,5},{2,0},{3,7},{4,6},{5,1},{6,4},{7,3},{8,10},{9,13},{10,... | collective-permute-start | bytes 1118216 | tf_op jit(solution)/shard_map/ppermute | solution.py:372
  4.7 11.1 %collective-permute-start.5 = (bf16[1456,128]{1,0:T(8,128)(2,1)S(1)}, bf16[1456,128]{1,0:T(8,128)(2,1)S(1)}, u32[]{:S(2)}, u32[]{:S(2)}) collective-permute-start(bf16[1456,128]{1,0:T(8,128)(2,1)S(1)} %shard_map.68.a_ref.refs_1_.refs_0_), channel_id=1, source_target_pairs={{8,16},{16,8},{9,17},{17,9},{10,18},{18,10},{11,19},{19,11},{12,20... | collective-permute-start | bytes 1118216 | tf_op jit(solution)/shard_map/ppermute | solution.py:378
  5.4 12.6 %collective-permute-start.3 = (bf16[1456,128]{1,0:T(8,128)(2,1)S(1)}, bf16[1456,128]{1,0:T(8,128)(2,1)S(1)}, u32[]{:S(2)}, u32[]{:S(2)}) collective-permute-start(bf16[1456,128]{1,0:T(8,128)(2,1)S(1)} %shard_map.68.a_ref.refs_1_.refs_0_), channel_id=1, source_target_pairs={{0,8},{8,0},{16,24},{24,16},{1,9},{9,1},{17,25},{25,17},{2,10},{10... | collective-permute-start | bytes 1118216 | tf_op jit(solution)/shard_map/ppermute | solution.py:372
  10.3 15.2 %collective-permute-start.2 = (bf16[2,1456,128]{2,1,0:T(8,128)(2,1)S(1)}, bf16[2,1456,128]{2,1,0:T(8,128)(2,1)S(1)}, u32[]{:S(2)}, u32[]{:S(2)}) collective-permute-start(bf16[2,1456,128]{2,1,0:T(8,128)(2,1)S(1)} %shard_map.71), channel_id=1, source_target_pairs={{0,4},{1,3},{2,6},{3,1},{4,0},{5,7},{6,2},{7,5},{8,12},{9,11},{10,... | collective-permute-start | bytes 2236424 | tf_op jit(solution)/shard_map/ppermute | solution.py:372
  14.2 6.6 %collective-permute-start = (bf16[1440,256]{1,0:T(8,128)(2,1)S(1)}, bf16[1440,256]{1,0:T(8,128)(2,1)S(1)}, u32[]{:S(2)}, u32[]{:S(2)}) collective-permute-start(bf16[1440,256]{1,0:T(8,128)(2,1)S(1)} %get-tuple-element.31), channel_id=1, source_target_pairs={{0,1},{1,0},{2,3},{3,2},{4,5},{5,4},{6,7},{7,6},{8,9},{9,8},{10,11... | collective-permute-start | bytes 2211848 | tf_op jit(solution)/shard_map/ppermute | solution.py:372
  18.0 7.6 %collective-permute-start.10 = (bf16[1456,128]{1,0:T(8,128)(2,1)S(1)}, bf16[1456,128]{1,0:T(8,128)(2,1)S(1)}, u32[]{:S(2)}, u32[]{:S(2)}) collective-permute-start(bf16[1456,128]{1,0:T(8,128)(2,1)S(1)} %collective-permute-done.3.a_ref.refs_3_), channel_id=1, source_target_pairs={{0,2},{1,5},{2,0},{3,7},{4,6},{5,1},{6,4},{7,3},{8,10},{9,13},{10,... | collective-permute-start | bytes 1118216 | tf_op jit(solution)/shard_map/ppermute | solution.py:372
  19.4 8.6 %collective-permute-start.7 = (bf16[2880,128]{1,0:T(8,128)(2,1)S(1)}, bf16[2880,128]{1,0:T(8,128)(2,1)S(1)}, u32[]{:S(2)}, u32[]{:S(2)}) collective-permute-start(bf16[2880,128]{1,0:T(8,128)(2,1)S(1)} %shard_map.73), channel_id=1, source_target_pairs={{0,1},{1,0},{2,3},{3,2},{4,5},{5,4},{6,7},{7,6},{8,9},{9,8},{10,11... | collective-permute-start | bytes 2211848 | tf_op jit(solution)/shard_map/ppermute | solution.py:372
  19.5 13.0 %collective-permute-start.6 = (bf16[1456,128]{1,0:T(8,128)(2,1)S(1)}, bf16[1456,128]{1,0:T(8,128)(2,1)S(1)}, u32[]{:S(2)}, u32[]{:S(2)}) collective-permute-start(bf16[1456,128]{1,0:T(8,128)(2,1)S(1)} %collective-permute-done.5.inner_ref), channel_id=1, source_target_pairs={{8,0},{16,24},{9,1},{17,25},{10,2},{18,26},{11,3},{19,27},{12,4},{... | collective-permute-start | bytes 1118216 | tf_op jit(solution)/shard_map/ppermute | solution.py:380
  21.0 11.5 %collective-permute-start.4 = (bf16[1456,128]{1,0:T(8,128)(2,1)S(1)}, bf16[1456,128]{1,0:T(8,128)(2,1)S(1)}, u32[]{:S(2)}, u32[]{:S(2)}) collective-permute-start(bf16[1456,128]{1,0:T(8,128)(2,1)S(1)} %collective-permute-done.3.a_ref.refs_3_), channel_id=1, source_target_pairs={{8,16},{16,8},{9,17},{17,9},{10,18},{18,10},{11,19},{19,11},{12,20... | collective-permute-start | bytes 1118216 | tf_op jit(solution)/shard_map/ppermute | solution.py:378
  25.6 20.3 %collective-permute-start.11 = (bf16[2,1456,128]{2,1,0:T(8,128)(2,1)S(1)}, bf16[2,1456,128]{2,1,0:T(8,128)(2,1)S(1)}, u32[]{:S(2)}, u32[]{:S(2)}) collective-permute-start(bf16[2,1456,128]{2,1,0:T(8,128)(2,1)S(1)} %shard_map.74), channel_id=1, source_target_pairs={{0,4},{1,3},{2,6},{3,1},{4,0},{5,7},{6,2},{7,5},{8,12},{9,11},{10,... | collective-permute-start | bytes 2236424 | tf_op jit(solution)/shard_map/ppermute | solution.py:372
  32.4 13.4 %collective-permute-start.8 = (bf16[1456,128]{1,0:T(8,128)(2,1)S(1)}, bf16[1456,128]{1,0:T(8,128)(2,1)S(1)}, u32[]{:S(2)}, u32[]{:S(2)}) collective-permute-start(bf16[1456,128]{1,0:T(8,128)(2,1)S(1)} %collective-permute-done.4.inner_ref), channel_id=1, source_target_pairs={{8,0},{16,24},{9,1},{17,25},{10,2},{18,26},{11,3},{19,27},{12,4},{... | collective-permute-start | bytes 1118216 | tf_op jit(solution)/shard_map/ppermute | solution.py:380
  33.7 13.0 %collective-permute-start.12 = (bf16[360,512]{1,0:T(8,128)(2,1)S(1)}, bf16[360,512]{1,0:T(8,128)(2,1)S(1)}, u32[]{:S(2)}, u32[]{:S(2)}) collective-permute-start(bf16[360,512]{1,0:T(8,128)(2,1)S(1)} %get-tuple-element.51), channel_id=1, source_target_pairs={{8,16},{16,8},{9,17},{17,9},{10,18},{18,10},{11,19},{19,11},{12,20... | collective-permute-start | bytes 1105928 | tf_op jit(solution)/shard_map/ppermute | solution.py:378
  34.5 12.0 %collective-permute-start.14 = (bf16[1456,128]{1,0:T(8,128)(2,1)S(1)}, bf16[1456,128]{1,0:T(8,128)(2,1)S(1)}, u32[]{:S(2)}, u32[]{:S(2)}) collective-permute-start(bf16[1456,128]{1,0:T(8,128)(2,1)S(1)} %shard_map.76.a_ref.refs_3_), channel_id=1, source_target_pairs={{0,2},{1,5},{2,0},{3,7},{4,6},{5,1},{6,4},{7,3},{8,10},{9,13},{10,... | collective-permute-start | bytes 1118216 | tf_op jit(solution)/shard_map/ppermute | solution.py:372
  45.9 15.8 %collective-permute-start.17 = (bf16[1472,128]{1,0:T(8,128)(2,1)S(1)}, bf16[1472,128]{1,0:T(8,128)(2,1)S(1)}, u32[]{:S(2)}, u32[]{:S(2)}) collective-permute-start(bf16[1472,128]{1,0:T(8,128)(2,1)S(1)} %shard_map.80.a_ref.refs_3_), channel_id=1, source_target_pairs={{0,2},{1,5},{2,0},{3,7},{4,6},{5,1},{6,4},{7,3},{8,10},{9,13},{10,... | collective-permute-start | bytes 1130504 | tf_op jit(solution)/shard_map/ppermute | solution.py:372
  46.5 15.2 %collective-permute-start.9 = (bf16[360,512]{1,0:T(8,128)(2,1)S(1)}, bf16[360,512]{1,0:T(8,128)(2,1)S(1)}, u32[]{:S(2)}, u32[]{:S(2)}) collective-permute-start(bf16[360,512]{1,0:T(8,128)(2,1)S(1)} %get-tuple-element.41), channel_id=1, source_target_pairs={{0,8},{8,0},{16,24},{24,16},{1,9},{9,1},{17,25},{25,17},{2,10},{10... | collective-permute-start | bytes 1105928 | tf_op jit(solution)/shard_map/ppermute | solution.py:372
  46.5 26.0 %collective-permute-start.15 = (bf16[2,1456,128]{2,1,0:T(8,128)(2,1)S(1)}, bf16[2,1456,128]{2,1,0:T(8,128)(2,1)S(1)}, u32[]{:S(2)}, u32[]{:S(2)}) collective-permute-start(bf16[2,1456,128]{2,1,0:T(8,128)(2,1)S(1)} %shard_map.77), channel_id=1, source_target_pairs={{0,4},{1,3},{2,6},{3,1},{4,0},{5,7},{6,2},{7,5},{8,12},{9,11},{10,... | collective-permute-start | bytes 2236424 | tf_op jit(solution)/shard_map/ppermute | solution.py:372
  46.7 18.0 %collective-permute-start.13 = (bf16[360,512]{1,0:T(8,128)(2,1)S(1)}, bf16[360,512]{1,0:T(8,128)(2,1)S(1)}, u32[]{:S(2)}, u32[]{:S(2)}) collective-permute-start(bf16[360,512]{1,0:T(8,128)(2,1)S(1)} %get-tuple-element.48), channel_id=1, source_target_pairs={{0,16},{8,24},{16,0},{24,8},{1,17},{9,25},{17,1},{25,9},{2,18},{10... | collective-permute-start | bytes 1105928 | tf_op jit(solution)/shard_map/ppermute | solution.py:372
  61.7 14.2 %collective-permute-start.18 = (bf16[2,1472,128]{2,1,0:T(8,128)(2,1)S(1)}, bf16[2,1472,128]{2,1,0:T(8,128)(2,1)S(1)}, u32[]{:S(2)}, u32[]{:S(2)}) collective-permute-start(bf16[2,1472,128]{2,1,0:T(8,128)(2,1)S(1)} %shard_map.81), channel_id=1, source_target_pairs={{0,4},{1,3},{2,6},{3,1},{4,0},{5,7},{6,2},{7,5},{8,12},{9,11},{10,... | collective-permute-start | bytes 2261000 | tf_op jit(solution)/shard_map/ppermute | solution.py:372
  64.7 11.2 %collective-permute-start.16 = (bf16[360,512]{1,0:T(8,128)(2,1)S(1)}, bf16[360,512]{1,0:T(8,128)(2,1)S(1)}, u32[]{:S(2)}, u32[]{:S(2)}) collective-permute-start(bf16[360,512]{1,0:T(8,128)(2,1)S(1)} %get-tuple-element.51), channel_id=1, source_target_pairs={{0,24},{24,0},{1,25},{25,1},{2,26},{26,2},{3,27},{27,3},{4,28},{28... | collective-permute-start | bytes 1105928 | tf_op jit(solution)/shard_map/ppermute | solution.py:379
  77.0 2.8 %collective-permute-start.19 = (bf16[360,1440]{1,0:T(8,128)(2,1)S(1)}, bf16[360,1440]{1,0:T(8,128)(2,1)S(1)}, u32[]{:S(2)}, u32[]{:S(2)}) collective-permute-start(bf16[360,1440]{1,0:T(8,128)(2,1)S(1)} %shard_map.83), channel_id=1, source_target_pairs={{0,1},{1,0},{2,3},{3,2},{4,5},{5,4},{6,7},{7,6},{8,9},{9,8},{10,11... | collective-permute-start | bytes 3110408 | tf_op jit(solution)/shard_map/ppermute | solution.py:372
